TPU v7x, 32 devices: a whole 2x2x4 slice. The times are simulated.
32 devices in a mesh: gz: 8 (over z, x), gx: 4 (over y, core).
Axes of the slice: x: 2, y: 2, z: 4, core: 2. Of those that a mesh axis runs over, the one named last changes fastest.
Arguments:
- atom_velocity: float32 [3, 4096, 128], P(None, ('gz', 'gx')), may hold values from -4.2 to 4.2
- atom_noise: float32 [3, 4096, 128], P(None, ('gz', 'gx')), may hold values from -6 to 6
- atom_plane: int32 [4096, 128], P(('gz', 'gx')), may hold values from 0 to 127, as said below
- atom_column: int32 [4096, 128], P(('gz', 'gx')), may hold values from 0 to 4095
- brick_count: int32 [4096], P(('gz', 'gx')), may hold values from 32 to 128, as said below
- electron_temp: float32 [128, 64, 256], P('gz', 'gx'), may hold values from 0.05 to 3.8
Outputs:
- new_temp: float32 [128, 64, 256], P('gz', 'gx')
- new_velocity: float32 [3, 4096, 128], P(None, ('gz', 'gx'))
Inputs may be any that keep to these rules, and one draw needn't show every extreme that they name: `atom_plane`: all 128 entries of a brick lie in one slab of 16 planes (the planes of one gz index). No slab holds more than 32 bricks of one device, and in every draw one slab holds exactly 32 bricks of every device. `brick_count`: every device holds a brick with 128 used slots.
All inputs are finite; a program needn't handle non-finite values.
Results may differ from a plain program's by a relative error of at most 0.00035.
Values sent between devices are 32-bit elements; how exact they have to be, the bound alone decides.
No kernel may reach another device: no remote copies, remote signals or barrier semaphores. Data moves between devices by JAX's collectives and lax.ppermute only.
A program may use at most 128 MiB of HBM per device.

v0:
```python
import jax
import jax.numpy as jnp
from jax import lax
from jax.sharding import PartitionSpec as P

STIFFNESS = 10000.0
LATERAL = 0.1
COUPLE = 0.5
TWO_THIRDS = 2.0 / 3.0
KICK_RATE = 0.2


def extended_2(cells, sides, width, closed):
    for axis, dim in sides:
        count = lax.axis_size(axis)
        ends = count if closed else count - 1
        head = lax.slice_in_dim(cells, 0, width, axis=dim)
        tail = lax.slice_in_dim(cells, cells.shape[dim] - width, cells.shape[dim], axis=dim)
        cells = jnp.concatenate(
            [
                lax.ppermute(tail, axis, [(i, (i + 1) % count) for i in range(ends)]),
                cells,
                lax.ppermute(head, axis, [((i + 1) % count, i) for i in range(ends)]),
            ],
            axis=dim,
        )
    return cells


def level_update(system, below_rows, above_rows, below_valid, above_valid):
    lower_ratio = -system[0] / jnp.where(below_valid, below_rows[1], 1.0)
    upper_ratio = -system[2] / jnp.where(above_valid, above_rows[1], 1.0)
    return jnp.stack(
        [
            lower_ratio * below_rows[0],
            system[1] + lower_ratio * below_rows[2] + upper_ratio * above_rows[0],
            upper_ratio * above_rows[2],
            system[3] + lower_ratio * below_rows[3] + upper_ratio * above_rows[3],
        ]
    )


def chain_solve(lower_band, diagonal, upper_band, right_side):

    def forward(state_pair, entries):
        sweep_ratio, sweep_value = state_pair
        below_band, middle, above_band, source = entries
        pivot_value = middle - below_band * sweep_ratio
        next_ratio = above_band / pivot_value
        next_value = (source - below_band * sweep_value) / pivot_value
        return ((next_ratio, next_value), (next_ratio, next_value))

    zero_start = jnp.zeros_like(diagonal[0])
    _, (ratios, values) = lax.scan(
        forward, (zero_start, zero_start), (lower_band, diagonal, upper_band, right_side)
    )

    def backward(later_value, entries):
        ratio_here, value_here = entries
        result = value_here - ratio_here * later_value
        return (result, result)

    _, solution = lax.scan(backward, zero_start, (ratios, values), reverse=True)
    return solution


def solve_items(regrouped):
    return chain_solve(regrouped[0], regrouped[1], regrouped[2], regrouped[3])[None]


def cell_tables(cell_block, row_count, width_y):
    row_hot = (
        cell_block[:, None] // width_y == lax.broadcasted_iota(jnp.int32, (1, row_count), 1)
    ).astype(jnp.float32)
    y_hot = (
        cell_block[:, None] % width_y == lax.broadcasted_iota(jnp.int32, (1, width_y), 1)
    ).astype(jnp.float32)
    return (row_hot, y_hot)


def bin_cells(speed, cell, row_count, width_y):
    brick_rows = cell.shape[0]
    block = min(brick_rows, 64)
    turns = brick_rows // block
    kinetic = (0.5 * jnp.sum(speed * speed, axis=0)).reshape(turns, -1)
    cell_blocks = cell.reshape(turns, -1)

    def add_block(totals, entries):
        kinetic_block, cell_block = entries
        row_hot, y_hot = cell_tables(cell_block, row_count, width_y)
        energy = totals[0] + jnp.einsum(
            "ar,ay->ry", row_hot * kinetic_block[:, None], y_hot, precision=lax.Precision.HIGHEST
        )
        count = totals[1] + jnp.einsum(
            "ar,ay->ry",
            row_hot.astype(jnp.bfloat16),
            y_hot.astype(jnp.bfloat16),
            preferred_element_type=jnp.float32,
        )
        return ((energy, count), None)

    empty = jnp.zeros((row_count, width_y), jnp.float32)
    (energy, count), _ = lax.scan(add_block, (empty, empty), (kinetic, cell_blocks))
    return (energy, count)


def look_up(temp_rows, cell):
    row_count, width_y = temp_rows.shape
    brick_rows, lanes = cell.shape
    block = min(brick_rows, 64)
    turns = brick_rows // block

    def pick_block(cell_block):
        row_hot, y_hot = cell_tables(cell_block, row_count, width_y)
        picked = jnp.dot(row_hot, temp_rows, precision=lax.Precision.HIGHEST)
        return jnp.sum(picked * y_hot, axis=1)

    return lax.map(pick_block, cell.reshape(turns, -1)).reshape(brick_rows, lanes)


def body(atom_velocity, atom_noise, atom_plane, atom_column, brick_count, electron_temp):
    planes, width_x, width_y = electron_temp.shape
    columns = width_x * width_y
    row_count = planes * width_x
    slab_count = lax.axis_size("gz")
    bricks = atom_plane.shape[0]
    slot_count = 2 * bricks // slab_count
    total_planes = planes * slab_count
    first_plane = lax.axis_index("gz") * planes
    atom_lane = lax.broadcasted_iota(jnp.int32, atom_plane.shape, 1)
    in_use = atom_lane < brick_count[:, None]
    spare_cell = planes * columns
    padded = extended_2(electron_temp, (("gz", 0), ("gx", 1)), 1, True)
    middle = padded[:, 1:-1]
    lateral = LATERAL * (
        padded[1:-1, :-2]
        + padded[1:-1, 2:]
        + jnp.roll(electron_temp, 1, 2)
        + jnp.roll(electron_temp, -1, 2)
        - 4.0 * electron_temp
    )
    plane_ids = first_plane + lax.broadcasted_iota(jnp.int32, (planes, 1, 1), 0)
    lower_face = jnp.where(plane_ids > 0, STIFFNESS * (0.5 * (electron_temp + middle[:-2])), 0.0)
    upper_face = jnp.where(
        plane_ids < total_planes - 1, STIFFNESS * (0.5 * (middle[2:] + electron_temp)), 0.0
    )
    owner_slab = atom_plane[:, 0] // planes
    owner_hits = (
        owner_slab[:, None] == lax.broadcasted_iota(jnp.int32, (1, slab_count), 1)
    ).astype(jnp.int32)
    before = jnp.cumsum(owner_hits, axis=0) - owner_hits
    brick_slot = owner_slab * slot_count + jnp.sum(before * owner_hits, axis=1)
    local_cell = jnp.where(
        in_use, (atom_plane - owner_slab[:, None] * planes) * columns + atom_column, spare_cell
    )
    slot_match = brick_slot[None, :] == lax.broadcasted_iota(
        jnp.int32, (slab_count * slot_count, 1), 0
    )
    source = (
        jnp.sum(
            jnp.where(slot_match, lax.broadcasted_iota(jnp.int32, (1, bricks), 1) + 1, 0), axis=1
        )
        - 1
    )
    filled = source >= 0
    source_brick = jnp.maximum(source, 0)
    send_speed = jnp.where(
        filled[None, :, None], jnp.take(atom_velocity, source_brick, axis=1), 0.0
    )
    send_cell = jnp.where(filled[:, None], jnp.take(local_cell, source_brick, axis=0), spare_cell)[
        None
    ]
    got_speed, got_cell = (
        lax.all_to_all(send_speed, "gz", split_axis=1, concat_axis=1, tiled=True),
        lax.all_to_all(send_cell, "gz", split_axis=1, concat_axis=1, tiled=True),
    )
    energy_rows, count_rows = bin_cells(got_speed, got_cell[0], row_count, width_y)
    energy = energy_rows.reshape(planes, columns)
    atom_count = count_rows.reshape(planes, columns)
    centre_flat = electron_temp.reshape(planes, columns)
    lower_flat = lower_face.reshape(planes, columns)
    upper_flat = upper_face.reshape(planes, columns)
    diagonal = centre_flat + lower_flat + upper_flat + COUPLE * atom_count
    right_side = (
        centre_flat * centre_flat + lateral.reshape(planes, columns) + COUPLE * TWO_THIRDS * energy
    )
    system = jnp.stack([-lower_flat, diagonal, -upper_flat, right_side])
    plane_column = first_plane + lax.broadcasted_iota(jnp.int32, (planes, 1), 0)
    for level in range(planes.bit_length() - 1):
        stride = 1 << level
        extended = extended_2(system, (("gz", 1),), stride, False)
        system = level_update(
            system,
            extended[:, :planes],
            extended[:, 2 * stride :],
            plane_column - stride >= 0,
            plane_column + stride < total_planes,
        )
    packed = system.reshape(4, 1, planes, columns)
    solved = solve_items(lax.all_to_all(packed, "gz", split_axis=2, concat_axis=1, tiled=True))
    solution = lax.all_to_all(solved, "gz", split_axis=1, concat_axis=2, tiled=True).reshape(
        planes, columns
    )
    reply = look_up(solution.reshape(row_count, width_y), got_cell[0])[None]
    returned = lax.all_to_all(reply, "gz", split_axis=1, concat_axis=1, tiled=True)
    atom_temp = jnp.take(returned[0], brick_slot, axis=0)
    new_velocity = jnp.where(
        in_use[None],
        (1.0 - KICK_RATE) * atom_velocity
        + jnp.sqrt(2.0 * KICK_RATE * atom_temp)[None] * atom_noise,
        0.0,
    )
    return (solution.reshape(planes, width_x, width_y), new_velocity)


def solution(mesh):
    placed = (
        P(None, ("gz", "gx"), None),
        P(None, ("gz", "gx"), None),
        P(("gz", "gx"), None),
        P(("gz", "gx"), None),
        P(("gz", "gx")),
        P("gz", "gx", None),
    )
    return jax.shard_map(
        body,
        mesh=mesh,
        in_specs=placed,
        out_specs=(P("gz", "gx", None), P(None, ("gz", "gx"), None)),
        check_vma=False,
    )
```

profile of v0, /device:TPU:0, one launch (start us, length us, event | category | flops | bytes accessed | tf_op | source)
XLA Modules:
  0.0 274.5 jit_solution(13788882303620604601)
XLA Ops:
  4.7 7.3 %all-to-all-start = ((s32[1,256,128]{2,0,1:T(1,128)}), s32[1,256,128]{2,0,1:T(1,128)S(1)}, u32[]{:S(2)}, u32[]{:S(2)}) async-start(s32[1,256,128]{2,0,1:T(1,128)} %bitcast.6), calls=%async_computation | async-start | bytes 262144 | tf_op jit(solution)/shard_map/all_to_all | solution.py:175
  19.8 4.9 %all-to-all-start.1 = ((f32[3,256,128]{2,0,1:T(4,128)}), f32[3,256,128]{2,0,1:T(4,128)S(1)}, u32[]{:S(2)}, u32[]{:S(2)}) async-start(f32[3,256,128]{2,0,1:T(4,128)} %copy.15), calls=%async_computation.1 | async-start | bytes 1048576 | tf_op jit(solution)/shard_map/all_to_all | solution.py:174
  30.8 6.6 %all-to-all-done.1 = f32[3,256,128]{2,0,1:T(4,128)S(1)} async-done(((f32[3,256,128]{2,0,1:T(4,128)}), f32[3,256,128]{2,0,1:T(4,128)S(1)}, u32[]{:S(2)}, u32[]{:S(2)}) %all-to-all-start.1) | async-done | bytes 393248 | tf_op jit(solution)/shard_map/all_to_all | solution.py:174
  37.9 56.7 %while.62 = (s32[]{:T(128)}, f32[256,256]{1,0:T(8,128)S(1)}, f32[256,256]{1,0:T(8,128)S(1)}, s32[4,8192]{1,0:T(4,128)S(1)}, f32[4,8192]{1,0:T(4,128)S(1)}, /*index=5*/s32[]{:T(128)}, s32[]{:T(128)}) while((s32[]{:T(128)}, f32[256,256]{1,0:T(8,128)S(1)}, f32[256,256]{1,0:T(8,128)S(1)}, s32[4,8192]{1,0:T(4,128)S(1)}, ...), condition=%wide.region_5.6_spmd.clone, body=%wide.region_4.5_spmd.clone.sunk | while | flops 7535484928 | bytes 1441888 | solution.py:103
  38.2 10.2 %fusion.95 = f32[256,256]{1,0:T(8,128)S(1)} fusion(s32[8192]{0:T(1024)S(1)} %get-tuple-element.613, f32[8192]{0:T(1024)S(1)} %bitcast.136, s32[8192]{0:T(1024)S(1)} %get-tuple-element.614, f32[256,256]{1,0:T(8,128)S(1)} %get-tuple-element.643, pred[]{:T(512)S(6)} %compare.52), kind=kOutput, calls=%fused_computation.31.clone.1 | convolution fusion | flops 6448873472 | bytes 622593 | tf_op jit(solution)/shard_map/while/body/eval_jaxpr/ar,ay->ry/dot_general | solution.py:91
  48.4 3.7 %fusion.96 = f32[256,256]{1,0:T(8,128)S(1)} fusion(s32[8192]{0:T(1024)S(1)} %get-tuple-element.613, s32[8192]{0:T(1024)S(1)} %get-tuple-element.614, f32[256,256]{1,0:T(8,128)S(1)} %get-tuple-element.644, pred[]{:T(512)S(6)} %compare.52), kind=kOutput, calls=%fused_computation.30.clone.1 | convolution fusion | flops 1086455808 | bytes 589825 | tf_op jit(solution)/shard_map/while/body/eval_jaxpr/ar,ay->ry/dot_general | solution.py:94
  52.3 10.2 %fusion.95 = f32[256,256]{1,0:T(8,128)S(1)} fusion(s32[8192]{0:T(1024)S(1)} %get-tuple-element.613, f32[8192]{0:T(1024)S(1)} %bitcast.136, s32[8192]{0:T(1024)S(1)} %get-tuple-element.614, f32[256,256]{1,0:T(8,128)S(1)} %get-tuple-element.643, pred[]{:T(512)S(6)} %compare.52), kind=kOutput, calls=%fused_computation.31.clone.1 | convolution fusion | flops 6448873472 | bytes 622593 | tf_op jit(solution)/shard_map/while/body/eval_jaxpr/ar,ay->ry/dot_general | solution.py:91
  66.3 10.2 %fusion.95 = f32[256,256]{1,0:T(8,128)S(1)} fusion(s32[8192]{0:T(1024)S(1)} %get-tuple-element.613, f32[8192]{0:T(1024)S(1)} %bitcast.136, s32[8192]{0:T(1024)S(1)} %get-tuple-element.614, f32[256,256]{1,0:T(8,128)S(1)} %get-tuple-element.643, pred[]{:T(512)S(6)} %compare.52), kind=kOutput, calls=%fused_computation.31.clone.1 | convolution fusion | flops 6448873472 | bytes 622593 | tf_op jit(solution)/shard_map/while/body/eval_jaxpr/ar,ay->ry/dot_general | solution.py:91
  76.5 3.7 %fusion.96 = f32[256,256]{1,0:T(8,128)S(1)} fusion(s32[8192]{0:T(1024)S(1)} %get-tuple-element.613, s32[8192]{0:T(1024)S(1)} %get-tuple-element.614, f32[256,256]{1,0:T(8,128)S(1)} %get-tuple-element.644, pred[]{:T(512)S(6)} %compare.52), kind=kOutput, calls=%fused_computation.30.clone.1 | convolution fusion | flops 1086455808 | bytes 589825 | tf_op jit(solution)/shard_map/while/body/eval_jaxpr/ar,ay->ry/dot_general | solution.py:94
  80.3 10.2 %fusion.95 = f32[256,256]{1,0:T(8,128)S(1)} fusion(s32[8192]{0:T(1024)S(1)} %get-tuple-element.613, f32[8192]{0:T(1024)S(1)} %bitcast.136, s32[8192]{0:T(1024)S(1)} %get-tuple-element.614, f32[256,256]{1,0:T(8,128)S(1)} %get-tuple-element.643, pred[]{:T(512)S(6)} %compare.52), kind=kOutput, calls=%fused_computation.31.clone.1 | convolution fusion | flops 6448873472 | bytes 622593 | tf_op jit(solution)/shard_map/while/body/eval_jaxpr/ar,ay->ry/dot_general | solution.py:91
  90.6 3.7 %fusion.96 = f32[256,256]{1,0:T(8,128)S(1)} fusion(s32[8192]{0:T(1024)S(1)} %get-tuple-element.613, s32[8192]{0:T(1024)S(1)} %get-tuple-element.614, f32[256,256]{1,0:T(8,128)S(1)} %get-tuple-element.644, pred[]{:T(512)S(6)} %compare.52), kind=kOutput, calls=%fused_computation.30.clone.1 | convolution fusion | flops 1086455808 | bytes 589825 | tf_op jit(solution)/shard_map/while/body/eval_jaxpr/ar,ay->ry/dot_general | solution.py:94
  105.0 4.2 %fusion.53 = (f32[1,16,4096]{2,0,1:T(1,128)S(1)}, f32[1,16,4096]{2,0,1:T(1,128)S(1)}) fusion(f32[4,1,4096]{2,0,1:T(4,128)S(1)} %collective-permute-done.5, f32[1,16,4096]{2,0,1:T(1,128)S(1)} %bitcast.120, f32[1,16,4096]{2,0,1:T(1,128)S(1)} %bitcast.124, f32[1,16,4096]{2,0,1:T(1,128)S(1)} %bitcast.116, f32[1,16,4096]{2,0,1:T(1,128)S(1)} %bitcast.112, ...), kind=kLoop, calls=%fused_computation.150 | loop fusion | flops 1179648 | bytes 2228240 | tf_op jit(solution)/shard_map/add | solution.py:36
  122.8 4.6 %fusion.47 = (f32[1,16,4096]{2,0,1:T(1,128)S(1)}, f32[1,16,4096]{2,0,1:T(1,128)S(1)}) fusion(f32[4,2,4096]{2,0,1:T(4,128)S(1)} %collective-permute-done.7, f32[1,16,4096]{2,0,1:T(1,128)S(1)} %get-tuple-element.439, f32[1,16,4096]{2,0,1:T(1,128)S(1)} %get-tuple-element.438, f32[1,16,4096]{2,0,1:T(1,128)S(1)} %get-tuple-element.422, ...), kind=kLoop, calls=%fused_computation.132 | loop fusion | flops 1245184 | bytes 2097168 | tf_op jit(solution)/shard_map/add | solution.py:36
  153.7 15.0 %collective-permute-done.10 = f32[4,8,4096]{2,0,1:T(4,128)S(1)} collective-permute-done((f32[4,8,4096]{2,0,1:T(4,128)S(1)}, f32[4,8,4096]{2,0,1:T(4,128)S(1)}, u32[]{:S(2)}, u32[]{:S(2)}) %collective-permute-start.10) | collective-permute-done | bytes 524320 | tf_op jit(solution)/shard_map/ppermute | solution.py:21
  179.0 8.3 %all-to-all-start.2 = ((f32[4,1,16,4096]{3,1,0,2:T(1,128)}), f32[4,1,16,4096]{3,1,0,2:T(1,128)S(1)}, u32[]{:S(2)}, u32[]{:S(2)}) async-start(f32[4,1,16,4096]{3,1,0,2:T(1,128)} %reshape.1002), calls=%async_computation.2 | async-start | bytes 2097152 | tf_op jit(solution)/shard_map/all_to_all | solution.py:200
  187.3 25.6 %all-to-all-done.2 = f32[4,1,16,4096]{3,1,0,2:T(1,128)S(1)} async-done(((f32[4,1,16,4096]{3,1,0,2:T(1,128)}), f32[4,1,16,4096]{3,1,0,2:T(1,128)S(1)}, u32[]{:S(2)}, u32[]{:S(2)}) %all-to-all-start.2) | async-done | bytes 1048608 | tf_op jit(solution)/shard_map/all_to_all | solution.py:200
  218.0 5.3 %while.64 = (s32[]{:T(128)}, f32[2,4096]{1,0:T(2,128)S(1)}, f32[8,2,4096]{2,1,0:T(2,128)}, f32[8,2,4096]{2,1,0:T(2,128)S(1)}, f32[8,2,4096]{2,1,0:T(2,128)S(1)}, /*index=5*/s32[]{:T(128)}, s32[]{:T(128)}, s32[]{:T(128)}) while((s32[]{:T(128)}, f32[2,4096]{1,0:T(2,128)S(1)}, f32[8,2,4096]{2,1,0:T(2,128)}, ...), condition=%wide.region_9.10_spmd.clone, body=%wide.region_8.9_spmd.clone.sunk | while | flops 24580 | bytes 163951 | solution.py:63
  226.8 9.1 %all-to-all-done.3 = f32[1,8,2,4096]{3,2,0,1:T(2,128)S(1)} async-done(((f32[1,8,2,4096]{3,2,0,1:T(2,128)}), f32[1,8,2,4096]{3,2,0,1:T(2,128)S(1)}, u32[]{:S(2)}, u32[]{:S(2)}) %all-to-all-start.3) | async-done | bytes 262176 | tf_op jit(solution)/shard_map/all_to_all | solution.py:201
  236.1 24.9 %while.61 = (s32[]{:T(128)}, f32[4,8192]{1,0:T(4,128)S(1)}, s32[4,8192]{1,0:T(4,128)S(1)}, f32[256,256]{1,0:T(8,128)S(1)}, s32[]{:T(128)}, /*index=5*/s32[]{:T(128)}) while((s32[]{:T(128)}, f32[4,8192]{1,0:T(4,128)S(1)}, s32[4,8192]{1,0:T(4,128)S(1)}, f32[256,256]{1,0:T(8,128)S(1)}, s32[]{:T(128)}, /*index=5*/s32[]{:T(128)}) %tuple.166), condition=%wide.region_12.13_spmd, body=%wide.region_10.12_spmd.sunk | while | flops 6450987008 | bytes 589901 | solution.py:118
  236.2 5.6 %fusion.93 = f32[8192]{0:T(1024)S(1)} fusion(f32[256,256]{1,0:T(8,128)S(1)} %get-tuple-element.728, s32[8192]{0:T(1024)S(1)} %get-tuple-element.606, s32[8192]{0:T(1024)S(1)} %get-tuple-element.607), kind=kOutput, calls=%fused_computation.7.clone.1 | convolution fusion | flops 6450831360 | bytes 360448 | tf_op jit(solution)/shard_map/while/body/eval_jaxpr/dot_general | solution.py:115
  242.4 5.6 %fusion.93 = f32[8192]{0:T(1024)S(1)} fusion(f32[256,256]{1,0:T(8,128)S(1)} %get-tuple-element.728, s32[8192]{0:T(1024)S(1)} %get-tuple-element.606, s32[8192]{0:T(1024)S(1)} %get-tuple-element.607), kind=kOutput, calls=%fused_computation.7.clone.1 | convolution fusion | flops 6450831360 | bytes 360448 | tf_op jit(solution)/shard_map/while/body/eval_jaxpr/dot_general | solution.py:115
  248.7 5.6 %fusion.93 = f32[8192]{0:T(1024)S(1)} fusion(f32[256,256]{1,0:T(8,128)S(1)} %get-tuple-element.728, s32[8192]{0:T(1024)S(1)} %get-tuple-element.606, s32[8192]{0:T(1024)S(1)} %get-tuple-element.607), kind=kOutput, calls=%fused_computation.7.clone.1 | convolution fusion | flops 6450831360 | bytes 360448 | tf_op jit(solution)/shard_map/while/body/eval_jaxpr/dot_general | solution.py:115
  254.9 5.6 %fusion.93 = f32[8192]{0:T(1024)S(1)} fusion(f32[256,256]{1,0:T(8,128)S(1)} %get-tuple-element.728, s32[8192]{0:T(1024)S(1)} %get-tuple-element.606, s32[8192]{0:T(1024)S(1)} %get-tuple-element.607), kind=kOutput, calls=%fused_computation.7.clone.1 | convolution fusion | flops 6450831360 | bytes 360448 | tf_op jit(solution)/shard_map/while/body/eval_jaxpr/dot_general | solution.py:115
  266.5 6.3 %all-to-all-done.4 = f32[1,256,128]{2,0,1:T(1,128)S(1)} async-done(((f32[1,256,128]{2,0,1:T(1,128)}), f32[1,256,128]{2,0,1:T(1,128)S(1)}, u32[]{:S(2)}, u32[]{:S(2)}) %all-to-all-start.4) | async-done | bytes 131104 | tf_op jit(solution)/shard_map/all_to_all | solution.py:205
  (168 shorter events, 106.6 us)
Async XLA Ops:
  1.7 10.3 %copy-start.1 = (f32[16,16,256]{2,1,0:T(8,128)S(1)}, f32[16,16,256]{2,1,0:T(8,128)}, u32[]{:S(2)}) copy-start(f32[16,16,256]{2,1,0:T(8,128)} %param.19) | copy-start | bytes 786436
  3.9 13.1 %copy-start = (f32[3,128,128]{2,1,0:T(8,128)S(1)}, f32[3,128,128]{2,1,0:T(8,128)}, u32[]{:S(2)}) copy-start(f32[3,128,128]{2,1,0:T(8,128)} %param.14) | copy-start | bytes 589828
  4.7 15.1 %all-to-all-start = ((s32[1,256,128]{2,0,1:T(1,128)}), s32[1,256,128]{2,0,1:T(1,128)S(1)}, u32[]{:S(2)}, u32[]{:S(2)}) async-start(s32[1,256,128]{2,0,1:T(1,128)} %bitcast.6), calls=%async_computation | async-start | bytes 262144 | tf_op jit(solution)/shard_map/all_to_all | solution.py:175
  12.0 7.7 %collective-permute-start = (f32[1,16,256]{2,1,0:T(8,128)S(1)}, f32[1,16,256]{2,1,0:T(8,128)S(1)}, u32[]{:S(2)}, u32[]{:S(2)}) collective-permute-start(f32[1,16,256]{2,1,0:T(8,128)S(1)} %get-tuple-element.462), channel_id=1, source_target_pairs={{0,4},{4,8},{8,12},{12,16},{16,20},{20,24},{24,28},{28,0},{1,5},{5... | collective-permute-start | bytes 49160 | tf_op jit(solution)/shard_map/ppermute | solution.py:21
  14.0 5.6 %collective-permute-start.1 = (f32[1,16,256]{2,1,0:T(8,128)S(1)}, f32[1,16,256]{2,1,0:T(8,128)S(1)}, u32[]{:S(2)}, u32[]{:S(2)}) collective-permute-start(f32[1,16,256]{2,1,0:T(8,128)S(1)} %get-tuple-element.461), channel_id=1, source_target_pairs={{4,0},{8,4},{12,8},{16,12},{20,16},{24,20},{28,24},{0,28},{5,1},{9... | collective-permute-start | bytes 49160 | tf_op jit(solution)/shard_map/ppermute | solution.py:23
  19.8 17.7 %all-to-all-start.1 = ((f32[3,256,128]{2,0,1:T(4,128)}), f32[3,256,128]{2,0,1:T(4,128)S(1)}, u32[]{:S(2)}, u32[]{:S(2)}) async-start(f32[3,256,128]{2,0,1:T(4,128)} %copy.15), calls=%async_computation.1 | async-start | bytes 1048576 | tf_op jit(solution)/shard_map/all_to_all | solution.py:174
  24.7 3.3 %collective-permute-start.2 = (f32[18,1,256]{2,1,0:T(1,128)S(1)}, f32[18,1,256]{2,1,0:T(1,128)}, u32[]{:S(2)}, u32[]{:S(2)}) collective-permute-start(f32[18,1,256]{2,1,0:T(1,128)S(1)} %get-tuple-element.448), channel_id=1, source_target_pairs={{0,1},{1,2},{2,3},{3,0},{4,5},{5,6},{6,7},{7,4},{8,9},{9,10},{10,1... | collective-permute-start | bytes 55304 | tf_op jit(solution)/shard_map/ppermute | solution.py:21
  24.8 3.3 %collective-permute-start.3 = (f32[18,1,256]{2,1,0:T(1,128)S(1)}, f32[18,1,256]{2,1,0:T(1,128)}, u32[]{:S(2)}, u32[]{:S(2)}) collective-permute-start(f32[18,1,256]{2,1,0:T(1,128)S(1)} %get-tuple-element.449), channel_id=1, source_target_pairs={{1,0},{2,1},{3,2},{0,3},{5,4},{6,5},{7,6},{4,7},{9,8},{10,9},{11,1... | collective-permute-start | bytes 55304 | tf_op jit(solution)/shard_map/ppermute | solution.py:23
  29.0 8.9 %copy-start.2 = (f32[256,256]{1,0:T(8,128)S(1)}, f32[256,256]{1,0:T(8,128)}, u32[]{:S(2)}) copy-start(f32[256,256]{1,0:T(8,128)} %custom-call.1) | copy-start | bytes 786436
  95.4 5.4 %copy-start.5 = (pred[16]{0:T(512)(128)(4,1)S(1)}, pred[16]{0:T(512)(128)(4,1)}, u32[]{:S(2)}) copy-start(pred[16]{0:T(512)(128)(4,1)} %add_compare_fusion.8) | copy-start | bytes 52
  95.5 5.2 %collective-permute-start.4 = (f32[4,1,4096]{2,0,1:T(4,128)S(1)}, f32[4,1,4096]{2,0,1:T(4,128)S(1)}, u32[]{:S(2)}, u32[]{:S(2)}) collective-permute-start(f32[4,1,4096]{2,0,1:T(4,128)S(1)} %get-tuple-element.446), channel_id=1, source_target_pairs={{0,4},{4,8},{8,12},{12,16},{16,20},{20,24},{24,28},{1,5},{5,9},{9,... | collective-permute-start | bytes 196616 | tf_op jit(solution)/shard_map/ppermute | solution.py:21
  98.9 6.2 %collective-permute-start.5 = (f32[4,1,4096]{2,0,1:T(4,128)S(1)}, f32[4,1,4096]{2,0,1:T(4,128)S(1)}, u32[]{:S(2)}, u32[]{:S(2)}) collective-permute-start(f32[4,1,4096]{2,0,1:T(4,128)S(1)} %get-tuple-element.447), channel_id=1, source_target_pairs={{4,0},{8,4},{12,8},{16,12},{20,16},{24,20},{28,24},{5,1},{9,5},{13... | collective-permute-start | bytes 196616 | tf_op jit(solution)/shard_map/ppermute | solution.py:23
  112.4 6.1 %collective-permute-start.6 = (f32[4,2,4096]{2,0,1:T(4,128)S(1)}, f32[4,2,4096]{2,0,1:T(4,128)S(1)}, u32[]{:S(2)}, u32[]{:S(2)}) collective-permute-start(f32[4,2,4096]{2,0,1:T(4,128)S(1)} %get-tuple-element.444), channel_id=1, source_target_pairs={{0,4},{4,8},{8,12},{12,16},{16,20},{20,24},{24,28},{1,5},{5,9},{9,... | collective-permute-start | bytes 393224 | tf_op jit(solution)/shard_map/ppermute | solution.py:21
  116.0 6.9 %collective-permute-start.7 = (f32[4,2,4096]{2,0,1:T(4,128)S(1)}, f32[4,2,4096]{2,0,1:T(4,128)S(1)}, u32[]{:S(2)}, u32[]{:S(2)}) collective-permute-start(f32[4,2,4096]{2,0,1:T(4,128)S(1)} %get-tuple-element.445), channel_id=1, source_target_pairs={{4,0},{8,4},{12,8},{16,12},{20,16},{24,20},{28,24},{5,1},{9,5},{13... | collective-permute-start | bytes 393224 | tf_op jit(solution)/shard_map/ppermute | solution.py:23
  130.9 7.5 %collective-permute-start.8 = (f32[4,4,4096]{2,0,1:T(4,128)S(1)}, f32[4,4,4096]{2,0,1:T(4,128)S(1)}, u32[]{:S(2)}, u32[]{:S(2)}) collective-permute-start(f32[4,4,4096]{2,0,1:T(4,128)S(1)} %get-tuple-element.442), channel_id=1, source_target_pairs={{0,4},{4,8},{8,12},{12,16},{16,20},{20,24},{24,28},{1,5},{5,9},{9,... | collective-permute-start | bytes 786440 | tf_op jit(solution)/shard_map/ppermute | solution.py:21
  134.2 8.3 %collective-permute-start.9 = (f32[4,4,4096]{2,0,1:T(4,128)S(1)}, f32[4,4,4096]{2,0,1:T(4,128)S(1)}, u32[]{:S(2)}, u32[]{:S(2)}) collective-permute-start(f32[4,4,4096]{2,0,1:T(4,128)S(1)} %get-tuple-element.443), channel_id=1, source_target_pairs={{4,0},{8,4},{12,8},{16,12},{20,16},{24,20},{28,24},{5,1},{9,5},{13... | collective-permute-start | bytes 786440 | tf_op jit(solution)/shard_map/ppermute | solution.py:23
  148.8 19.9 %collective-permute-start.10 = (f32[4,8,4096]{2,0,1:T(4,128)S(1)}, f32[4,8,4096]{2,0,1:T(4,128)S(1)}, u32[]{:S(2)}, u32[]{:S(2)}) collective-permute-start(f32[4,8,4096]{2,0,1:T(4,128)S(1)} %get-tuple-element.440), channel_id=1, source_target_pairs={{0,4},{4,8},{8,12},{12,16},{16,20},{20,24},{24,28},{1,5},{5,9},{9,... | collective-permute-start | bytes 1572872 | tf_op jit(solution)/shard_map/ppermute | solution.py:21
  152.4 19.2 %collective-permute-start.11 = (f32[4,8,4096]{2,0,1:T(4,128)S(1)}, f32[4,8,4096]{2,0,1:T(4,128)S(1)}, u32[]{:S(2)}, u32[]{:S(2)}) collective-permute-start(f32[4,8,4096]{2,0,1:T(4,128)S(1)} %get-tuple-element.441), channel_id=1, source_target_pairs={{4,0},{8,4},{12,8},{16,12},{20,16},{24,20},{28,24},{5,1},{9,5},{13... | collective-permute-start | bytes 1572872 | tf_op jit(solution)/shard_map/ppermute | solution.py:23
  179.0 33.9 %all-to-all-start.2 = ((f32[4,1,16,4096]{3,1,0,2:T(1,128)}), f32[4,1,16,4096]{3,1,0,2:T(1,128)S(1)}, u32[]{:S(2)}, u32[]{:S(2)}) async-start(f32[4,1,16,4096]{3,1,0,2:T(1,128)} %reshape.1002), calls=%async_computation.2 | async-start | bytes 2097152 | tf_op jit(solution)/shard_map/all_to_all | solution.py:200
  223.3 12.6 %all-to-all-start.3 = ((f32[1,8,2,4096]{3,2,0,1:T(2,128)}), f32[1,8,2,4096]{3,2,0,1:T(2,128)S(1)}, u32[]{:S(2)}, u32[]{:S(2)}) async-start(f32[1,8,2,4096]{3,2,0,1:T(2,128)} %bitcast.8), calls=%async_computation.3 | async-start | bytes 524288 | tf_op jit(solution)/shard_map/all_to_all | solution.py:201
  236.1 29.4 %copy-start.4 = (s32[128]{0:T(128)S(1)}, s32[128]{0:T(128)}, u32[]{:S(2)}) copy-start(s32[128]{0:T(128)} %param.18) | copy-start | bytes 1540
  261.0 12.5 %copy-start.3 = (f32[3,128,128]{2,1,0:T(8,128)S(1)}, f32[3,128,128]{2,1,0:T(8,128)}, u32[]{:S(2)}) copy-start(f32[3,128,128]{2,1,0:T(8,128)} %param.15) | copy-start | bytes 589828
  261.9 10.9 %all-to-all-start.4 = ((f32[1,256,128]{2,0,1:T(1,128)}), f32[1,256,128]{2,0,1:T(1,128)S(1)}, u32[]{:S(2)}, u32[]{:S(2)}) async-start(f32[1,256,128]{2,0,1:T(1,128)} %broadcast_in_dim_reshape.3), calls=%async_computation.4 | async-start | bytes 262144 | tf_op jit(solution)/shard_map/all_to_all | solution.py:205
where the time goes:
time: 279 us; the launch traced here: 274 us
  matrix products  78 us (28%)
  waiting for transfers between devices  72.8 us (26%)
  starting transfers between devices  53 us (19%)
  other arithmetic  50.2 us (18%)
  local copies, waits for them, and re-layouts  17.8 us (6%)
    dot_general x4, matrix products, add_block(): jnp.einsum('ar,ay->ry', row_hot * kinetic_block[:, None], y_hot, precisio...  40.9 us
    all_to_all x1, waiting for transfers between devices, body(): lax.all_to_all(packed, 'gz', split_axis=2, concat_axis=1, tiled=True)  25.6 us
    dot_general x4, matrix products, pick_block(): picked = jnp.dot(row_hot, temp_rows, precision=lax.Precision.HIGHEST)  22.5 us
    ppermute x6, waiting for transfers between devices, extended_2(): lax.ppermute(tail, axis, [(i, (i + 1) % count) for i in range(ends)])  20 us
    ppermute x6, starting transfers between devices, extended_2(): lax.ppermute(tail, axis, [(i, (i + 1) % count) for i in range(ends)])  15.9 us
    dot_general x4, matrix products, add_block(): jnp.einsum('ar,ay->ry', row_hot.astype(jnp.bfloat16), y_hot.astype(jnp.bf...  14.7 us
    add x4, other arithmetic, level_update(): system[1] + lower_ratio * below_rows[2] + upper_ratio * above_rows[0]  13.5 us
    mul x4, other arithmetic, level_update(): upper_ratio * above_rows[2]  10.5 us
  transfers between devices with their start and end apart: 17, of which 13 were waited for; matrix products, arithmetic and copies ran while one was open for 7% of the time, Pallas kernels for 0%

commit v1 on v0

v1 whole, which is shorter than its diff:
```python
import functools

import jax
import jax.numpy as jnp
from jax import lax
from jax.experimental import pallas as pl
from jax.experimental.pallas import tpu as pltpu
from jax.sharding import PartitionSpec as P

STIFFNESS = 10000.0
LATERAL = 0.1
COUPLE = 0.5
TWO_THIRDS = 2.0 / 3.0
KICK_RATE = 0.2
F32 = jnp.float32
BF16 = jnp.bfloat16
VMEM_LIMIT = 48 * 1024 * 1024


def quotient(value, size):
    if size & (size - 1) == 0:
        return lax.shift_right_logical(value, size.bit_length() - 1)
    return value // size


def iota(shape, dim):
    return lax.broadcasted_iota(jnp.int32, shape, dim)


def split(value, pieces):
    parts = []
    for _ in range(pieces):
        part = value.astype(BF16)
        parts.append(part)
        value = value - part.astype(F32)
    return parts


def merge(left, right):
    g_a, sl_a, rl_a, s_a, r_a = left
    g_b, sl_b, rl_b, s_b, r_b = right
    excess = s_a + sl_b
    source = r_a + rl_b
    inverse = 1.0 / (g_a + g_b + excess)
    to_left = g_a * inverse
    to_right = g_b * inverse
    return (
        g_a * to_right,
        sl_a + to_left * excess,
        rl_a + to_left * source,
        s_b + to_right * excess,
        r_b + to_right * source,
    )


def prefix_step(state, segment):
    gate, sl, rl, s, r = segment
    excess = state[0] + sl
    source = state[1] + rl
    ratio = gate / (gate + excess)
    return (s + ratio * excess, r + ratio * source)


def suffix_step(state, segment):
    gate, sl, rl, s, r = segment
    excess = s + state[0]
    source = r + state[1]
    ratio = gate / (gate + excess)
    return (sl + ratio * excess, rl + ratio * source)


def route_kernel(dims, slabs, rows, velocity, plane, column, count, send, meta):
    planes, width_x, width_y = dims
    bricks, lanes = plane.shape
    lane = iota((bricks, lanes), 1)
    sub_b = iota((bricks, bricks), 0)
    lane_b = iota((bricks, bricks), 1)
    eye = sub_b == lane_b
    owner = quotient(plane[:, 0:1], planes)
    owner_f = jnp.broadcast_to(owner.astype(F32), (bricks, bricks))
    owner_row = jnp.sum(jnp.where(eye, owner_f, 0.0), axis=0, keepdims=True)
    count_row = jnp.broadcast_to(count[...].astype(F32), (bricks, bricks))
    count_col = jnp.sum(jnp.where(eye, count_row, 0.0), axis=1, keepdims=True).astype(jnp.int32)
    ahead = (owner_f == owner_row) & (lane_b < sub_b)
    offset = jnp.sum(jnp.where(ahead, count_row, 0.0), axis=1, keepdims=True).astype(jnp.int32)
    place = owner * (rows * lanes) + offset
    place_f = jnp.broadcast_to(place.astype(F32), (bricks, bricks))
    place_row = jnp.sum(jnp.where(eye, place_f, 0.0), axis=0, keepdims=True).astype(jnp.int32)
    shift = jnp.broadcast_to(place & (lanes - 1), (bricks, lanes))
    meta[...] = jnp.broadcast_to(place * (2 * lanes) + count_col, (bricks, lanes))
    in_use = lane < count_col
    vx, vy, vz = velocity[0], velocity[1], velocity[2]
    kinetic = jnp.where(in_use, 0.5 * (vx * vx + vy * vy + vz * vz), 0.0)
    col = column[...]
    x_cell = quotient(col, width_y)
    y_cell = col - x_cell * width_y
    row = (plane[...] - owner * planes) * width_x + x_cell + 1
    code = jnp.where(in_use, row * width_y + y_cell, 0)
    turned = (lane - shift) & (lanes - 1)
    kinetic = jnp.take_along_axis(kinetic, turned, axis=1)
    code = jnp.take_along_axis(code, turned, axis=1)
    row = quotient(code, width_y)
    y_cell = code - row * width_y
    parts = split(kinetic, 2) + [row.astype(F32).astype(BF16), y_cell.astype(F32).astype(BF16)]
    first = lane >= shift
    zero = jnp.zeros((bricks, lanes), BF16)
    values = jnp.concatenate(
        [
            jnp.concatenate([jnp.where(first, part, zero) for part in parts], axis=1),
            jnp.concatenate([jnp.where(first, zero, part) for part in parts], axis=1),
        ],
        axis=0,
    )
    target = quotient(place_row, lanes)
    slot = iota((slabs * rows, bricks), 0)
    spots = jnp.concatenate([slot == target, slot == target + 1], axis=1)
    moved = jnp.dot(
        jnp.where(spots, 1.0, 0.0).astype(BF16), values, preferred_element_type=F32
    )
    send[:, 0] = (moved[:, :lanes] + moved[:, lanes : 2 * lanes]).reshape(slabs, rows, lanes)
    send[:, 1] = (moved[:, 2 * lanes : 3 * lanes] * width_y + moved[:, 3 * lanes :]).reshape(
        slabs, rows, lanes
    )


def filled_rows(got):
    slabs, _, rows, lanes = got.shape
    codes = got[:, 1]
    heights = iota((slabs, rows, lanes), 1).astype(F32) + 1.0
    return jnp.max(jnp.where(codes > 0.0, heights, 0.0)).astype(jnp.int32)


def decode(code, width_y):
    row = jnp.floor((code + 0.5) * (1.0 / width_y))
    return row, code - row * width_y


def bin_kernel(
    dims, got, temp, below, x_low, x_high, summary, factors, lhs, rhs, totals
):
    planes, width_x, width_y = dims
    slabs, _, rows, lanes = got.shape
    cells = planes * width_x
    one = jnp.ones((), BF16)
    zero = jnp.zeros((), BF16)
    row_id = (iota((cells, lanes), 0) + 1).astype(F32).astype(BF16)
    y_id = iota((width_y, lanes), 0).astype(F32).astype(BF16)
    totals[...] = jnp.zeros(totals.shape, F32)

    def add_rows(turn, carry):
        kinetic = got[:, 0, pl.ds(turn, 1), :].reshape(slabs, lanes)
        code = got[:, 1, pl.ds(turn, 1), :].reshape(slabs, lanes)
        row, y_cell = decode(code, width_y)
        high, low = split(kinetic, 2)
        row = row.astype(BF16)
        y_cell = y_cell.astype(BF16)
        for s in range(slabs):
            here = pl.ds(s * lanes, lanes)
            hit = row_id == row[s : s + 1]
            lhs[pl.ds(0, cells), here] = jnp.where(hit, high[s : s + 1], zero)
            lhs[pl.ds(cells, cells), here] = jnp.where(hit, low[s : s + 1], zero)
            lhs[pl.ds(2 * cells, cells), here] = jnp.where(hit, one, zero)
            rhs[:, here] = jnp.where(y_id == y_cell[s : s + 1], one, zero)
        totals[...] += lax.dot_general(
            lhs[...], rhs[...], (((1,), (1,)), ((), ())), preferred_element_type=F32
        )
        return carry

    lax.fori_loop(0, filled_rows(got), add_rows, 0)

    def plane_terms(z):
        here = temp[z]
        x_minus = jnp.concatenate([x_low[z], here[:-1]], axis=0)
        x_plus = jnp.concatenate([here[1:], x_high[z]], axis=0)
        lateral = LATERAL * (
            x_minus
            + x_plus
            + pltpu.roll(here, 1, 1)
            + pltpu.roll(here, width_y - 1, 1)
            - 4.0 * here
        )
        at = z * width_x
        energy = totals[pl.ds(at, width_x), :] + totals[pl.ds(cells + at, width_x), :]
        count = totals[pl.ds(2 * cells + at, width_x), :]
        return here + COUPLE * count, here * here + lateral + COUPLE * TWO_THIRDS * energy

    start = temp[0]
    gate = jnp.where(
        lax.axis_index("gz") > 0, STIFFNESS * (0.5 * (start + below[0])), jnp.zeros_like(start)
    )
    excess, source = plane_terms(0)
    left_excess = jnp.zeros_like(start)
    left_source = jnp.zeros_like(start)
    for z in range(planes - 1):
        face = STIFFNESS * (0.5 * (temp[z + 1] + temp[z]))
        inverse = 1.0 / (gate + face + excess)
        to_left = gate * inverse
        to_right = face * inverse
        factors[z, 0] = to_left
        factors[z, 1] = to_right
        factors[z, 2] = source * inverse
        next_excess, next_source = plane_terms(z + 1)
        left_excess = left_excess + to_left * excess
        left_source = left_source + to_left * source
        gate = gate * to_right
        excess = next_excess + to_right * excess
        source = next_source + to_right * source
    for i, value in enumerate((gate, left_excess, left_source, excess, source)):
        summary[i] = value


def load_five(ref):
    return tuple(ref[i] for i in range(5))


def merge_kernel(level, last, mine, other, total):
    upper = (lax.axis_index("gz") & (1 << level)) != 0
    own = load_five(mine)
    came = load_five(other)
    low = tuple(jnp.where(upper, b, a) for a, b in zip(own, came))
    high = tuple(jnp.where(upper, a, b) for a, b in zip(own, came))
    joined = merge(low, high)
    if not last:
        for i in range(5):
            total[i] = joined[i]
        return
    in_upper = (lax.axis_index("gz") & (1 << (level + 1))) != 0
    end = jnp.zeros_like(joined[0])
    closed = suffix_step((end, end), joined)
    total[0] = jnp.where(in_upper, closed[0], joined[3])
    total[1] = jnp.where(in_upper, closed[1], joined[4])


def look_kernel(dims, levels, got, factors, *refs):
    planes, width_x, width_y = dims
    others = refs[1:levels]
    own = load_five(refs[0])
    far = refs[levels]
    new_temp, reply, rhs, table = refs[levels + 1 :]
    slabs, _, rows, lanes = got.shape
    cells = planes * width_x
    index = lax.axis_index("gz")
    zeros = jnp.zeros_like(own[0])
    top = (index & (1 << (levels - 1))) != 0
    before = (jnp.where(top, far[0], zeros + 1.0), jnp.where(top, far[1], zeros))
    after = (jnp.where(top, zeros, far[0]), jnp.where(top, zeros, far[1]))
    for level in range(levels - 2, -1, -1):
        upper = (index & (1 << level)) != 0
        segment = load_five(others[level])
        with_before = prefix_step(before, segment)
        with_after = suffix_step(after, segment)
        before = tuple(jnp.where(upper, a, b) for a, b in zip(with_before, before))
        after = tuple(jnp.where(upper, b, a) for a, b in zip(with_after, after))
    through = prefix_step(before, own)
    value = (through[1] + after[1]) / (through[0] + after[0])
    edge = (before[1] + own[2] + own[0] * value) / (before[0] + own[1] + own[0])

    def put(z, value):
        new_temp[z] = value
        high, low = split(value, 2)
        table[pl.ds(z * width_x, width_x), pl.ds(0, width_y)] = high
        table[pl.ds(z * width_x, width_x), pl.ds(width_y, width_y)] = low

    put(planes - 1, value)
    for z in range(planes - 2, -1, -1):
        value = factors[z, 2] + factors[z, 0] * edge + factors[z, 1] * value
        put(z, value)

    one = jnp.ones((), BF16)
    zero = jnp.zeros((), BF16)
    row_id = (iota((cells, lanes), 0) + 1).astype(F32)
    y_id = iota((width_y, lanes), 0).astype(F32).astype(BF16)
    reply[...] = jnp.zeros(reply.shape, F32)

    def find_rows(turn, carry):
        code = got[:, 1, pl.ds(turn, 1), :].reshape(slabs, lanes)
        row, y_cell = decode(code, width_y)
        y_cell = y_cell.astype(BF16)
        for s in range(slabs):
            here = pl.ds(s * lanes, lanes)
            hot = jnp.where(y_id == y_cell[s : s + 1], one, zero)
            rhs[pl.ds(0, width_y), here] = hot
            rhs[pl.ds(width_y, width_y), here] = hot
        picked = jnp.dot(table[...], rhs[...], preferred_element_type=F32)
        for s in range(slabs):
            chosen = jnp.where(row_id == row[s : s + 1], picked[:, s * lanes : (s + 1) * lanes], 0.0)
            reply[s, pl.ds(turn, 1), :] = jnp.sum(chosen, axis=0, keepdims=True)
        return carry

    lax.fori_loop(0, filled_rows(got), find_rows, 0)


def kick_kernel(returned, meta, velocity, noise, out):
    bricks, lanes = meta.shape
    slots = returned.shape[0]
    packed = meta[...]
    lane = iota((bricks, lanes), 1)
    place = quotient(packed, 2 * lanes)
    in_use = lane < packed - place * (2 * lanes)
    shift = place & (lanes - 1)
    target = quotient(place[:, 0:1], lanes)
    slot = iota((bricks, slots), 1)
    spots = jnp.concatenate([slot == target, slot == target + 1], axis=0)
    values = jnp.concatenate(split(returned[...], 3), axis=1)
    moved = jnp.dot(
        jnp.where(spots, 1.0, 0.0).astype(BF16), values, preferred_element_type=F32
    )
    moved = moved[:, :lanes] + moved[:, lanes : 2 * lanes] + moved[:, 2 * lanes :]
    found = jnp.where(lane >= shift, moved[:bricks], moved[bricks:])
    found = jnp.take_along_axis(found, (lane + shift) & (lanes - 1), axis=1)
    root = jnp.sqrt(2.0 * KICK_RATE * found)
    for i in range(3):
        out[i] = jnp.where(in_use, (1.0 - KICK_RATE) * velocity[i] + root * noise[i], 0.0)


def call(kernel, out_shape, scratch=()):
    return pl.pallas_call(
        kernel,
        out_shape=out_shape,
        scratch_shapes=list(scratch),
        compiler_params=pltpu.CompilerParams(vmem_limit_bytes=VMEM_LIMIT),
    )


def struct(*shape, dtype=F32):
    return jax.ShapeDtypeStruct(shape, dtype)


def body(atom_velocity, atom_noise, atom_plane, atom_column, brick_count, electron_temp):
    dims = electron_temp.shape
    planes, width_x, width_y = dims
    cells = planes * width_x
    slabs = lax.axis_size("gz")
    groups = lax.axis_size("gx")
    levels = slabs.bit_length() - 1
    assert slabs == 1 << levels and levels > 0
    bricks, lanes = atom_plane.shape
    rows = 2 * bricks // slabs

    send, meta = call(
        functools.partial(route_kernel, dims, slabs, rows),
        (struct(slabs, 2, rows, lanes), struct(bricks, lanes, dtype=jnp.int32)),
    )(atom_velocity, atom_plane, atom_column, brick_count.reshape(1, bricks))
    got = lax.all_to_all(send, "gz", split_axis=0, concat_axis=0, tiled=True)
    below = lax.ppermute(electron_temp[-1:], "gz", [(i, i + 1) for i in range(slabs - 1)])
    x_low = lax.ppermute(
        electron_temp[:, -1:], "gx", [(i, (i + 1) % groups) for i in range(groups)]
    )
    x_high = lax.ppermute(
        electron_temp[:, :1], "gx", [((i + 1) % groups, i) for i in range(groups)]
    )
    total, factors = call(
        functools.partial(bin_kernel, dims),
        (struct(5, width_x, width_y), struct(planes - 1, 3, width_x, width_y)),
        (
            pltpu.VMEM((3 * cells, slabs * lanes), BF16),
            pltpu.VMEM((width_y, slabs * lanes), BF16),
            pltpu.VMEM((3 * cells, width_y), F32),
        ),
    )(got, electron_temp, below, x_low, x_high)
    pieces = [total]
    for level in range(levels):
        other = lax.ppermute(total, "gz", [(i, i ^ (1 << level)) for i in range(slabs)])
        pieces.append(other)
        if level < levels - 1:
            last = level == levels - 2
            total = call(
                functools.partial(merge_kernel, level, last),
                struct(2 if last else 5, width_x, width_y),
            )(total, other)
    new_temp, reply = call(
        functools.partial(look_kernel, dims, levels),
        (struct(*dims), struct(slabs, rows, lanes)),
        (
            pltpu.VMEM((2 * width_y, slabs * lanes), BF16),
            pltpu.VMEM((cells, 2 * width_y), BF16),
        ),
    )(got, factors, *pieces)
    returned = lax.all_to_all(reply, "gz", split_axis=0, concat_axis=0, tiled=True)
    new_velocity = call(kick_kernel, struct(*atom_velocity.shape))(
        returned.reshape(slabs * rows, lanes), meta, atom_velocity, atom_noise
    )
    return (new_temp, new_velocity)


def solution(mesh):
    placed = (
        P(None, ("gz", "gx"), None),
        P(None, ("gz", "gx"), None),
        P(("gz", "gx"), None),
        P(("gz", "gx"), None),
        P(("gz", "gx")),
        P("gz", "gx", None),
    )
    return jax.shard_map(
        body,
        mesh=mesh,
        in_specs=placed,
        out_specs=(P("gz", "gx", None), P(None, ("gz", "gx"), None)),
        check_vma=False,
    )
```

time: 279 us -> 77.1 us (0.28); the launches traced: 274 us -> 77 us
  matrix products: 78 us -> 0 us
  waiting for transfers between devices: 72.8 us -> 13.4 us
  other arithmetic: 50.2 us -> 0 us
  starting transfers between devices: 53 us -> 22.7 us
  blocking collectives: 0 us -> 21 us
  Pallas kernels: 0 us -> 16 us
  local copies, waits for them, and re-layouts: 17.8 us -> 3.29 us
    dot_general x12 -> x0, matrix products: 78 us -> none  [the longest x4 40.9 us: add_block(): jnp.einsum('ar,ay->ry', row_hot * kinetic_block[:, None], y_hot, precisio...]
    all_to_all x5 -> x1, waiting for transfers between devices: 47.6 us -> 1.48 us  [body(): got = lax.all_to_all(send, 'gz', split_axis=0, concat_axis=0, tiled=True)]
    mul x12 -> x0, other arithmetic: 21.8 us -> none  [the longest x4 10.5 us: level_update(): upper_ratio * above_rows[2]]
    all_to_all x0 -> x1, blocking collectives: none -> 21 us  [body(): lax.all_to_all(reply, 'gz', split_axis=0, concat_axis=0, tiled=True)]
    all_to_all x5 -> x1, starting transfers between devices: 27.4 us -> 7.39 us  [body(): got = lax.all_to_all(send, 'gz', split_axis=0, concat_axis=0, tiled=True)]
    pallas_call x0 -> x6, Pallas kernels: none -> 16 us  [the longest x1 7.33 us: body(): call(functools.partial(bin_kernel, dims), (struct(5, width_x, width_y), s...]
    add x5 -> x0, other arithmetic: 13.6 us -> none  [the longest x4 13.5 us: level_update(): system[1] + lower_ratio * below_rows[2] + upper_ratio * above_rows[0]]
    ppermute x12 -> x6, waiting for transfers between devices: 25.2 us -> 11.9 us  [the longest x3 8.98 us: body(): lax.ppermute(total, 'gz', [(i, i ^ 1 << level) for i in range(slabs)])]
  transfers between devices with their start and end apart: 17 -> 7, of which waited for: 13 -> 7; matrix products, arithmetic and copies ran while one was open for 7% -> 0% of each run, Pallas kernels for 0% -> 0%
where the time goes in v1:
time: 77.1 us; the launch traced here: 77 us
  starting transfers between devices  22.7 us (29%)
  blocking collectives  21 us (27%)
  Pallas kernels  16 us (21%)
  waiting for transfers between devices  13.4 us (17%)
  local copies, waits for them, and re-layouts  3.29 us (4%)
    all_to_all x1, blocking collectives, body(): lax.all_to_all(reply, 'gz', split_axis=0, concat_axis=0, tiled=True)  21 us
    ppermute x3, starting transfers between devices, body(): lax.ppermute(total, 'gz', [(i, i ^ 1 << level) for i in range(slabs)])  10.8 us
    ppermute x3, waiting for transfers between devices, body(): lax.ppermute(total, 'gz', [(i, i ^ 1 << level) for i in range(slabs)])  8.98 us
    all_to_all x1, starting transfers between devices, body(): got = lax.all_to_all(send, 'gz', split_axis=0, concat_axis=0, tiled=True)  7.39 us
    pallas_call x1, Pallas kernels, body(): call(functools.partial(bin_kernel, dims), (struct(5, width_x, width_y), s...  7.33 us
    pallas_call x1, Pallas kernels, body(): call(functools.partial(look_kernel, dims, levels), (struct(*dims), struct...  6.22 us
    ppermute x1, starting transfers between devices, body(): lax.ppermute(electron_temp[-1:], 'gz', [(i, i + 1) for i in range(slabs -...  3.92 us
    unnamed x14, local copies, waits for them, and re-layouts  3.26 us
  transfers between devices with their start and end apart: 7, of which 7 were waited for; matrix products, arithmetic and copies ran while one was open for 0% of the time, Pallas kernels for 0%

profile of v1, /device:TPU:0, one launch (start us, length us, event | category | flops | bytes accessed | tf_op | source)
XLA Modules:
  0.0 77.0 jit_solution(13554235424075946563)
XLA Ops:
  0.6 0.0 copy-start.6
  0.6 0.6 copy-done.6
  1.3 0.9 %copy-done = f32[3,128,128]{2,1,0:T(8,128)S(1)} copy-done((f32[3,128,128]{2,1,0:T(8,128)S(1)}, f32[3,128,128]{2,1,0:T(8,128)}, u32[]{:S(2)}) %copy-start) | copy-done | bytes 196632
  2.2 0.8 %copy-done.4 = s32[128,128]{1,0:T(8,128)S(1)} copy-done((s32[128,128]{1,0:T(8,128)S(1)}, s32[128,128]{1,0:T(8,128)}, u32[]{:S(2)}) %copy-start.4) | copy-done | bytes 65560
  3.1 0.8 %copy-done.5 = s32[128,128]{1,0:T(8,128)S(1)} copy-done((s32[128,128]{1,0:T(8,128)S(1)}, s32[128,128]{1,0:T(8,128)}, u32[]{:S(2)}) %copy-start.5) | copy-done | bytes 65560
  3.9 1.3 %shard_map.77 = (f32[8,2,32,128]{3,2,1,0:T(8,128)}, s32[128,128]{1,0:T(8,128)S(1)}) custom-call(f32[3,128,128]{2,1,0:T(8,128)S(1)} %copy-done, s32[128,128]{1,0:T(8,128)S(1)} %copy-done.4, s32[128,128]{1,0:T(8,128)S(1)} %copy-done.5, s32[1,128]{1,0:T(1,128)S(1)} %bitcast.3), custom_call_target="tpu_custom_call" | custom-call | tf_op jit(solution)/shard_map/pallas_call | solution.py:340
  5.2 7.4 %all-to-all-start = ((f32[8,2,32,128]{3,2,1,0:T(8,128)}), f32[8,2,32,128]{3,2,1,0:T(8,128)S(1)}, u32[]{:S(2)}, u32[]{:S(2)}) async-start(f32[8,2,32,128]{3,2,1,0:T(8,128)} %get-tuple-element.8), calls=%async_computation | async-start | bytes 524288 | tf_op jit(solution)/shard_map/all_to_all | solution.py:344
  12.6 3.9 %collective-permute-start = (f32[1,16,256]{2,1,0:T(8,128)S(1)}, f32[1,16,256]{2,1,0:T(8,128)S(1)}, u32[]{:S(2)}, u32[]{:S(2)}) collective-permute-start(f32[1,16,256]{2,1,0:T(8,128)S(1)} %slice.9), channel_id=1, source_target_pairs={{0,4},{4,8},{8,12},{12,16},{16,20},{20,24},{24,28},{1,5},{5,9},{9,... | collective-permute-start | bytes 49160 | tf_op jit(solution)/shard_map/ppermute | solution.py:345
  16.6 0.2 collective-permute-start.2
  16.8 0.4 collective-permute-start.1
  17.2 0.8 %collective-permute-done.below = f32[1,16,256]{2,1,0:T(8,128)S(1)} collective-permute-done((f32[1,16,256]{2,1,0:T(8,128)S(1)}, f32[1,16,256]{2,1,0:T(8,128)S(1)}, u32[]{:S(2)}, u32[]{:S(2)}) %collective-permute-start) | collective-permute-done | bytes 16416 | tf_op jit(solution)/shard_map/ppermute | solution.py:345
  18.0 0.2 collective-permute-done.2.x_high
  18.2 1.8 %collective-permute-done.1.x_low = f32[16,1,256]{2,1,0:T(1,128)S(1)} collective-permute-done((f32[16,1,256]{2,1,0:T(1,128)S(1)}, f32[16,1,256]{2,1,0:T(1,128)S(1)}, u32[]{:S(2)}, u32[]{:S(2)}) %collective-permute-start.1) | collective-permute-done | bytes 16416 | tf_op jit(solution)/shard_map/ppermute | solution.py:346
  20.1 1.5 %all-to-all-done.got = f32[8,2,32,128]{3,2,1,0:T(8,128)S(1)} async-done(((f32[8,2,32,128]{3,2,1,0:T(8,128)}), f32[8,2,32,128]{3,2,1,0:T(8,128)S(1)}, u32[]{:S(2)}, u32[]{:S(2)}) %all-to-all-start) | async-done | bytes 262176 | tf_op jit(solution)/shard_map/all_to_all | solution.py:344
  21.5 7.3 %shard_map.78 = (f32[5,16,256]{2,1,0:T(8,128)S(1)}, f32[15,3,16,256]{3,2,1,0:T(8,128)S(1)}) custom-call(f32[8,2,32,128]{3,2,1,0:T(8,128)S(1)} %all-to-all-done.got, f32[16,16,256]{2,1,0:T(8,128)S(1)} %copy-done.2, f32[1,16,256]{2,1,0:T(8,128)S(1)} %collective-permute-done.below, f32[16,1,256]{2,1,0:T(1,128)S(1)} %collective-permute-done.1.x_low, ...), custom_call_target="tpu_custom_call" | custom-call | tf_op jit(solution)/shard_map/pallas_call | solution.py:352
  28.9 0.8 %collective-permute-start.3 = (f32[5,16,256]{2,1,0:T(8,128)S(1)}, f32[5,16,256]{2,1,0:T(8,128)S(1)}, u32[]{:S(2)}, u32[]{:S(2)}) collective-permute-start(f32[5,16,256]{2,1,0:T(8,128)S(1)} %get-tuple-element.10.mine.refs_0_), channel_id=1, source_target_pairs={{0,4},{4,0},{8,12},{12,8},{16,20},{20,16},{24,28},{28,24},{1,5},{5... | collective-permute-start | bytes 245768 | tf_op jit(solution)/shard_map/ppermute | solution.py:363
  29.7 3.7 %collective-permute-done.3.other.refs_1_ = f32[5,16,256]{2,1,0:T(8,128)S(1)} collective-permute-done((f32[5,16,256]{2,1,0:T(8,128)S(1)}, f32[5,16,256]{2,1,0:T(8,128)S(1)}, u32[]{:S(2)}, u32[]{:S(2)}) %collective-permute-start.3) | collective-permute-done | bytes 81952 | tf_op jit(solution)/shard_map/ppermute | solution.py:363
  33.4 1.1 %collective-permute-start.4 = (f32[5,16,256]{2,1,0:T(8,128)S(1)}, f32[5,16,256]{2,1,0:T(8,128)S(1)}, u32[]{:S(2)}, u32[]{:S(2)}) collective-permute-start(f32[5,16,256]{2,1,0:T(8,128)S(1)} %shard_map.79.mine), channel_id=1, source_target_pairs={{0,8},{4,12},{8,0},{12,4},{16,24},{20,28},{24,16},{28,20},{1,9},{5... | collective-permute-start | bytes 245768 | tf_op jit(solution)/shard_map/ppermute | solution.py:363
  34.5 3.4 %collective-permute-done.4.other.refs_2_ = f32[5,16,256]{2,1,0:T(8,128)S(1)} collective-permute-done((f32[5,16,256]{2,1,0:T(8,128)S(1)}, f32[5,16,256]{2,1,0:T(8,128)S(1)}, u32[]{:S(2)}, u32[]{:S(2)}) %collective-permute-start.4) | collective-permute-done | bytes 81952 | tf_op jit(solution)/shard_map/ppermute | solution.py:363
  38.0 8.9 %collective-permute-start.5 = (f32[2,16,256]{2,1,0:T(8,128)S(1)}, f32[2,16,256]{2,1,0:T(8,128)S(1)}, u32[]{:S(2)}, u32[]{:S(2)}) collective-permute-start(f32[2,16,256]{2,1,0:T(8,128)S(1)} %shard_map.80), channel_id=1, source_target_pairs={{0,16},{4,20},{8,24},{12,28},{16,0},{20,4},{24,8},{28,12},{1,17},{... | collective-permute-start | bytes 98312 | tf_op jit(solution)/shard_map/ppermute | solution.py:363
  46.8 1.9 %collective-permute-done.5.refs_3_ = f32[2,16,256]{2,1,0:T(8,128)S(1)} collective-permute-done((f32[2,16,256]{2,1,0:T(8,128)S(1)}, f32[2,16,256]{2,1,0:T(8,128)S(1)}, u32[]{:S(2)}, u32[]{:S(2)}) %collective-permute-start.5) | collective-permute-done | bytes 32800 | tf_op jit(solution)/shard_map/ppermute | solution.py:363
  48.7 6.2 %shard_map.81 = (f32[16,16,256]{2,1,0:T(8,128)}, f32[8,32,128]{2,1,0:T(8,128)S(1)}) custom-call(f32[8,2,32,128]{3,2,1,0:T(8,128)S(1)} %all-to-all-done.got, f32[15,3,16,256]{3,2,1,0:T(8,128)S(1)} %get-tuple-element.9.factors, f32[5,16,256]{2,1,0:T(8,128)S(1)} %get-tuple-element.10.mine.refs_0_, f32[5,16,256]{2,1,0:T(8,128)S(1)} %collective-permute-done.3.other.refs_1_, ...), custom_call_target="tpu_custom_call" | custom-call | tf_op jit(solution)/shard_map/pallas_call | solution.py:371
  55.0 21.0 %all_to_all.10 = f32[8,32,128]{2,1,0:T(8,128)S(1)} all-to-all(f32[8,32,128]{2,1,0:T(8,128)S(1)} %get-tuple-element.12), channel_id=1, replica_groups=mesh['gz'=8,'gx'=4] {'gz'}, dimensions={0} | all-to-all | bytes 262144 | tf_op jit(solution)/shard_map/all_to_all | solution.py:379
  76.0 1.0 %shard_map.82 = f32[3,128,128]{2,1,0:T(8,128)} custom-call(f32[256,128]{1,0:T(8,128)S(1)} %bitcast.2, s32[128,128]{1,0:T(8,128)S(1)} %get-tuple-element.13.meta, f32[3,128,128]{2,1,0:T(8,128)S(1)} %copy-done.1, f32[3,128,128]{2,1,0:T(8,128)S(1)} %copy-done.3), custom_call_target="tpu_custom_call" | custom-call | tf_op jit(solution)/shard_map/pallas_call | solution.py:380
  (13 shorter events, 0.1 us)
Async XLA Ops:
  0.6 0.7 copy-start.6
  1.3 0.9 %copy-start = (f32[3,128,128]{2,1,0:T(8,128)S(1)}, f32[3,128,128]{2,1,0:T(8,128)}, u32[]{:S(2)}) copy-start(f32[3,128,128]{2,1,0:T(8,128)} %velocity.3) | copy-start | bytes 589828
  2.2 0.8 %copy-start.4 = (s32[128,128]{1,0:T(8,128)S(1)}, s32[128,128]{1,0:T(8,128)}, u32[]{:S(2)}) copy-start(s32[128,128]{1,0:T(8,128)} %plane.1) | copy-start | bytes 196612
  3.1 0.8 %copy-start.5 = (s32[128,128]{1,0:T(8,128)S(1)}, s32[128,128]{1,0:T(8,128)}, u32[]{:S(2)}) copy-start(s32[128,128]{1,0:T(8,128)} %column.1) | copy-start | bytes 196612
  5.2 7.4 %copy-start.2 = (f32[16,16,256]{2,1,0:T(8,128)S(1)}, f32[16,16,256]{2,1,0:T(8,128)}, u32[]{:S(2)}) copy-start(f32[16,16,256]{2,1,0:T(8,128)} %temp.1) | copy-start | bytes 786436
  5.2 16.3 %all-to-all-start = ((f32[8,2,32,128]{3,2,1,0:T(8,128)}), f32[8,2,32,128]{3,2,1,0:T(8,128)S(1)}, u32[]{:S(2)}, u32[]{:S(2)}) async-start(f32[8,2,32,128]{3,2,1,0:T(8,128)} %get-tuple-element.8), calls=%async_computation | async-start | bytes 524288 | tf_op jit(solution)/shard_map/all_to_all | solution.py:344
  12.6 5.4 %collective-permute-start = (f32[1,16,256]{2,1,0:T(8,128)S(1)}, f32[1,16,256]{2,1,0:T(8,128)S(1)}, u32[]{:S(2)}, u32[]{:S(2)}) collective-permute-start(f32[1,16,256]{2,1,0:T(8,128)S(1)} %slice.9), channel_id=1, source_target_pairs={{0,4},{4,8},{8,12},{12,16},{16,20},{20,24},{24,28},{1,5},{5,9},{9,... | collective-permute-start | bytes 49160 | tf_op jit(solution)/shard_map/ppermute | solution.py:345
  16.6 1.6 %collective-permute-start.2 = (f32[16,1,256]{2,1,0:T(1,128)S(1)}, f32[16,1,256]{2,1,0:T(1,128)S(1)}, u32[]{:S(2)}, u32[]{:S(2)}) collective-permute-start(f32[16,1,256]{2,1,0:T(1,128)S(1)} %get-tuple-element.14), channel_id=1, source_target_pairs={{1,0},{2,1},{3,2},{0,3},{5,4},{6,5},{7,6},{4,7},{9,8},{10,9},{11,1... | collective-permute-start | bytes 49160 | tf_op jit(solution)/shard_map/ppermute | solution.py:349
  16.8 3.3 %collective-permute-start.1 = (f32[16,1,256]{2,1,0:T(1,128)S(1)}, f32[16,1,256]{2,1,0:T(1,128)S(1)}, u32[]{:S(2)}, u32[]{:S(2)}) collective-permute-start(f32[16,1,256]{2,1,0:T(1,128)S(1)} %get-tuple-element.15), channel_id=1, source_target_pairs={{0,1},{1,2},{2,3},{3,0},{4,5},{5,6},{6,7},{7,4},{8,9},{9,10},{10,1... | collective-permute-start | bytes 49160 | tf_op jit(solution)/shard_map/ppermute | solution.py:346
  28.9 4.5 %collective-permute-start.3 = (f32[5,16,256]{2,1,0:T(8,128)S(1)}, f32[5,16,256]{2,1,0:T(8,128)S(1)}, u32[]{:S(2)}, u32[]{:S(2)}) collective-permute-start(f32[5,16,256]{2,1,0:T(8,128)S(1)} %get-tuple-element.10.mine.refs_0_), channel_id=1, source_target_pairs={{0,4},{4,0},{8,12},{12,8},{16,20},{20,16},{24,28},{28,24},{1,5},{5... | collective-permute-start | bytes 245768 | tf_op jit(solution)/shard_map/ppermute | solution.py:363
  33.4 4.5 %collective-permute-start.4 = (f32[5,16,256]{2,1,0:T(8,128)S(1)}, f32[5,16,256]{2,1,0:T(8,128)S(1)}, u32[]{:S(2)}, u32[]{:S(2)}) collective-permute-start(f32[5,16,256]{2,1,0:T(8,128)S(1)} %shard_map.79.mine), channel_id=1, source_target_pairs={{0,8},{4,12},{8,0},{12,4},{16,24},{20,28},{24,16},{28,20},{1,9},{5... | collective-permute-start | bytes 245768 | tf_op jit(solution)/shard_map/ppermute | solution.py:363
  38.0 10.8 %collective-permute-start.5 = (f32[2,16,256]{2,1,0:T(8,128)S(1)}, f32[2,16,256]{2,1,0:T(8,128)S(1)}, u32[]{:S(2)}, u32[]{:S(2)}) collective-permute-start(f32[2,16,256]{2,1,0:T(8,128)S(1)} %shard_map.80), channel_id=1, source_target_pairs={{0,16},{4,20},{8,24},{12,28},{16,0},{20,4},{24,8},{28,12},{1,17},{... | collective-permute-start | bytes 98312 | tf_op jit(solution)/shard_map/ppermute | solution.py:363
  48.7 27.2 %copy-start.3 = (f32[3,128,128]{2,1,0:T(8,128)S(1)}, f32[3,128,128]{2,1,0:T(8,128)}, u32[]{:S(2)}) copy-start(f32[3,128,128]{2,1,0:T(8,128)} %noise.1) | copy-start | bytes 589828
  55.0 21.0 %copy-start.1 = (f32[3,128,128]{2,1,0:T(8,128)S(1)}, f32[3,128,128]{2,1,0:T(8,128)}, u32[]{:S(2)}) copy-start(f32[3,128,128]{2,1,0:T(8,128)} %velocity.3) | copy-start | bytes 589828

commit v2 on v1

v2 whole, which is shorter than its diff:
```python
import functools

import jax
import jax.numpy as jnp
from jax import lax
from jax.experimental import pallas as pl
from jax.experimental.pallas import tpu as pltpu
from jax.sharding import PartitionSpec as P

STIFFNESS = 10000.0
LATERAL = 0.1
COUPLE = 0.5
TWO_THIRDS = 2.0 / 3.0
KICK_RATE = 0.2
F32 = jnp.float32
BF16 = jnp.bfloat16
F8 = jnp.float8_e4m3fn
SCALE = 8.0
STEP = 16.0
PIECES = 3
PARTS = 4
ROUTE_LIMIT = 63 * 1024 * 1024
VMEM_LIMIT = 48 * 1024 * 1024


def quotient(value, size):
    if size & (size - 1) == 0:
        return lax.shift_right_logical(value, size.bit_length() - 1)
    return value // size


def iota(shape, dim):
    return lax.broadcasted_iota(jnp.int32, shape, dim)


def split(value, pieces):
    parts = []
    for _ in range(pieces):
        part = value.astype(BF16)
        parts.append(part)
        value = value - part.astype(F32)
    return parts


def split_small(value):
    value = value * SCALE
    parts = []
    for _ in range(PIECES):
        part = value.astype(F8)
        parts.append(part)
        value = (value - part.astype(F32)) * STEP
    return parts


def join_small(parts):
    total = parts[-1]
    for part in parts[-2::-1]:
        total = part + total * (1.0 / STEP)
    return total * (1.0 / SCALE)


def merge(left, right):
    g_a, sl_a, rl_a, s_a, r_a = left
    g_b, sl_b, rl_b, s_b, r_b = right
    excess = s_a + sl_b
    source = r_a + rl_b
    inverse = 1.0 / (g_a + g_b + excess)
    to_left = g_a * inverse
    to_right = g_b * inverse
    return (
        g_a * to_right,
        sl_a + to_left * excess,
        rl_a + to_left * source,
        s_b + to_right * excess,
        r_b + to_right * source,
    )


def prefix_step(state, segment):
    gate, sl, rl, s, r = segment
    excess = state[0] + sl
    source = state[1] + rl
    ratio = gate / (gate + excess)
    return (s + ratio * excess, r + ratio * source)


def suffix_step(state, segment):
    gate, sl, rl, s, r = segment
    excess = s + state[0]
    source = r + state[1]
    ratio = gate / (gate + excess)
    return (sl + ratio * excess, rl + ratio * source)


def route_kernel(
    dims, slabs, rows, parts, count, velocity_hbm, plane_hbm, column_hbm, send, meta, starts,
    velocity, plane, column, arrived,
):
    copies = [
        pltpu.make_async_copy(source, target, arrived.at[i])
        for i, (source, target) in enumerate(
            ((plane_hbm, plane), (column_hbm, column), (velocity_hbm, velocity))
        )
    ]
    for copy in copies:
        copy.start()
    planes, width_x, width_y = dims
    bricks, lanes = plane.shape
    part_rows = planes * width_x // parts
    lane = iota((bricks, lanes), 1)
    sub_b = iota((bricks, bricks), 0)
    lane_b = iota((bricks, bricks), 1)
    eye = sub_b == lane_b
    count_row = jnp.broadcast_to(count[...].astype(F32), (bricks, bricks))
    count_col = jnp.sum(jnp.where(eye, count_row, 0.0), axis=1, keepdims=True).astype(jnp.int32)
    in_use = lane < count_col
    sub_l = iota((lanes, lanes), 0)
    lane_l = iota((lanes, lanes), 1)
    prefix = jnp.concatenate(
        [jnp.where(sub_l <= lane_l, 1.0, 0.0), jnp.ones((lanes, lanes), F32)], axis=1
    ).astype(BF16)
    copies[0].wait()
    owner = quotient(plane[:, 0:1], planes)
    owner_f = jnp.broadcast_to(owner.astype(F32), (bricks, bricks))
    owner_row = jnp.sum(jnp.where(eye, owner_f, 0.0), axis=0, keepdims=True)
    same = owner_f == owner_row
    ahead = same & (lane_b < sub_b)
    peers = jnp.where(jnp.concatenate([same, ahead], axis=1), 1.0, 0.0).astype(BF16)
    copies[1].wait()
    col = column[...]
    x_cell = quotient(col, width_y)
    y_cell = col - x_cell * width_y
    row = (plane[...] - owner * planes) * width_x + x_cell
    code = jnp.where(in_use, (row + 1) * width_y + y_cell, 0)
    part = jnp.where(in_use, quotient(row, part_rows), parts)
    inside = [jnp.where(part == c, 1.0, 0.0).astype(BF16) for c in range(parts)]
    sums = jnp.dot(jnp.concatenate(inside, axis=0), prefix, preferred_element_type=F32)
    ranks = [sums[c * bricks : (c + 1) * bricks, :lanes] for c in range(parts)]
    sizes = [sums[c * bricks : (c + 1) * bricks, lanes:] for c in range(parts)]
    earlier = [jnp.zeros_like(sizes[0])]
    for c in range(parts - 1):
        earlier.append(earlier[-1] + sizes[c])
    offsets = jnp.dot(
        peers,
        jnp.concatenate(
            [jnp.concatenate(earlier, axis=1), jnp.concatenate(sizes, axis=1)], axis=0
        ).astype(BF16),
        preferred_element_type=F32,
    )
    copies[2].wait()
    vx, vy, vz = velocity[0], velocity[1], velocity[2]
    kinetic = 0.5 * (vx * vx + vy * vy + vz * vz)
    zero = jnp.zeros((bricks, lanes), BF16)
    slot = iota((slabs * rows, bricks), 0)
    values = []
    spots = []
    place = jnp.full((bricks, lanes), -1, jnp.int32)
    for c in range(parts):
        start = offsets[:, c * lanes : (c + 1) * lanes].astype(jnp.int32) + owner * (rows * lanes)
        starts[c] = start
        place = jnp.where(
            part == c, (start + ranks[c].astype(jnp.int32) - 1) * parts + c, place
        )
        shift = start & (lanes - 1)
        wanted = (lane - shift) & (lanes - 1)
        wanted_f = wanted.astype(F32)
        found = jnp.zeros((bricks, lanes), jnp.int32)
        step = lanes // 2
        while step:
            at = jnp.take_along_axis(ranks[c], found + (step - 1), axis=1)
            found = jnp.where(at <= wanted_f, found + step, found)
            step //= 2
        valid = wanted_f < sizes[c]
        kin = jnp.where(valid, jnp.take_along_axis(kinetic, found, axis=1), 0.0)
        cell = jnp.where(valid, jnp.take_along_axis(code, found, axis=1), 0)
        cell_row = quotient(cell, width_y)
        cell_y = cell - cell_row * width_y
        pieces = split(kin, 2) + [cell_row.astype(F32).astype(BF16), cell_y.astype(F32).astype(BF16)]
        first = lane >= shift
        values.append(jnp.concatenate([jnp.where(first, p, zero) for p in pieces], axis=1))
        values.append(jnp.concatenate([jnp.where(first, zero, p) for p in pieces], axis=1))
        start_row = jnp.sum(
            jnp.where(eye, start.astype(F32), 0.0), axis=0, keepdims=True
        ).astype(jnp.int32)
        target = quotient(start_row, lanes)
        spots.append(slot == target)
        spots.append(slot == target + 1)
    meta[...] = place
    moved = jnp.dot(
        jnp.where(jnp.concatenate(spots, axis=1), 1.0, 0.0).astype(BF16),
        jnp.concatenate(values, axis=0),
        preferred_element_type=F32,
    )
    send[:, 0] = (moved[:, :lanes] + moved[:, lanes : 2 * lanes]).reshape(slabs, rows, lanes)
    send[:, 1] = (moved[:, 2 * lanes : 3 * lanes] * width_y + moved[:, 3 * lanes :]).reshape(
        slabs, rows, lanes
    )


def decode(code, width_y):
    row = jnp.floor((code + 0.5) * (1.0 / width_y))
    return row, code - row * width_y


def find_runs(dims, parts, got, runs_vmem, runs, arrived):
    planes, width_x, width_y = dims
    slabs, _, rows, lanes = got.shape
    part_rows = planes * width_x // parts
    codes = got[:, 1]
    lane = iota((slabs, lanes), 1)
    table = jnp.zeros((slabs, lanes), jnp.int32)
    for c in range(1, parts + 1):
        limit = float((c * part_rows + 1) * width_y)
        below = jnp.where((codes > 0.0) & (codes < limit), 1.0, 0.0)
        ends = jnp.sum(jnp.sum(below, axis=1), axis=1, keepdims=True).astype(jnp.int32)
        table = jnp.where(lane == c, ends, table)
    runs_vmem[...] = table
    copy = pltpu.make_async_copy(runs_vmem, runs, arrived.at[0])
    copy.start()
    copy.wait()


def run_bounds(runs, parts, slabs, lanes):
    ends = [[runs[s, c] for s in range(slabs)] for c in range(parts + 1)]
    first = [[quotient(end, lanes) for end in ends[c]] for c in range(parts)]
    last = [[quotient(end + (lanes - 1), lanes) for end in ends[c + 1]] for c in range(parts)]
    longest = last[0][0] - first[0][0]
    for c in range(parts):
        for s in range(slabs):
            longest = jnp.maximum(longest, last[c][s] - first[c][s])
    return first, last, longest


def run_row(got, field, s, spot, last):
    rows = got.shape[2]
    loaded = got[s, field, pl.ds(jnp.minimum(spot, rows - 1), 1), :]
    return jnp.where(spot < last, loaded, 0.0)


def bin_kernel(
    dims, parts, got, temp, below, x_low, x_high, summary, factors,
    lhs, rhs, totals, runs_vmem, runs, arrived,
):
    planes, width_x, width_y = dims
    slabs, _, rows, lanes = got.shape
    part_rows = planes * width_x // parts
    one = jnp.ones((), F8)
    zero = jnp.zeros((), F8)
    y_id = iota((width_y, lanes), 0).astype(F32).astype(BF16)
    totals[...] = jnp.zeros(totals.shape, F32)
    find_runs(dims, parts, got, runs_vmem, runs, arrived)
    first, last, longest = run_bounds(runs, parts, slabs, lanes)

    def add_rows(turn, carry):
        for c in range(parts):
            row_id = (iota((part_rows, lanes), 0) + (c * part_rows + 1)).astype(F32).astype(BF16)
            for s in range(slabs):
                spot = first[c][s] + turn
                pieces = split_small(run_row(got, 0, s, spot, last[c][s]))
                row, y_cell = decode(run_row(got, 1, s, spot, last[c][s]), width_y)
                here = pl.ds(s * lanes, lanes)
                hit = row_id == row.astype(BF16)
                for i, piece in enumerate(pieces):
                    lhs[c, pl.ds(i * part_rows, part_rows), here] = jnp.where(hit, piece, zero)
                lhs[c, pl.ds(PIECES * part_rows, part_rows), here] = jnp.where(hit, one, zero)
                rhs[c, :, here] = jnp.where(y_id == y_cell.astype(BF16), one, zero)
        for c in range(parts):
            totals[c] += lax.dot_general(
                lhs[c], rhs[c], (((1,), (1,)), ((), ())), preferred_element_type=F32
            )
        return carry

    lax.fori_loop(0, longest, add_rows, 0)

    def plane_terms(z):
        here = temp[z]
        x_minus = jnp.concatenate([x_low[z], here[:-1]], axis=0)
        x_plus = jnp.concatenate([here[1:], x_high[z]], axis=0)
        lateral = LATERAL * (
            x_minus
            + x_plus
            + pltpu.roll(here, 1, 1)
            + pltpu.roll(here, width_y - 1, 1)
            - 4.0 * here
        )
        c, at = divmod(z * width_x, part_rows)
        energy = join_small(
            [totals[c, pl.ds(i * part_rows + at, width_x), :] for i in range(PIECES)]
        )
        count = totals[c, pl.ds(PIECES * part_rows + at, width_x), :]
        return here + COUPLE * count, here * here + lateral + COUPLE * TWO_THIRDS * energy

    start = temp[0]
    gate = jnp.where(
        lax.axis_index("gz") > 0, STIFFNESS * (0.5 * (start + below[0])), jnp.zeros_like(start)
    )
    excess, source = plane_terms(0)
    left_excess = jnp.zeros_like(start)
    left_source = jnp.zeros_like(start)
    for z in range(planes - 1):
        face = STIFFNESS * (0.5 * (temp[z + 1] + temp[z]))
        inverse = 1.0 / (gate + face + excess)
        to_left = gate * inverse
        to_right = face * inverse
        factors[z, 0] = to_left
        factors[z, 1] = to_right
        factors[z, 2] = source * inverse
        next_excess, next_source = plane_terms(z + 1)
        left_excess = left_excess + to_left * excess
        left_source = left_source + to_left * source
        gate = gate * to_right
        excess = next_excess + to_right * excess
        source = next_source + to_right * source
    for i, value in enumerate((gate, left_excess, left_source, excess, source)):
        summary[i] = value


def load_five(ref):
    return tuple(ref[i] for i in range(5))


def merge_kernel(level, last, mine, other, total):
    upper = (lax.axis_index("gz") & (1 << level)) != 0
    own = load_five(mine)
    came = load_five(other)
    low = tuple(jnp.where(upper, b, a) for a, b in zip(own, came))
    high = tuple(jnp.where(upper, a, b) for a, b in zip(own, came))
    joined = merge(low, high)
    if not last:
        for i in range(5):
            total[i] = joined[i]
        return
    in_upper = (lax.axis_index("gz") & (1 << (level + 1))) != 0
    end = jnp.zeros_like(joined[0])
    closed = suffix_step((end, end), joined)
    total[0] = jnp.where(in_upper, closed[0], joined[3])
    total[1] = jnp.where(in_upper, closed[1], joined[4])


def look_kernel(dims, parts, levels, got, factors, *refs):
    planes, width_x, width_y = dims
    others = refs[1:levels]
    own = load_five(refs[0])
    far = refs[levels]
    new_temp, reply, rhs, table, runs_vmem, runs, arrived = refs[levels + 1 :]
    slabs, _, rows, lanes = got.shape
    part_rows = planes * width_x // parts
    find_runs(dims, parts, got, runs_vmem, runs, arrived)
    index = lax.axis_index("gz")
    zeros = jnp.zeros_like(own[0])
    top = (index & (1 << (levels - 1))) != 0
    before = (jnp.where(top, far[0], zeros + 1.0), jnp.where(top, far[1], zeros))
    after = (jnp.where(top, zeros, far[0]), jnp.where(top, zeros, far[1]))
    for level in range(levels - 2, -1, -1):
        upper = (index & (1 << level)) != 0
        segment = load_five(others[level])
        with_before = prefix_step(before, segment)
        with_after = suffix_step(after, segment)
        before = tuple(jnp.where(upper, a, b) for a, b in zip(with_before, before))
        after = tuple(jnp.where(upper, b, a) for a, b in zip(with_after, after))
    through = prefix_step(before, own)
    value = (through[1] + after[1]) / (through[0] + after[0])
    edge = (before[1] + own[2] + own[0] * value) / (before[0] + own[1] + own[0])

    def put(z, value):
        new_temp[z] = value

    put(planes - 1, value)
    for z in range(planes - 2, -1, -1):
        value = factors[z, 2] + factors[z, 0] * edge + factors[z, 1] * value
        put(z, value)

    for c in range(parts):
        depth = planes // parts
        block = new_temp[pl.ds(c * depth, depth)].reshape(part_rows, width_y)
        for i, piece in enumerate(split_small(block)):
            table[c, pl.ds(i * part_rows, part_rows), :] = piece

    one = jnp.ones((), F8)
    zero = jnp.zeros((), F8)
    y_id = iota((width_y, lanes), 0).astype(F32).astype(BF16)
    reply[...] = jnp.zeros(reply.shape, F32)
    first, last, longest = run_bounds(runs, parts, slabs, lanes)

    def find_rows(turn, carry):
        wanted = []
        for c in range(parts):
            for s in range(slabs):
                row, y_cell = decode(run_row(got, 1, s, first[c][s] + turn, last[c][s]), width_y)
                wanted.append(row)
                rhs[c, :, pl.ds(s * lanes, lanes)] = jnp.where(
                    y_id == y_cell.astype(BF16), one, zero
                )
        for c in range(parts):
            row_id = (iota((part_rows, lanes), 0) + (c * part_rows + 1)).astype(F32)
            picked = jnp.dot(table[c], rhs[c], preferred_element_type=F32)
            picked = join_small(
                [picked[i * part_rows : (i + 1) * part_rows] for i in range(PIECES)]
            )
            for s in range(slabs):
                chosen = jnp.where(
                    row_id == wanted[c * slabs + s], picked[:, s * lanes : (s + 1) * lanes], 0.0
                )
                spot = pl.ds(jnp.minimum(first[c][s] + turn, rows - 1), 1)
                reply[s, spot, :] += jnp.sum(chosen, axis=0, keepdims=True)
        return carry

    lax.fori_loop(0, longest, find_rows, 0)


def kick_kernel(parts, returned, meta, starts, velocity, noise, out):
    bricks, lanes = meta.shape
    slots = returned.shape[0]
    packed = meta[...]
    lane = iota((bricks, lanes), 1)
    in_use = packed >= 0
    place = quotient(jnp.maximum(packed, 0), parts)
    part = jnp.maximum(packed, 0) - place * parts
    slot = iota((bricks, slots), 1)
    spots = []
    for c in range(parts):
        target = quotient(starts[c][:, 0:1], lanes)
        spots.append(slot == target)
        spots.append(slot == target + 1)
    values = jnp.concatenate(split(returned[...], 3), axis=1)
    moved = jnp.dot(
        jnp.where(jnp.concatenate(spots, axis=0), 1.0, 0.0).astype(BF16),
        values,
        preferred_element_type=F32,
    )
    moved = moved[:, :lanes] + moved[:, lanes : 2 * lanes] + moved[:, 2 * lanes :]
    at = place & (lanes - 1)
    temp = jnp.zeros((bricks, lanes), F32)
    for c in range(parts):
        here = moved[2 * c * bricks : (2 * c + 1) * bricks]
        after = moved[(2 * c + 1) * bricks : (2 * c + 2) * bricks]
        whole = jnp.where(lane >= (starts[c] & (lanes - 1)), here, after)
        temp = jnp.where(part == c, jnp.take_along_axis(whole, at, axis=1), temp)
    root = jnp.sqrt(2.0 * KICK_RATE * temp)
    for i in range(3):
        out[i] = jnp.where(in_use, (1.0 - KICK_RATE) * velocity[i] + root * noise[i], 0.0)


def call(kernel, out_shape, scratch=(), spaces=None, limit=VMEM_LIMIT):
    extra = {} if spaces is None else {"in_specs": [pl.BlockSpec(memory_space=m) for m in spaces]}
    return pl.pallas_call(
        kernel,
        out_shape=out_shape,
        **extra,
        scratch_shapes=list(scratch),
        compiler_params=pltpu.CompilerParams(vmem_limit_bytes=limit),
    )


def struct(*shape, dtype=F32):
    return jax.ShapeDtypeStruct(shape, dtype)


def body(atom_velocity, atom_noise, atom_plane, atom_column, brick_count, electron_temp):
    dims = electron_temp.shape
    planes, width_x, width_y = dims
    cells = planes * width_x
    slabs = lax.axis_size("gz")
    groups = lax.axis_size("gx")
    levels = slabs.bit_length() - 1
    assert slabs == 1 << levels and levels > 0
    bricks, lanes = atom_plane.shape
    rows = 2 * bricks // slabs
    parts = PARTS
    assert planes % parts == 0
    run_scratch = (
        pltpu.VMEM((slabs, lanes), jnp.int32),
        pltpu.SMEM((slabs, lanes), jnp.int32),
        pltpu.SemaphoreType.DMA((1,)),
    )

    send, meta, starts = call(
        functools.partial(route_kernel, dims, slabs, rows, parts),
        (
            struct(slabs, 2, rows, lanes),
            struct(bricks, lanes, dtype=jnp.int32),
            struct(parts, bricks, lanes, dtype=jnp.int32),
        ),
        (
            pltpu.VMEM(atom_velocity.shape, F32),
            pltpu.VMEM(atom_plane.shape, jnp.int32),
            pltpu.VMEM(atom_column.shape, jnp.int32),
            pltpu.SemaphoreType.DMA((3,)),
        ),
        (pltpu.VMEM, pltpu.HBM, pltpu.HBM, pltpu.HBM),
        ROUTE_LIMIT,
    )(brick_count.reshape(1, bricks), atom_velocity, atom_plane, atom_column)
    got = lax.all_to_all(send, "gz", split_axis=0, concat_axis=0, tiled=True)
    below = lax.ppermute(electron_temp[-1:], "gz", [(i, i + 1) for i in range(slabs - 1)])
    x_low = lax.ppermute(
        electron_temp[:, -1:], "gx", [(i, (i + 1) % groups) for i in range(groups)]
    )
    x_high = lax.ppermute(
        electron_temp[:, :1], "gx", [((i + 1) % groups, i) for i in range(groups)]
    )
    total, factors = call(
        functools.partial(bin_kernel, dims, parts),
        (struct(5, width_x, width_y), struct(planes - 1, 3, width_x, width_y)),
        (
            pltpu.VMEM((parts, (PIECES + 1) * cells // parts, slabs * lanes), F8),
            pltpu.VMEM((parts, width_y, slabs * lanes), F8),
            pltpu.VMEM((parts, (PIECES + 1) * cells // parts, width_y), F32),
        )
        + run_scratch,
    )(got, electron_temp, below, x_low, x_high)
    pieces = [total]
    for level in range(levels):
        other = lax.ppermute(total, "gz", [(i, i ^ (1 << level)) for i in range(slabs)])
        pieces.append(other)
        if level < levels - 1:
            last = level == levels - 2
            total = call(
                functools.partial(merge_kernel, level, last),
                struct(2 if last else 5, width_x, width_y),
            )(total, other)
    new_temp, reply = call(
        functools.partial(look_kernel, dims, parts, levels),
        (struct(*dims), struct(slabs, rows, lanes)),
        (
            pltpu.VMEM((parts, width_y, slabs * lanes), F8),
            pltpu.VMEM((parts, PIECES * cells // parts, width_y), F8),
        )
        + run_scratch,
    )(got, factors, *pieces)
    returned = lax.all_to_all(reply, "gz", split_axis=0, concat_axis=0, tiled=True)
    new_velocity = call(functools.partial(kick_kernel, parts), struct(*atom_velocity.shape))(
        returned.reshape(slabs * rows, lanes), meta, starts, atom_velocity, atom_noise
    )
    return (new_temp, new_velocity)


def solution(mesh):
    placed = (
        P(None, ("gz", "gx"), None),
        P(None, ("gz", "gx"), None),
        P(("gz", "gx"), None),
        P(("gz", "gx"), None),
        P(("gz", "gx")),
        P("gz", "gx", None),
    )
    return jax.shard_map(
        body,
        mesh=mesh,
        in_specs=placed,
        out_specs=(P("gz", "gx", None), P(None, ("gz", "gx"), None)),
        check_vma=False,
    )
```

time: 77.1 us -> 57.2 us (0.74)
  blocking collectives: 21 us -> 12 us
  starting transfers between devices: 22.7 us -> 16.5 us
  local copies, waits for them, and re-layouts: 3.29 us -> 0.06 us
  Pallas kernels: 16 us -> 13.1 us
  waiting for transfers between devices: 13.4 us -> 14.5 us
    all_to_all x1, blocking collectives: 21 us -> 12 us  [body(): lax.all_to_all(reply, 'gz', split_axis=0, concat_axis=0, tiled=True)]
    ppermute x3, starting transfers between devices: 10.8 us -> 4.65 us  [body(): lax.ppermute(total, 'gz', [(i, i ^ 1 << level) for i in range(slabs)])]
    unnamed x14 -> x10, local copies, waits for them, and re-layouts: 3.26 us -> 0.03 us
    pallas_call x4, Pallas kernels: 15.9 us -> 13 us  [the longest x1 4.9 us: body(): call(functools.partial(route_kernel, dims, slabs, rows, parts), (struct(s...]
    ppermute x3, waiting for transfers between devices: 8.98 us -> 10.1 us  [body(): lax.ppermute(total, 'gz', [(i, i ^ 1 << level) for i in range(slabs)])]
where the time goes in v2:
time: 57.2 us; the launch traced here: 56.9 us
  starting transfers between devices  16.5 us (29%)
  waiting for transfers between devices  14.5 us (25%)
  Pallas kernels  13.1 us (23%)
  blocking collectives  12 us (21%)
  between operations  0.74 us (1%)
    all_to_all x1, blocking collectives, body(): lax.all_to_all(reply, 'gz', split_axis=0, concat_axis=0, tiled=True)  12 us
    ppermute x3, waiting for transfers between devices, body(): lax.ppermute(total, 'gz', [(i, i ^ 1 << level) for i in range(slabs)])  10.1 us
    all_to_all x1, starting transfers between devices, body(): got = lax.all_to_all(send, 'gz', split_axis=0, concat_axis=0, tiled=True)  7.39 us
    pallas_call x1, Pallas kernels, body(): call(functools.partial(route_kernel, dims, slabs, rows, parts), (struct(s...  4.9 us
    ppermute x3, starting transfers between devices, body(): lax.ppermute(total, 'gz', [(i, i ^ 1 << level) for i in range(slabs)])  4.65 us
    ppermute x1, starting transfers between devices, body(): lax.ppermute(electron_temp[-1:], 'gz', [(i, i + 1) for i in range(slabs -...  3.92 us
    pallas_call x1, Pallas kernels, body(): call(functools.partial(look_kernel, dims, parts, levels), (struct(*dims),...  3.76 us
    pallas_call x1, Pallas kernels, body(): call(functools.partial(bin_kernel, dims, parts), (struct(5, width_x, widt...  3.1 us
  transfers between devices with their start and end apart: 7, of which 7 were waited for; matrix products, arithmetic and copies ran while one was open for 0% of the time, Pallas kernels for 0%

profile of v2, /device:TPU:0, one launch (start us, length us, event | category | flops | bytes accessed | tf_op | source)
XLA Modules:
  0.0 56.9 jit_solution(15617665288641027835)
XLA Ops:
  0.6 4.9 %shard_map.77 = (f32[8,2,32,128]{3,2,1,0:T(8,128)}, s32[128,128]{1,0:T(8,128)}, s32[4,128,128]{2,1,0:T(8,128)}) custom-call(s32[1,128]{1,0:T(1,128)} %bitcast.3, f32[3,128,128]{2,1,0:T(8,128)} %velocity.1, s32[128,128]{1,0:T(8,128)} %plane_hbm.1, s32[128,128]{1,0:T(8,128)} %column_hbm.1), custom_call_target="tpu_custom_call" | custom-call | tf_op jit(solution)/shard_map/pallas_call | solution.py:477
  5.5 0.0 copy-start.1
  5.6 7.4 %all-to-all-start = ((f32[8,2,32,128]{3,2,1,0:T(8,128)}), f32[8,2,32,128]{3,2,1,0:T(8,128)S(1)}, u32[]{:S(2)}, u32[]{:S(2)}) async-start(f32[8,2,32,128]{3,2,1,0:T(8,128)} %get-tuple-element.9), calls=%async_computation | async-start | bytes 524288 | tf_op jit(solution)/shard_map/all_to_all | solution.py:493
  12.9 0.0 copy-done.1
  13.0 3.9 %collective-permute-start = (f32[1,16,256]{2,1,0:T(8,128)S(1)}, f32[1,16,256]{2,1,0:T(8,128)S(1)}, u32[]{:S(2)}, u32[]{:S(2)}) collective-permute-start(f32[1,16,256]{2,1,0:T(8,128)S(1)} %slice.9), channel_id=1, source_target_pairs={{0,4},{4,8},{8,12},{12,16},{16,20},{20,24},{24,28},{1,5},{5,9},{9,... | collective-permute-start | bytes 49160 | tf_op jit(solution)/shard_map/ppermute | solution.py:494
  16.9 0.2 collective-permute-start.2
  17.1 0.4 collective-permute-start.1
  17.5 0.8 %collective-permute-done.below = f32[1,16,256]{2,1,0:T(8,128)S(1)} collective-permute-done((f32[1,16,256]{2,1,0:T(8,128)S(1)}, f32[1,16,256]{2,1,0:T(8,128)S(1)}, u32[]{:S(2)}, u32[]{:S(2)}) %collective-permute-start) | collective-permute-done | bytes 16416 | tf_op jit(solution)/shard_map/ppermute | solution.py:494
  18.3 0.2 collective-permute-done.2.x_high
  18.5 1.9 %collective-permute-done.1.x_low = f32[16,1,256]{2,1,0:T(1,128)S(1)} collective-permute-done((f32[16,1,256]{2,1,0:T(1,128)S(1)}, f32[16,1,256]{2,1,0:T(1,128)S(1)}, u32[]{:S(2)}, u32[]{:S(2)}) %collective-permute-start.1) | collective-permute-done | bytes 16416 | tf_op jit(solution)/shard_map/ppermute | solution.py:495
  20.4 1.5 %all-to-all-done.got = f32[8,2,32,128]{3,2,1,0:T(8,128)S(1)} async-done(((f32[8,2,32,128]{3,2,1,0:T(8,128)}), f32[8,2,32,128]{3,2,1,0:T(8,128)S(1)}, u32[]{:S(2)}, u32[]{:S(2)}) %all-to-all-start) | async-done | bytes 262176 | tf_op jit(solution)/shard_map/all_to_all | solution.py:493
  21.9 3.1 %shard_map.78 = (f32[5,16,256]{2,1,0:T(8,128)S(1)}, f32[15,3,16,256]{3,2,1,0:T(8,128)S(1)}) custom-call(f32[8,2,32,128]{3,2,1,0:T(8,128)S(1)} %all-to-all-done.got, f32[16,16,256]{2,1,0:T(8,128)S(1)} %copy-done.1, f32[1,16,256]{2,1,0:T(8,128)S(1)} %collective-permute-done.below, f32[16,1,256]{2,1,0:T(1,128)S(1)} %collective-permute-done.1.x_low, ...), custom_call_target="tpu_custom_call" | custom-call | tf_op jit(solution)/shard_map/pallas_call | solution.py:501
  25.0 2.8 %collective-permute-start.3 = (f32[5,16,256]{2,1,0:T(8,128)S(1)}, f32[5,16,256]{2,1,0:T(8,128)S(1)}, u32[]{:S(2)}, u32[]{:S(2)}) collective-permute-start(f32[5,16,256]{2,1,0:T(8,128)S(1)} %get-tuple-element.11.mine.refs_0_), channel_id=1, source_target_pairs={{0,4},{4,0},{8,12},{12,8},{16,20},{20,16},{24,28},{28,24},{1,5},{5... | collective-permute-start | bytes 245768 | tf_op jit(solution)/shard_map/ppermute | solution.py:513
  27.8 2.4 %collective-permute-done.3.other.refs_1_ = f32[5,16,256]{2,1,0:T(8,128)S(1)} collective-permute-done((f32[5,16,256]{2,1,0:T(8,128)S(1)}, f32[5,16,256]{2,1,0:T(8,128)S(1)}, u32[]{:S(2)}, u32[]{:S(2)}) %collective-permute-start.3) | collective-permute-done | bytes 81952 | tf_op jit(solution)/shard_map/ppermute | solution.py:513
  30.3 0.4 collective-permute-start.4
  30.6 4.1 %collective-permute-done.4.other.refs_2_ = f32[5,16,256]{2,1,0:T(8,128)S(1)} collective-permute-done((f32[5,16,256]{2,1,0:T(8,128)S(1)}, f32[5,16,256]{2,1,0:T(8,128)S(1)}, u32[]{:S(2)}, u32[]{:S(2)}) %collective-permute-start.4) | collective-permute-done | bytes 81952 | tf_op jit(solution)/shard_map/ppermute | solution.py:513
  34.8 1.4 %collective-permute-start.5 = (f32[2,16,256]{2,1,0:T(8,128)S(1)}, f32[2,16,256]{2,1,0:T(8,128)S(1)}, u32[]{:S(2)}, u32[]{:S(2)}) collective-permute-start(f32[2,16,256]{2,1,0:T(8,128)S(1)} %shard_map.80), channel_id=1, source_target_pairs={{0,16},{4,20},{8,24},{12,28},{16,0},{20,4},{24,8},{28,12},{1,17},{... | collective-permute-start | bytes 98312 | tf_op jit(solution)/shard_map/ppermute | solution.py:513
  36.3 3.5 %collective-permute-done.5.refs_3_ = f32[2,16,256]{2,1,0:T(8,128)S(1)} collective-permute-done((f32[2,16,256]{2,1,0:T(8,128)S(1)}, f32[2,16,256]{2,1,0:T(8,128)S(1)}, u32[]{:S(2)}, u32[]{:S(2)}) %collective-permute-start.5) | collective-permute-done | bytes 32800 | tf_op jit(solution)/shard_map/ppermute | solution.py:513
  39.8 3.8 %shard_map.81 = (f32[16,16,256]{2,1,0:T(8,128)}, f32[8,32,128]{2,1,0:T(8,128)S(1)}) custom-call(f32[8,2,32,128]{3,2,1,0:T(8,128)S(1)} %all-to-all-done.got, f32[15,3,16,256]{3,2,1,0:T(8,128)S(1)} %get-tuple-element.10.factors, f32[5,16,256]{2,1,0:T(8,128)S(1)} %get-tuple-element.11.mine.refs_0_, f32[5,16,256]{2,1,0:T(8,128)S(1)} %collective-permute-done.3.other.refs_1_, ...), custom_call_target="tpu_custom_call" | custom-call | tf_op jit(solution)/shard_map/pallas_call | solution.py:521
  43.6 0.0 copy-start
  43.6 0.0 copy-start.4
  43.6 12.0 %all_to_all.10 = f32[8,32,128]{2,1,0:T(8,128)S(1)} all-to-all(f32[8,32,128]{2,1,0:T(8,128)S(1)} %get-tuple-element.13), channel_id=1, replica_groups=mesh['gz'=8,'gx'=4] {'gz'}, dimensions={0} | all-to-all | bytes 262144 | tf_op jit(solution)/shard_map/all_to_all | solution.py:530
  55.6 0.0 copy-done.3
  55.6 1.3 %shard_map.82 = f32[3,128,128]{2,1,0:T(8,128)} custom-call(f32[256,128]{1,0:T(8,128)S(1)} %bitcast.2, s32[128,128]{1,0:T(8,128)S(1)} %copy-done.4, s32[4,128,128]{2,1,0:T(8,128)S(1)} %copy-done.2, f32[3,128,128]{2,1,0:T(8,128)S(1)} %copy-done, f32[3,128,128]{2,1,0:T(8,128)S(1)} %copy-done.3), custom_call_target="tpu_custom_call" | custom-call | tf_op jit(solution)/shard_map/pallas_call | solution.py:531
  (9 shorter events, 0.1 us)
Async XLA Ops:
  5.5 7.4 %copy-start.1 = (f32[16,16,256]{2,1,0:T(8,128)S(1)}, f32[16,16,256]{2,1,0:T(8,128)}, u32[]{:S(2)}) copy-start(f32[16,16,256]{2,1,0:T(8,128)} %temp.1) | copy-start | bytes 786436
  5.6 16.3 %all-to-all-start = ((f32[8,2,32,128]{3,2,1,0:T(8,128)}), f32[8,2,32,128]{3,2,1,0:T(8,128)S(1)}, u32[]{:S(2)}, u32[]{:S(2)}) async-start(f32[8,2,32,128]{3,2,1,0:T(8,128)} %get-tuple-element.9), calls=%async_computation | async-start | bytes 524288 | tf_op jit(solution)/shard_map/all_to_all | solution.py:493
  13.0 5.4 %collective-permute-start = (f32[1,16,256]{2,1,0:T(8,128)S(1)}, f32[1,16,256]{2,1,0:T(8,128)S(1)}, u32[]{:S(2)}, u32[]{:S(2)}) collective-permute-start(f32[1,16,256]{2,1,0:T(8,128)S(1)} %slice.9), channel_id=1, source_target_pairs={{0,4},{4,8},{8,12},{12,16},{16,20},{20,24},{24,28},{1,5},{5,9},{9,... | collective-permute-start | bytes 49160 | tf_op jit(solution)/shard_map/ppermute | solution.py:494
  16.9 1.6 %collective-permute-start.2 = (f32[16,1,256]{2,1,0:T(1,128)S(1)}, f32[16,1,256]{2,1,0:T(1,128)S(1)}, u32[]{:S(2)}, u32[]{:S(2)}) collective-permute-start(f32[16,1,256]{2,1,0:T(1,128)S(1)} %get-tuple-element.16), channel_id=1, source_target_pairs={{1,0},{2,1},{3,2},{0,3},{5,4},{6,5},{7,6},{4,7},{9,8},{10,9},{11,1... | collective-permute-start | bytes 49160 | tf_op jit(solution)/shard_map/ppermute | solution.py:498
  17.1 3.3 %collective-permute-start.1 = (f32[16,1,256]{2,1,0:T(1,128)S(1)}, f32[16,1,256]{2,1,0:T(1,128)S(1)}, u32[]{:S(2)}, u32[]{:S(2)}) collective-permute-start(f32[16,1,256]{2,1,0:T(1,128)S(1)} %get-tuple-element.17), channel_id=1, source_target_pairs={{0,1},{1,2},{2,3},{3,0},{4,5},{5,6},{6,7},{7,4},{8,9},{9,10},{10,1... | collective-permute-start | bytes 49160 | tf_op jit(solution)/shard_map/ppermute | solution.py:495
  25.0 5.3 %collective-permute-start.3 = (f32[5,16,256]{2,1,0:T(8,128)S(1)}, f32[5,16,256]{2,1,0:T(8,128)S(1)}, u32[]{:S(2)}, u32[]{:S(2)}) collective-permute-start(f32[5,16,256]{2,1,0:T(8,128)S(1)} %get-tuple-element.11.mine.refs_0_), channel_id=1, source_target_pairs={{0,4},{4,0},{8,12},{12,8},{16,20},{20,16},{24,28},{28,24},{1,5},{5... | collective-permute-start | bytes 245768 | tf_op jit(solution)/shard_map/ppermute | solution.py:513
  30.3 4.5 %collective-permute-start.4 = (f32[5,16,256]{2,1,0:T(8,128)S(1)}, f32[5,16,256]{2,1,0:T(8,128)S(1)}, u32[]{:S(2)}, u32[]{:S(2)}) collective-permute-start(f32[5,16,256]{2,1,0:T(8,128)S(1)} %shard_map.79.mine), channel_id=1, source_target_pairs={{0,8},{4,12},{8,0},{12,4},{16,24},{20,28},{24,16},{28,20},{1,9},{5... | collective-permute-start | bytes 245768 | tf_op jit(solution)/shard_map/ppermute | solution.py:513
  34.8 5.0 %collective-permute-start.5 = (f32[2,16,256]{2,1,0:T(8,128)S(1)}, f32[2,16,256]{2,1,0:T(8,128)S(1)}, u32[]{:S(2)}, u32[]{:S(2)}) collective-permute-start(f32[2,16,256]{2,1,0:T(8,128)S(1)} %shard_map.80), channel_id=1, source_target_pairs={{0,16},{4,20},{8,24},{12,28},{16,0},{20,4},{24,8},{28,12},{1,17},{... | collective-permute-start | bytes 98312 | tf_op jit(solution)/shard_map/ppermute | solution.py:513
  39.8 15.8 %copy-start.2 = (s32[4,128,128]{2,1,0:T(8,128)S(1)}, s32[4,128,128]{2,1,0:T(8,128)}, u32[]{:S(2)}) copy-start(s32[4,128,128]{2,1,0:T(8,128)} %get-tuple-element.15.starts) | copy-start | bytes 786436
  39.8 15.8 %copy-start.3 = (f32[3,128,128]{2,1,0:T(8,128)S(1)}, f32[3,128,128]{2,1,0:T(8,128)}, u32[]{:S(2)}) copy-start(f32[3,128,128]{2,1,0:T(8,128)} %noise.1) | copy-start | bytes 589828
  43.6 12.1 %copy-start = (f32[3,128,128]{2,1,0:T(8,128)S(1)}, f32[3,128,128]{2,1,0:T(8,128)}, u32[]{:S(2)}) copy-start(f32[3,128,128]{2,1,0:T(8,128)} %velocity.1) | copy-start | bytes 589828
  43.6 12.1 %copy-start.4 = (s32[128,128]{1,0:T(8,128)S(1)}, s32[128,128]{1,0:T(8,128)}, u32[]{:S(2)}) copy-start(s32[128,128]{1,0:T(8,128)} %get-tuple-element.14.meta) | copy-start | bytes 196612

commit v3 on v2

v3 whole, which is shorter than its diff:
```python
import functools

import jax
import jax.numpy as jnp
from jax import lax
from jax.experimental import pallas as pl
from jax.experimental.pallas import tpu as pltpu
from jax.sharding import PartitionSpec as P

STIFFNESS = 10000.0
LATERAL = 0.1
COUPLE = 0.5
TWO_THIRDS = 2.0 / 3.0
KICK_RATE = 0.2
F32 = jnp.float32
BF16 = jnp.bfloat16
F8 = jnp.float8_e4m3fn
SCALE = 8.0
STEP = 16.0
PIECES = 3
PARTS = 4
ROUTE_LIMIT = 32 * 1024 * 1024
VMEM_LIMIT = 32 * 1024 * 1024
LOOK_COST = pl.CostEstimate(flops=2 * 10**9, bytes_accessed=10**7, transcendentals=0)


def quotient(value, size):
    if size & (size - 1) == 0:
        return lax.shift_right_logical(value, size.bit_length() - 1)
    return value // size


def iota(shape, dim):
    return lax.broadcasted_iota(jnp.int32, shape, dim)


def split(value, pieces):
    parts = []
    for _ in range(pieces):
        part = value.astype(BF16)
        parts.append(part)
        value = value - part.astype(F32)
    return parts


def split_small(value):
    value = value * SCALE
    parts = []
    for _ in range(PIECES):
        part = value.astype(F8)
        parts.append(part)
        value = (value - part.astype(F32)) * STEP
    return parts


def join_small(parts):
    total = parts[-1]
    for part in parts[-2::-1]:
        total = part + total * (1.0 / STEP)
    return total * (1.0 / SCALE)


def merge(left, right):
    g_a, sl_a, rl_a, s_a, r_a = left
    g_b, sl_b, rl_b, s_b, r_b = right
    excess = s_a + sl_b
    source = r_a + rl_b
    inverse = 1.0 / (g_a + g_b + excess)
    to_left = g_a * inverse
    to_right = g_b * inverse
    return (
        g_a * to_right,
        sl_a + to_left * excess,
        rl_a + to_left * source,
        s_b + to_right * excess,
        r_b + to_right * source,
    )


def prefix_step(state, segment):
    gate, sl, rl, s, r = segment
    excess = state[0] + sl
    source = state[1] + rl
    ratio = gate / (gate + excess)
    return (s + ratio * excess, r + ratio * source)


def suffix_step(state, segment):
    gate, sl, rl, s, r = segment
    excess = s + state[0]
    source = r + state[1]
    ratio = gate / (gate + excess)
    return (sl + ratio * excess, rl + ratio * source)


def route_kernel(
    dims, slabs, rows, parts, count_hbm, velocity_hbm, plane_hbm, column_hbm, send, meta, starts,
    velocity, plane, column, count, arrived,
):
    copies = [
        pltpu.make_async_copy(source, target, arrived.at[i])
        for i, (source, target) in enumerate(
            (
                (count_hbm, count),
                (plane_hbm, plane),
                (column_hbm, column),
                (velocity_hbm, velocity),
            )
        )
    ]
    for copy in copies:
        copy.start()
    planes, width_x, width_y = dims
    bricks, lanes = plane.shape
    part_rows = planes * width_x // parts
    lane = iota((bricks, lanes), 1)
    sub_b = iota((bricks, bricks), 0)
    lane_b = iota((bricks, bricks), 1)
    eye = sub_b == lane_b
    sub_l = iota((lanes, lanes), 0)
    lane_l = iota((lanes, lanes), 1)
    prefix = jnp.concatenate(
        [jnp.where(sub_l <= lane_l, 1.0, 0.0), jnp.ones((lanes, lanes), F32)], axis=1
    ).astype(BF16)
    copies[0].wait()
    count_row = jnp.broadcast_to(count[...].astype(F32), (bricks, bricks))
    count_col = jnp.sum(jnp.where(eye, count_row, 0.0), axis=1, keepdims=True).astype(jnp.int32)
    in_use = lane < count_col
    copies[1].wait()
    owner = quotient(plane[:, 0:1], planes)
    owner_f = jnp.broadcast_to(owner.astype(F32), (bricks, bricks))
    owner_row = jnp.sum(jnp.where(eye, owner_f, 0.0), axis=0, keepdims=True)
    same = owner_f == owner_row
    ahead = same & (lane_b < sub_b)
    peers = jnp.where(jnp.concatenate([same, ahead], axis=1), 1.0, 0.0).astype(BF16)
    copies[2].wait()
    col = column[...]
    x_cell = quotient(col, width_y)
    y_cell = col - x_cell * width_y
    row = x_cell * planes + plane[...] - owner * planes
    code = jnp.where(in_use, (row + 1) * width_y + y_cell, 0)
    part = jnp.where(in_use, quotient(row, part_rows), parts)
    inside = [jnp.where(part == c, 1.0, 0.0).astype(BF16) for c in range(parts)]
    sums = jnp.dot(jnp.concatenate(inside, axis=0), prefix, preferred_element_type=F32)
    ranks = [sums[c * bricks : (c + 1) * bricks, :lanes] for c in range(parts)]
    sizes = [sums[c * bricks : (c + 1) * bricks, lanes:] for c in range(parts)]
    earlier = [jnp.zeros_like(sizes[0])]
    for c in range(parts - 1):
        earlier.append(earlier[-1] + sizes[c])
    offsets = jnp.dot(
        peers,
        jnp.concatenate(
            [jnp.concatenate(earlier, axis=1), jnp.concatenate(sizes, axis=1)], axis=0
        ).astype(BF16),
        preferred_element_type=F32,
    )
    copies[3].wait()
    vx, vy, vz = velocity[0], velocity[1], velocity[2]
    kinetic = 0.5 * (vx * vx + vy * vy + vz * vz)
    begins = [
        offsets[:, c * lanes : (c + 1) * lanes].astype(jnp.int32) + owner * (rows * lanes)
        for c in range(parts)
    ]
    shifts = [begin & (lanes - 1) for begin in begins]
    packed = ranks[0].astype(jnp.int32)
    run = jnp.zeros((bricks, lanes), jnp.int32)
    base = jnp.zeros((bricks, lanes), F32)
    lane_f = lane.astype(F32)
    for c in range(1, parts):
        packed = packed | (ranks[c].astype(jnp.int32) << (8 * c))
        run = jnp.where(lane_f >= earlier[c], 8 * c, run)
        base = jnp.where(lane_f >= earlier[c], earlier[c], base)
    wanted = lane - base.astype(jnp.int32)
    found = jnp.zeros((bricks, lanes), jnp.int32)
    step = lanes // 2
    while step:
        at = jnp.take_along_axis(packed, found + (step - 1), axis=1)
        at = lax.shift_right_logical(at, run) & 255
        found = jnp.where(at <= wanted, found + step, found)
        step //= 2
    kinetic = jnp.take_along_axis(kinetic, found, axis=1)
    code = jnp.take_along_axis(code, found, axis=1)
    zero = jnp.zeros((bricks, lanes), BF16)
    slot = iota((slabs * rows, bricks), 0).astype(F32).astype(BF16)
    values = []
    spots = []
    place = jnp.full((bricks, lanes), -1, jnp.int32)
    table = jnp.zeros((bricks, lanes), jnp.int32)
    for c in range(parts):
        table = jnp.where(lane == c, begins[c], table)
        place = jnp.where(
            part == c, (begins[c] + ranks[c].astype(jnp.int32) - 1) * parts + c, place
        )
        turn = (lane - shifts[c]) & (lanes - 1)
        valid = turn.astype(F32) < sizes[c]
        turn = (turn + earlier[c].astype(jnp.int32)) & (lanes - 1)
        kin = jnp.where(valid, jnp.take_along_axis(kinetic, turn, axis=1), 0.0)
        cell = jnp.where(valid, jnp.take_along_axis(code, turn, axis=1), 0)
        cell_row = quotient(cell, width_y)
        cell_y = cell - cell_row * width_y
        pieces = split(kin, 2) + [cell_row.astype(F32).astype(BF16), cell_y.astype(F32).astype(BF16)]
        first = lane >= shifts[c]
        values.append(jnp.concatenate([jnp.where(first, p, zero) for p in pieces], axis=1))
        values.append(jnp.concatenate([jnp.where(first, zero, p) for p in pieces], axis=1))
        begin_row = jnp.sum(
            jnp.where(eye, begins[c].astype(F32), 0.0), axis=0, keepdims=True
        ).astype(jnp.int32)
        target = quotient(begin_row, lanes).astype(F32)
        spots.append(slot == target.astype(BF16))
        spots.append(slot == (target + 1.0).astype(BF16))
    starts[...] = table
    meta[...] = place
    one = jnp.ones((), BF16)
    moved = jnp.dot(
        jnp.concatenate([jnp.where(spot, one, jnp.zeros((), BF16)) for spot in spots], axis=1),
        jnp.concatenate(values, axis=0),
        preferred_element_type=F32,
    )
    send[:, 0] = (moved[:, :lanes] + moved[:, lanes : 2 * lanes]).reshape(slabs, rows, lanes)
    send[:, 1] = (moved[:, 2 * lanes : 3 * lanes] * width_y + moved[:, 3 * lanes :]).reshape(
        slabs, rows, lanes
    )


def decode(code, width_y):
    row = jnp.floor((code + 0.5) * (1.0 / width_y))
    return row, code - row * width_y


def find_runs(dims, parts, got, runs_vmem):
    planes, width_x, width_y = dims
    slabs, _, rows, lanes = got.shape
    part_rows = planes * width_x // parts
    codes = got[:, 1]
    codes = jnp.where(codes > 0.0, codes, float((parts * part_rows + 1) * width_y + 1))
    longest = jnp.zeros((slabs, lanes), F32)
    first = jnp.zeros((slabs, lanes), F32)
    table = jnp.zeros((slabs, lanes), F32)
    lane = iota((slabs, lanes), 1)
    for c in range(parts):
        limit = float(((c + 1) * part_rows + 1) * width_y)
        last = jnp.sum(jnp.where(codes < limit, 1.0, 0.0), axis=1)
        longest = jnp.maximum(longest, last - first)
        table = jnp.where(lane == 2 * c, pltpu.roll(first, 2 * c, 1) if c else first, table)
        table = jnp.where(lane == 2 * c + 1, pltpu.roll(last, 2 * c + 1, 1), table)
        first = pltpu.roll(last, 1, 1)
    longest = jnp.max(jnp.where(lane == 0, longest, 0.0), keepdims=True)
    runs_vmem[...] = jnp.where(lane == 2 * parts, longest, table).astype(jnp.int32)


def run_row(got, field, s, spot, last):
    rows = got.shape[2]
    loaded = got[s, field, pl.ds(jnp.minimum(spot, rows - 1), 1), :]
    return jnp.where(spot < last, loaded, 0.0)


def bin_kernel(dims, parts, levels, got, totals, codes, runs_vmem, lhs, rhs, runs, arrived):
    planes, width_x, width_y = dims
    slabs, _, rows, lanes = got.shape
    part_rows = planes * width_x // parts
    find_runs(dims, parts, got, runs_vmem)
    copy = pltpu.make_async_copy(runs_vmem, runs, arrived.at[0])
    copy.start()
    one = jnp.ones((), F8)
    zero = jnp.zeros((), F8)
    y_id = iota((width_y, lanes), 0).astype(F32).astype(BF16)
    totals[...] = jnp.zeros(totals.shape, F32)
    copy.wait()
    longest = runs[0, 2 * parts]

    def add_rows(turn, carry):
        for c in range(parts):
            row_id = (iota((part_rows, lanes), 0) + (c * part_rows + 1)).astype(F32).astype(BF16)
            for s in range(slabs):
                spot = runs[s, 2 * c] + turn
                last = runs[s, 2 * c + 1]
                pieces = split_small(run_row(got, 0, s, spot, last))
                code = run_row(got, 1, s, spot, last)
                codes[turn * parts + c, pl.ds(s, 1), :] = code
                row, y_cell = decode(code, width_y)
                here = pl.ds(s * lanes, lanes)
                hit = row_id == row.astype(BF16)
                for i, piece in enumerate(pieces):
                    lhs[c, pl.ds(i * part_rows, part_rows), here] = jnp.where(hit, piece, zero)
                lhs[c, pl.ds(PIECES * part_rows, part_rows), here] = jnp.where(hit, one, zero)
                rhs[c, :, here] = jnp.where(y_id == y_cell.astype(BF16), one, zero)
        for c in range(parts):
            added = lax.dot_general(
                lhs[c], rhs[c], (((1,), (1,)), ((), ())), preferred_element_type=F32
            )
            for i in range(PIECES + 1):
                for h in range(width_y // lanes):
                    totals[i, h, pl.ds(c * part_rows, part_rows), :] += added[
                        i * part_rows : (i + 1) * part_rows, h * lanes : (h + 1) * lanes
                    ]
        return carry

    lax.fori_loop(0, longest, add_rows, 0)
    for i in range((levels - 1) * parts):
        codes[longest * parts + i] = jnp.zeros((slabs, lanes), F32)


def solve_kernel(dims, totals, temp, below, x_low, x_high, summary, factors):
    planes, width_x, width_y = dims
    lanes = totals.shape[3]

    def plane_terms(z):
        here = temp[z]
        x_minus = jnp.concatenate([x_low[z], here[:-1]], axis=0)
        x_plus = jnp.concatenate([here[1:], x_high[z]], axis=0)
        lateral = LATERAL * (
            x_minus
            + x_plus
            + pltpu.roll(here, 1, 1)
            + pltpu.roll(here, width_y - 1, 1)
            - 4.0 * here
        )
        at = pl.ds(z, width_x, stride=planes)
        sums = [
            jnp.concatenate([totals[i, h, at, :] for h in range(width_y // lanes)], axis=1)
            for i in range(PIECES + 1)
        ]
        energy = join_small(sums[:PIECES])
        count = sums[PIECES]
        return here + COUPLE * count, here * here + lateral + COUPLE * TWO_THIRDS * energy

    start = temp[0]
    gate = jnp.where(
        lax.axis_index("gz") > 0, STIFFNESS * (0.5 * (start + below[0])), jnp.zeros_like(start)
    )
    excess, source = plane_terms(0)
    left_excess = jnp.zeros_like(start)
    left_source = jnp.zeros_like(start)
    for z in range(planes - 1):
        face = STIFFNESS * (0.5 * (temp[z + 1] + temp[z]))
        inverse = 1.0 / (gate + face + excess)
        to_left = gate * inverse
        to_right = face * inverse
        factors[z, 0] = to_left
        factors[z, 1] = to_right
        factors[z, 2] = source * inverse
        next_excess, next_source = plane_terms(z + 1)
        left_excess = left_excess + to_left * excess
        left_source = left_source + to_left * source
        gate = gate * to_right
        excess = next_excess + to_right * excess
        source = next_source + to_right * source
    for i, value in enumerate((gate, left_excess, left_source, excess, source)):
        summary[i] = value


def load_five(ref):
    return tuple(ref[i] for i in range(5))


def merge_kernel(level, last, mine, other, _, total):
    upper = (lax.axis_index("gz") & (1 << level)) != 0
    own = load_five(mine)
    came = load_five(other)
    low = tuple(jnp.where(upper, b, a) for a, b in zip(own, came))
    high = tuple(jnp.where(upper, a, b) for a, b in zip(own, came))
    joined = merge(low, high)
    if not last:
        for i in range(5):
            total[i] = joined[i]
        return
    in_upper = (lax.axis_index("gz") & (1 << (level + 1))) != 0
    end = jnp.zeros_like(joined[0])
    closed = suffix_step((end, end), joined)
    total[0] = jnp.where(in_upper, closed[0], joined[3])
    total[1] = jnp.where(in_upper, closed[1], joined[4])


def table_kernel(dims, parts, factors, table, spread):
    planes, width_x, width_y = dims
    part_rows = planes * width_x // parts
    lanes = spread.shape[3]
    zeros = jnp.zeros((width_x, width_y), F32)
    state = (zeros, zeros, zeros + 1.0)
    for z in range(planes - 1, -1, -1):
        if z < planes - 1:
            to_left, to_right, fixed = factors[z, 0], factors[z, 1], factors[z, 2]
            state = (
                fixed + to_right * state[0],
                to_left + to_right * state[1],
                to_right * state[2],
            )
        for t in range(3):
            for h in range(spread.shape[1]):
                spread[t, h, pl.ds(z, width_x, stride=planes), :] = state[t][
                    :, h * lanes : (h + 1) * lanes
                ]
    for c in range(parts):
        for t in range(3):
            for h in range(spread.shape[1]):
                block = spread[t, h, pl.ds(c * part_rows, part_rows), :]
                for i, piece in enumerate(split_small(block)):
                    at = pl.ds((t * PIECES + i) * part_rows, part_rows)
                    table[c, at, pl.ds(h * lanes, lanes)] = piece


def look_kernel(dims, parts, levels, phase, codes, runs, *refs):
    if phase == 0:
        factors, found, keys, spots, table, spread, rhs = refs
        table_kernel(dims, parts, factors, table, spread)
    else:
        table, _, found, keys, spots, rhs = refs
    planes, width_x, width_y = dims
    _, slabs, lanes = codes.shape
    part_rows = planes * width_x // parts
    halves = width_y // lanes
    one = jnp.ones((), F8)
    zero = jnp.zeros((), F8)
    y_id = iota((width_y, lanes), 0).astype(F32).astype(BF16)
    last_lane = iota((1, lanes), 1) == 2 * parts
    turns = jnp.max(jnp.where(last_lane, runs[0:1, :].astype(F32), 0.0)).astype(jnp.int32)

    def find_rows(step, carry):
        wanted = []
        for c in range(parts):
            block = step * parts + c
            row, y_cell = decode(codes[(step * levels + phase) * parts + c], width_y)
            wanted.append(row)
            hot = y_cell.astype(BF16)
            for s in range(slabs):
                rhs[c, :, pl.ds(s * lanes, lanes)] = jnp.where(
                    y_id == hot[s : s + 1], one, zero
                )
            x_cell = jnp.floor((row - (c * part_rows + 0.5)) * (1.0 / planes))
            half = jnp.floor((y_cell + 0.5) * (1.0 / lanes))
            keys[block] = jnp.where(row > c * part_rows, x_cell * halves + half, -1.0)
            spots[block] = (y_cell - half * lanes).astype(jnp.int32)
        for c in range(parts):
            block = step * parts + c
            row_id = (iota((part_rows, lanes), 0) + (c * part_rows + 1)).astype(F32)
            picked = jnp.dot(table[c], rhs[c], preferred_element_type=F32)
            for s in range(slabs):
                hit = row_id == wanted[c][s : s + 1]
                for t in range(3):
                    pieces = [
                        picked[
                            (t * PIECES + i) * part_rows : (t * PIECES + i + 1) * part_rows,
                            s * lanes : (s + 1) * lanes,
                        ]
                        for i in range(PIECES)
                    ]
                    total = pieces[-1]
                    for piece in pieces[-2::-1]:
                        total = piece + total * (1.0 / STEP)
                    chosen = jnp.sum(jnp.where(hit, total, 0.0), axis=0, keepdims=True)
                    found[t, block, pl.ds(s, 1), :] = chosen * (1.0 / SCALE)
        return carry

    lax.fori_loop(0, quotient_up(turns, levels), find_rows, 0)


def quotient_up(value, size):
    return (value + (size - 1)) // size


def join_kernel(dims, parts, levels, runs_vmem, *refs):
    planes, width_x, width_y = dims
    own = load_five(refs[0])
    others = refs[1:levels]
    far = refs[levels]
    found = refs[levels + 1 : 2 * levels + 1]
    keys = refs[2 * levels + 1 : 3 * levels + 1]
    lane_of = refs[3 * levels + 1 : 4 * levels + 1]
    edges, reply, temps, runs, arrived = refs[4 * levels + 1 :]
    slabs, rows, lanes = reply.shape
    part_x = width_x // parts
    halves = width_y // lanes
    copy = pltpu.make_async_copy(runs_vmem, runs, arrived.at[0])
    copy.start()
    reply[...] = jnp.zeros(reply.shape, F32)
    index = lax.axis_index("gz")
    zeros = jnp.zeros_like(own[0])
    top = (index & (1 << (levels - 1))) != 0
    before = (jnp.where(top, far[0], zeros + 1.0), jnp.where(top, far[1], zeros))
    after = (jnp.where(top, zeros, far[0]), jnp.where(top, zeros, far[1]))
    for level in range(levels - 2, -1, -1):
        upper = (index & (1 << level)) != 0
        segment = load_five(others[level])
        with_before = prefix_step(before, segment)
        with_after = suffix_step(after, segment)
        before = tuple(jnp.where(upper, a, b) for a, b in zip(with_before, before))
        after = tuple(jnp.where(upper, b, a) for a, b in zip(with_after, after))
    through = prefix_step(before, own)
    value = (through[1] + after[1]) / (through[0] + after[0])
    edges[0] = (before[1] + own[2] + own[0] * value) / (before[0] + own[1] + own[0])
    edges[1] = value
    copy.wait()

    def fill_rows(step, carry):
        for phase in range(levels):
            for c in range(parts):
                block = step * parts + c
                key = keys[phase][block]
                lane = lane_of[phase][block]
                ends = [jnp.zeros((slabs, lanes), F32), jnp.zeros((slabs, lanes), F32)]
                for x in range(part_x):
                    for h in range(halves):
                        hit = key == float(x * halves + h)
                        for e in range(2):
                            line = edges[e, pl.ds(c * part_x + x, 1), pl.ds(h * lanes, lanes)]
                            line = jnp.broadcast_to(line, (slabs, lanes))
                            ends[e] = jnp.where(
                                hit, jnp.take_along_axis(line, lane, axis=1), ends[e]
                            )
                temps[phase * parts + c] = (
                    found[phase][0, block]
                    + found[phase][1, block] * ends[0]
                    + found[phase][2, block] * ends[1]
                )
        for phase in range(levels):
            for c in range(parts):
                for s in range(slabs):
                    spot = runs[s, 2 * c] + (step * levels + phase)
                    here = pl.ds(jnp.minimum(spot, rows - 1), 1)
                    reply[s, here, :] += temps[phase * parts + c, pl.ds(s, 1), :]
        return carry

    lax.fori_loop(0, quotient_up(runs[0, 2 * parts], levels), fill_rows, 0)


def fill_kernel(factors, edges, new_temp):
    planes = new_temp.shape[0]
    edge = edges[0]
    value = edges[1]
    new_temp[planes - 1] = value
    for z in range(planes - 2, -1, -1):
        value = factors[z, 2] + factors[z, 0] * edge + factors[z, 1] * value
        new_temp[z] = value


def kick_kernel(parts, returned, meta, starts, velocity, noise, out):
    bricks, lanes = meta.shape
    slots = returned.shape[0]
    packed = meta[...]
    lane = iota((bricks, lanes), 1)
    in_use = packed >= 0
    place = quotient(jnp.maximum(packed, 0), parts)
    part = jnp.maximum(packed, 0) - place * parts
    slot = iota((bricks, slots), 1)
    spots = []
    shifts = []
    for c in range(parts):
        begin = jnp.broadcast_to(starts[:, c : c + 1], (bricks, lanes))
        target = quotient(begin[:, 0:1], lanes)
        shifts.append(begin & (lanes - 1))
        spots.append(slot == target)
        spots.append(slot == target + 1)
    values = jnp.concatenate(split(returned[...], 2), axis=1)
    moved = jnp.dot(
        jnp.where(jnp.concatenate(spots, axis=0), 1.0, 0.0).astype(BF16),
        values,
        preferred_element_type=F32,
    )
    moved = moved[:, :lanes] + moved[:, lanes:]
    at = place & (lanes - 1)
    temp = jnp.zeros((bricks, lanes), F32)
    for c in range(parts):
        here = moved[2 * c * bricks : (2 * c + 1) * bricks]
        after = moved[(2 * c + 1) * bricks : (2 * c + 2) * bricks]
        whole = jnp.where(lane >= shifts[c], here, after)
        temp = jnp.where(part == c, jnp.take_along_axis(whole, at, axis=1), temp)
    root = jnp.sqrt(2.0 * KICK_RATE * temp)
    for i in range(3):
        out[i] = jnp.where(in_use, (1.0 - KICK_RATE) * velocity[i] + root * noise[i], 0.0)


def call(kernel, out_shape, scratch=(), spaces=None, limit=VMEM_LIMIT, cost=None):
    extra = {} if cost is None else {"cost_estimate": cost}
    if spaces is not None:
        extra["in_specs"] = [pl.BlockSpec(memory_space=m) for m in spaces]
    return pl.pallas_call(
        kernel,
        out_shape=out_shape,
        **extra,
        scratch_shapes=list(scratch),
        compiler_params=pltpu.CompilerParams(vmem_limit_bytes=limit),
    )


def struct(*shape, dtype=F32):
    return jax.ShapeDtypeStruct(shape, dtype)


def route_call(dims, slabs, rows, parts, velocity_shape, plane_shape):
    bricks, lanes = plane_shape
    return call(
        functools.partial(route_kernel, dims, slabs, rows, parts),
        (
            struct(slabs, 2, rows, lanes),
            struct(bricks, lanes, dtype=jnp.int32),
            struct(bricks, lanes, dtype=jnp.int32),
        ),
        (
            pltpu.VMEM(velocity_shape, F32),
            pltpu.VMEM(plane_shape, jnp.int32),
            pltpu.VMEM(plane_shape, jnp.int32),
            pltpu.VMEM((1, bricks), jnp.int32),
            pltpu.SemaphoreType.DMA((4,)),
        ),
        (pltpu.HBM,) * 4,
        ROUTE_LIMIT,
    )


def body(atom_velocity, atom_noise, atom_plane, atom_column, brick_count, electron_temp):
    dims = electron_temp.shape
    planes, width_x, width_y = dims
    cells = planes * width_x
    slabs = lax.axis_size("gz")
    groups = lax.axis_size("gx")
    levels = slabs.bit_length() - 1
    assert slabs == 1 << levels and levels > 0
    bricks, lanes = atom_plane.shape
    rows = 2 * bricks // slabs
    parts = PARTS
    assert width_x % parts == 0 and parts <= 4 and lanes <= 128
    run_shape = (slabs, lanes)
    run_scratch = (pltpu.SMEM(run_shape, jnp.int32), pltpu.SemaphoreType.DMA((1,)))

    send, meta, starts = route_call(
        dims, slabs, rows, parts, atom_velocity.shape, atom_plane.shape
    )(
        *(
            pltpu.with_memory_space_constraint(x, pltpu.HBM)
            for x in (brick_count.reshape(1, bricks), atom_velocity, atom_plane, atom_column)
        )
    )
    got = lax.all_to_all(send, "gz", split_axis=0, concat_axis=0, tiled=True)
    below = lax.ppermute(electron_temp[-1:], "gz", [(i, i + 1) for i in range(slabs - 1)])
    x_low = lax.ppermute(
        electron_temp[:, -1:], "gx", [(i, (i + 1) % groups) for i in range(groups)]
    )
    x_high = lax.ppermute(
        electron_temp[:, :1], "gx", [((i + 1) % groups, i) for i in range(groups)]
    )
    totals, codes, runs = call(
        functools.partial(bin_kernel, dims, parts, levels),
        (
            struct(PIECES + 1, width_y // lanes, cells, lanes),
            struct(parts * (rows + levels - 1), slabs, lanes),
            struct(*run_shape, dtype=jnp.int32),
        ),
        (
            pltpu.VMEM((parts, (PIECES + 1) * cells // parts, slabs * lanes), F8),
            pltpu.VMEM((parts, width_y, slabs * lanes), F8),
        )
        + run_scratch,
    )(got)
    total, factors = call(
        functools.partial(solve_kernel, dims),
        (struct(5, width_x, width_y), struct(planes - 1, 3, width_x, width_y)),
    )(totals, electron_temp, below, x_low, x_high)
    blocks = parts * quotient_up(rows, levels)
    found_shapes = (
        struct(3, blocks, slabs, lanes),
        struct(blocks, slabs, lanes),
        struct(blocks, slabs, lanes, dtype=jnp.int32),
    )
    table_shape = (parts, 3 * PIECES * cells // parts, width_y)
    pieces = [total]
    found = []
    for level in range(levels):
        other = lax.ppermute(total, "gz", [(i, i ^ (1 << level)) for i in range(slabs)])
        outs = call(
            functools.partial(look_kernel, dims, parts, levels, level),
            found_shapes + ((struct(*table_shape, dtype=F8),) if level == 0 else ()),
            (() if level else (pltpu.VMEM((3, width_y // lanes, cells, lanes), F32),))
            + (pltpu.VMEM((parts, width_y, slabs * lanes), F8),),
            cost=LOOK_COST,
        )(codes, runs, *((table, total) if level else (factors,)))
        if level == 0:
            table = outs[3]
        found.append(outs[:3])
        pieces.append(other)
        if level < levels - 1:
            last = level == levels - 2
            total = call(
                functools.partial(merge_kernel, level, last),
                struct(2 if last else 5, width_x, width_y),
            )(total, other, outs[1])
    edges, reply = call(
        functools.partial(join_kernel, dims, parts, levels),
        (struct(2, width_x, width_y), struct(slabs, rows, lanes)),
        (pltpu.VMEM((levels * parts, slabs, lanes), F32),) + run_scratch,
    )(runs, *pieces, *(phase[i] for i in range(3) for phase in found))
    new_temp = call(fill_kernel, struct(*dims))(factors, edges)
    returned = lax.all_to_all(reply, "gz", split_axis=0, concat_axis=0, tiled=True)
    new_velocity = call(functools.partial(kick_kernel, parts), struct(*atom_velocity.shape))(
        returned.reshape(slabs * rows, lanes), meta, starts, atom_velocity, atom_noise
    )
    return (new_temp, new_velocity)


def solution(mesh):
    placed = (
        P(None, ("gz", "gx"), None),
        P(None, ("gz", "gx"), None),
        P(("gz", "gx"), None),
        P(("gz", "gx"), None),
        P(("gz", "gx")),
        P("gz", "gx", None),
    )
    return jax.shard_map(
        body,
        mesh=mesh,
        in_specs=placed,
        out_specs=(P("gz", "gx", None), P(None, ("gz", "gx"), None)),
        check_vma=False,
    )
```

time: 57.2 us -> 53.6 us (0.937)
  blocking collectives: 12 us -> 0 us
  Pallas kernels: 13.1 us -> 18.8 us
  starting transfers between devices: 16.5 us -> 20.3 us
  waiting for transfers between devices: 14.5 us -> 13.4 us
    all_to_all x1 -> x0, blocking collectives: 12 us -> none  [body(): lax.all_to_all(reply, 'gz', split_axis=0, concat_axis=0, tiled=True)]
    ppermute x3, waiting for transfers between devices: 10.1 us -> 2.39 us  [body(): lax.ppermute(total, 'gz', [(i, i ^ 1 << level) for i in range(slabs)])]
    all_to_all x0 -> x1, waiting for transfers between devices: none -> 6.59 us  [body(): lax.all_to_all(reply, 'gz', split_axis=0, concat_axis=0, tiled=True)]
    pallas_call x3 -> x8, Pallas kernels: 11.8 us -> 17.5 us  [the longest x3 7.59 us: body(): call(functools.partial(look_kernel, dims, parts, levels, level), found_sh...]
    all_to_all x0 -> x1, starting transfers between devices: none -> 4.52 us  [body(): lax.all_to_all(reply, 'gz', split_axis=0, concat_axis=0, tiled=True)]
    all_to_all x1, waiting for transfers between devices: 1.47 us -> 4.38 us  [body(): got = lax.all_to_all(send, 'gz', split_axis=0, concat_axis=0, tiled=True)]
    ppermute x1, waiting for transfers between devices: 1.85 us -> 0.01 us  [body(): lax.ppermute(electron_temp[:, -1:], 'gx', [(i, (i + 1) % groups) for i in...]
    ppermute x1, waiting for transfers between devices: 0.83 us -> 0.01 us  [body(): lax.ppermute(electron_temp[-1:], 'gz', [(i, i + 1) for i in range(slabs -...]
  transfers between devices with their start and end apart: 7 -> 8, of which waited for: 7 -> 5; matrix products, arithmetic and copies ran while one was open for 0% -> 0% of each run, Pallas kernels for 0% -> 21%
where the time goes in v3:
time: 53.6 us; the launch traced here: 53.3 us
  starting transfers between devices  20.3 us (38%)
  Pallas kernels  18.8 us (35%)
  waiting for transfers between devices  13.4 us (25%)
  between operations  0.77 us (1%)
    pallas_call x3, Pallas kernels, body(): call(functools.partial(look_kernel, dims, parts, levels, level), found_sh...  7.59 us
    all_to_all x1, starting transfers between devices, body(): got = lax.all_to_all(send, 'gz', split_axis=0, concat_axis=0, tiled=True)  7.4 us
    all_to_all x1, waiting for transfers between devices, body(): lax.all_to_all(reply, 'gz', split_axis=0, concat_axis=0, tiled=True)  6.59 us
    all_to_all x1, starting transfers between devices, body(): lax.all_to_all(reply, 'gz', split_axis=0, concat_axis=0, tiled=True)  4.52 us
    all_to_all x1, waiting for transfers between devices, body(): got = lax.all_to_all(send, 'gz', split_axis=0, concat_axis=0, tiled=True)  4.38 us
    ppermute x1, starting transfers between devices, body(): lax.ppermute(electron_temp[-1:], 'gz', [(i, i + 1) for i in range(slabs -...  3.92 us
    ppermute x3, starting transfers between devices, body(): lax.ppermute(total, 'gz', [(i, i ^ 1 << level) for i in range(slabs)])  3.89 us
    pallas_call x1, Pallas kernels, body(): route_call(dims, slabs, rows, parts, atom_velocity.shape, atom_plane.shape)  3.45 us
  transfers between devices with their start and end apart: 8, of which 5 were waited for; matrix products, arithmetic and copies ran while one was open for 0% of the time, Pallas kernels for 21%

profile of v3, /device:TPU:0, one launch (start us, length us, event | category | flops | bytes accessed | tf_op | source)
XLA Modules:
  0.0 53.3 jit_solution(7879029121983258015)
XLA Ops:
  0.6 3.4 %shard_map.77 = (f32[8,2,32,128]{3,2,1,0:T(8,128)}, s32[128,128]{1,0:T(8,128)S(1)}, s32[128,128]{1,0:T(8,128)S(1)}) custom-call(s32[1,128]{1,0:T(1,128)} %bitcast.3, f32[3,128,128]{2,1,0:T(8,128)} %velocity.1, s32[128,128]{1,0:T(8,128)} %plane_hbm.1, s32[128,128]{1,0:T(8,128)} %column_hbm.1), custom_call_target="tpu_custom_call" | custom-call | tf_op jit(solution)/shard_map/pallas_call | solution.py:625
  4.1 0.0 copy-start.1
  4.1 7.4 %all-to-all-start = ((f32[8,2,32,128]{3,2,1,0:T(8,128)}), f32[8,2,32,128]{3,2,1,0:T(8,128)S(1)}, u32[]{:S(2)}, u32[]{:S(2)}) async-start(f32[8,2,32,128]{3,2,1,0:T(8,128)} %get-tuple-element.22), calls=%async_computation | async-start | bytes 524288 | tf_op jit(solution)/shard_map/all_to_all | solution.py:633
  11.5 3.9 %collective-permute-start = (f32[1,16,256]{2,1,0:T(8,128)S(1)}, f32[1,16,256]{2,1,0:T(8,128)S(1)}, u32[]{:S(2)}, u32[]{:S(2)}) collective-permute-start(f32[1,16,256]{2,1,0:T(8,128)S(1)} %slice.9), channel_id=1, source_target_pairs={{0,4},{4,8},{8,12},{12,16},{16,20},{20,24},{24,28},{1,5},{5,9},{9,... | collective-permute-start | bytes 49160 | tf_op jit(solution)/shard_map/ppermute | solution.py:634
  15.5 0.2 collective-permute-start.2
  15.6 0.4 collective-permute-start.1
  16.0 4.4 %all-to-all-done.got = f32[8,2,32,128]{3,2,1,0:T(8,128)S(1)} async-done(((f32[8,2,32,128]{3,2,1,0:T(8,128)}), f32[8,2,32,128]{3,2,1,0:T(8,128)S(1)}, u32[]{:S(2)}, u32[]{:S(2)}) %all-to-all-start) | async-done | bytes 262176 | tf_op jit(solution)/shard_map/all_to_all | solution.py:633
  20.4 2.7 %shard_map.78 = (f32[4,2,256,128]{3,2,1,0:T(8,128)S(1)}, f32[136,8,128]{2,1,0:T(8,128)S(1)}, s32[8,128]{1,0:T(8,128)S(1)}) custom-call(f32[8,2,32,128]{3,2,1,0:T(8,128)S(1)} %all-to-all-done.got), custom_call_target="tpu_custom_call" | custom-call | tf_op jit(solution)/shard_map/pallas_call | solution.py:641
  23.2 0.7 %shard_map.79 = (f32[5,16,256]{2,1,0:T(8,128)S(1)}, f32[15,3,16,256]{3,2,1,0:T(8,128)S(1)}) custom-call(f32[4,2,256,128]{3,2,1,0:T(8,128)S(1)} %get-tuple-element.23.totals, f32[16,16,256]{2,1,0:T(8,128)S(1)} %copy-done.1, f32[1,16,256]{2,1,0:T(8,128)S(1)} %collective-permute-done.below, f32[16,1,256]{2,1,0:T(1,128)S(1)} %collective-permute-done.1.x_low, ...), custom_call_target="tpu_custom_call" | custom-call | tf_op jit(solution)/shard_map/pallas_call | solution.py:654
  23.8 1.5 %collective-permute-start.3 = (f32[5,16,256]{2,1,0:T(8,128)S(1)}, f32[5,16,256]{2,1,0:T(8,128)S(1)}, u32[]{:S(2)}, u32[]{:S(2)}) collective-permute-start(f32[5,16,256]{2,1,0:T(8,128)S(1)} %get-tuple-element.26.mine.refs_0_), channel_id=1, source_target_pairs={{0,4},{4,0},{8,12},{12,8},{16,20},{20,16},{24,28},{28,24},{1,5},{5... | collective-permute-start | bytes 245768 | tf_op jit(solution)/shard_map/ppermute | solution.py:668
  25.3 3.0 %shard_map.80 = (f32[3,44,8,128]{3,2,1,0:T(8,128)S(1)}, f32[44,8,128]{2,1,0:T(8,128)S(1)}, s32[44,8,128]{2,1,0:T(8,128)S(1)}, f8e4m3fn[4,576,256]{2,1,0:T(32,128)(4,1)S(1)}) custom-call(f32[136,8,128]{2,1,0:T(8,128)S(1)} %get-tuple-element.27.codes, s32[8,128]{1,0:T(8,128)S(1)} %get-tuple-element.25.runs.runs_vmem, ...), custom_call_target="tpu_custom_call" | custom-call | flops 2000000000 | bytes 10000000 | tf_op jit(solution)/shard_map/pallas_call | solution.py:669
  28.3 0.1 collective-permute-done.3.other.refs_1_
  28.4 1.1 %collective-permute-start.4 = (f32[5,16,256]{2,1,0:T(8,128)S(1)}, f32[5,16,256]{2,1,0:T(8,128)S(1)}, u32[]{:S(2)}, u32[]{:S(2)}) collective-permute-start(f32[5,16,256]{2,1,0:T(8,128)S(1)} %shard_map.81.refs_1_.mine), channel_id=1, source_target_pairs={{0,8},{4,12},{8,0},{12,4},{16,24},{20,28},{24,16},{28,20},{1,9},{5... | collective-permute-start | bytes 245768 | tf_op jit(solution)/shard_map/ppermute | solution.py:668
  29.5 2.3 %shard_map.82 = (f32[3,44,8,128]{3,2,1,0:T(8,128)S(1)}, f32[44,8,128]{2,1,0:T(8,128)S(1)}, s32[44,8,128]{2,1,0:T(8,128)S(1)}) custom-call(f32[136,8,128]{2,1,0:T(8,128)S(1)} %get-tuple-element.27.codes, s32[8,128]{1,0:T(8,128)S(1)} %get-tuple-element.25.runs.runs_vmem, f8e4m3fn[4,576,256]{2,1,0:T(32,128)(4,1)S(1)} %get-tuple-element.29.refs_0_, ...), custom_call_target="tpu_custom_call" | custom-call | flops 2000000000 | bytes 10000000 | tf_op jit(solution)/shard_map/pallas_call | solution.py:669
  31.8 1.1 %collective-permute-done.4.other.refs_2_ = f32[5,16,256]{2,1,0:T(8,128)S(1)} collective-permute-done((f32[5,16,256]{2,1,0:T(8,128)S(1)}, f32[5,16,256]{2,1,0:T(8,128)S(1)}, u32[]{:S(2)}, u32[]{:S(2)}) %collective-permute-start.4) | collective-permute-done | bytes 81952 | tf_op jit(solution)/shard_map/ppermute | solution.py:668
  32.9 1.3 %collective-permute-start.5 = (f32[2,16,256]{2,1,0:T(8,128)S(1)}, f32[2,16,256]{2,1,0:T(8,128)S(1)}, u32[]{:S(2)}, u32[]{:S(2)}) collective-permute-start(f32[2,16,256]{2,1,0:T(8,128)S(1)} %shard_map.83.refs_1_), channel_id=1, source_target_pairs={{0,16},{4,20},{8,24},{12,28},{16,0},{20,4},{24,8},{28,12},{1,17},{... | collective-permute-start | bytes 98312 | tf_op jit(solution)/shard_map/ppermute | solution.py:668
  34.2 2.3 %shard_map.84 = (f32[3,44,8,128]{3,2,1,0:T(8,128)S(1)}, f32[44,8,128]{2,1,0:T(8,128)S(1)}, s32[44,8,128]{2,1,0:T(8,128)S(1)}) custom-call(f32[136,8,128]{2,1,0:T(8,128)S(1)} %get-tuple-element.27.codes, s32[8,128]{1,0:T(8,128)S(1)} %get-tuple-element.25.runs.runs_vmem, f8e4m3fn[4,576,256]{2,1,0:T(32,128)(4,1)S(1)} %get-tuple-element.29.refs_0_, ...), custom_call_target="tpu_custom_call" | custom-call | flops 2000000000 | bytes 10000000 | tf_op jit(solution)/shard_map/pallas_call | solution.py:669
  36.5 1.3 %collective-permute-done.5.refs_3_ = f32[2,16,256]{2,1,0:T(8,128)S(1)} collective-permute-done((f32[2,16,256]{2,1,0:T(8,128)S(1)}, f32[2,16,256]{2,1,0:T(8,128)S(1)}, u32[]{:S(2)}, u32[]{:S(2)}) %collective-permute-start.5) | collective-permute-done | bytes 32800 | tf_op jit(solution)/shard_map/ppermute | solution.py:668
  37.8 2.4 %shard_map.85 = (f32[2,16,256]{2,1,0:T(8,128)S(1)}, f32[8,32,128]{2,1,0:T(8,128)}) custom-call(s32[8,128]{1,0:T(8,128)S(1)} %get-tuple-element.25.runs.runs_vmem, f32[5,16,256]{2,1,0:T(8,128)S(1)} %get-tuple-element.26.mine.refs_0_, f32[5,16,256]{2,1,0:T(8,128)S(1)} %collective-permute-done.3.other.refs_1_, ...), custom_call_target="tpu_custom_call" | custom-call | tf_op jit(solution)/shard_map/pallas_call | solution.py:686
  40.2 4.5 %all-to-all-start.1 = ((f32[8,32,128]{2,1,0:T(8,128)}), f32[8,32,128]{2,1,0:T(8,128)S(1)}, u32[]{:S(2)}, u32[]{:S(2)}) async-start(f32[8,32,128]{2,1,0:T(8,128)} %get-tuple-element.39), calls=%async_computation.1 | async-start | bytes 262144 | tf_op jit(solution)/shard_map/all_to_all | solution.py:692
  44.7 0.0 copy-start.2
  44.7 0.7 %shard_map.86 = f32[16,16,256]{2,1,0:T(8,128)} custom-call(f32[15,3,16,256]{3,2,1,0:T(8,128)S(1)} %get-tuple-element.24.refs_0_.factors, f32[2,16,256]{2,1,0:T(8,128)S(1)} %get-tuple-element.38.edges), custom_call_target="tpu_custom_call" | custom-call | tf_op jit(solution)/shard_map/pallas_call | solution.py:691
  45.5 6.6 %all-to-all-done.1 = f32[8,32,128]{2,1,0:T(8,128)S(1)} async-done(((f32[8,32,128]{2,1,0:T(8,128)}), f32[8,32,128]{2,1,0:T(8,128)S(1)}, u32[]{:S(2)}, u32[]{:S(2)}) %all-to-all-start.1) | async-done | bytes 131104 | tf_op jit(solution)/shard_map/all_to_all | solution.py:692
  52.0 1.2 %shard_map.87 = f32[3,128,128]{2,1,0:T(8,128)} custom-call(f32[256,128]{1,0:T(8,128)S(1)} %bitcast.2, s32[128,128]{1,0:T(8,128)S(1)} %get-tuple-element.40.meta, s32[128,128]{1,0:T(8,128)S(1)} %get-tuple-element.41.starts, f32[3,128,128]{2,1,0:T(8,128)S(1)} %copy-done, f32[3,128,128]{2,1,0:T(8,128)S(1)} %copy-done.2), custom_call_target="tpu_custom_call" | custom-call | tf_op jit(solution)/shard_map/pallas_call | solution.py:693
  (11 shorter events, 0.1 us)
Async XLA Ops:
  4.1 7.4 %copy-start.1 = (f32[16,16,256]{2,1,0:T(8,128)S(1)}, f32[16,16,256]{2,1,0:T(8,128)}, u32[]{:S(2)}) copy-start(f32[16,16,256]{2,1,0:T(8,128)} %temp.1) | copy-start | bytes 786436
  4.1 16.3 %all-to-all-start = ((f32[8,2,32,128]{3,2,1,0:T(8,128)}), f32[8,2,32,128]{3,2,1,0:T(8,128)S(1)}, u32[]{:S(2)}, u32[]{:S(2)}) async-start(f32[8,2,32,128]{3,2,1,0:T(8,128)} %get-tuple-element.22), calls=%async_computation | async-start | bytes 524288 | tf_op jit(solution)/shard_map/all_to_all | solution.py:633
  11.5 11.6 %collective-permute-start = (f32[1,16,256]{2,1,0:T(8,128)S(1)}, f32[1,16,256]{2,1,0:T(8,128)S(1)}, u32[]{:S(2)}, u32[]{:S(2)}) collective-permute-start(f32[1,16,256]{2,1,0:T(8,128)S(1)} %slice.9), channel_id=1, source_target_pairs={{0,4},{4,8},{8,12},{12,16},{16,20},{20,24},{24,28},{1,5},{5,9},{9,... | collective-permute-start | bytes 49160 | tf_op jit(solution)/shard_map/ppermute | solution.py:634
  15.5 7.7 %collective-permute-start.2 = (f32[16,1,256]{2,1,0:T(1,128)S(1)}, f32[16,1,256]{2,1,0:T(1,128)S(1)}, u32[]{:S(2)}, u32[]{:S(2)}) collective-permute-start(f32[16,1,256]{2,1,0:T(1,128)S(1)} %get-tuple-element.42), channel_id=1, source_target_pairs={{1,0},{2,1},{3,2},{0,3},{5,4},{6,5},{7,6},{4,7},{9,8},{10,9},{11,1... | collective-permute-start | bytes 49160 | tf_op jit(solution)/shard_map/ppermute | solution.py:638
  15.6 7.5 %collective-permute-start.1 = (f32[16,1,256]{2,1,0:T(1,128)S(1)}, f32[16,1,256]{2,1,0:T(1,128)S(1)}, u32[]{:S(2)}, u32[]{:S(2)}) collective-permute-start(f32[16,1,256]{2,1,0:T(1,128)S(1)} %get-tuple-element.43), channel_id=1, source_target_pairs={{0,1},{1,2},{2,3},{3,0},{4,5},{5,6},{6,7},{7,4},{8,9},{9,10},{10,1... | collective-permute-start | bytes 49160 | tf_op jit(solution)/shard_map/ppermute | solution.py:635
  23.8 4.5 %collective-permute-start.3 = (f32[5,16,256]{2,1,0:T(8,128)S(1)}, f32[5,16,256]{2,1,0:T(8,128)S(1)}, u32[]{:S(2)}, u32[]{:S(2)}) collective-permute-start(f32[5,16,256]{2,1,0:T(8,128)S(1)} %get-tuple-element.26.mine.refs_0_), channel_id=1, source_target_pairs={{0,4},{4,0},{8,12},{12,8},{16,20},{20,16},{24,28},{28,24},{1,5},{5... | collective-permute-start | bytes 245768 | tf_op jit(solution)/shard_map/ppermute | solution.py:668
  28.4 4.5 %collective-permute-start.4 = (f32[5,16,256]{2,1,0:T(8,128)S(1)}, f32[5,16,256]{2,1,0:T(8,128)S(1)}, u32[]{:S(2)}, u32[]{:S(2)}) collective-permute-start(f32[5,16,256]{2,1,0:T(8,128)S(1)} %shard_map.81.refs_1_.mine), channel_id=1, source_target_pairs={{0,8},{4,12},{8,0},{12,4},{16,24},{20,28},{24,16},{28,20},{1,9},{5... | collective-permute-start | bytes 245768 | tf_op jit(solution)/shard_map/ppermute | solution.py:668
  32.9 4.9 %collective-permute-start.5 = (f32[2,16,256]{2,1,0:T(8,128)S(1)}, f32[2,16,256]{2,1,0:T(8,128)S(1)}, u32[]{:S(2)}, u32[]{:S(2)}) collective-permute-start(f32[2,16,256]{2,1,0:T(8,128)S(1)} %shard_map.83.refs_1_), channel_id=1, source_target_pairs={{0,16},{4,20},{8,24},{12,28},{16,0},{20,4},{24,8},{28,12},{1,17},{... | collective-permute-start | bytes 98312 | tf_op jit(solution)/shard_map/ppermute | solution.py:668
  40.2 11.9 %all-to-all-start.1 = ((f32[8,32,128]{2,1,0:T(8,128)}), f32[8,32,128]{2,1,0:T(8,128)S(1)}, u32[]{:S(2)}, u32[]{:S(2)}) async-start(f32[8,32,128]{2,1,0:T(8,128)} %get-tuple-element.39), calls=%async_computation.1 | async-start | bytes 262144 | tf_op jit(solution)/shard_map/all_to_all | solution.py:692
  44.7 7.3 %copy-start = (f32[3,128,128]{2,1,0:T(8,128)S(1)}, f32[3,128,128]{2,1,0:T(8,128)}, u32[]{:S(2)}) copy-start(f32[3,128,128]{2,1,0:T(8,128)} %velocity.1) | copy-start | bytes 589828
  44.7 7.3 %copy-start.2 = (f32[3,128,128]{2,1,0:T(8,128)S(1)}, f32[3,128,128]{2,1,0:T(8,128)}, u32[]{:S(2)}) copy-start(f32[3,128,128]{2,1,0:T(8,128)} %noise.1) | copy-start | bytes 589828

commit v4 on v3

--- a/solution.py
+++ b/solution.py
@@ -254,28 +254,27 @@
     return jnp.where(spot < last, loaded, 0.0)
 
 
-def bin_kernel(dims, parts, levels, got, totals, codes, runs_vmem, lhs, rhs, runs, arrived):
+def bin_kernel(dims, parts, got, totals, codes, runs_vmem, lhs, rhs):
     planes, width_x, width_y = dims
     slabs, _, rows, lanes = got.shape
     part_rows = planes * width_x // parts
     find_runs(dims, parts, got, runs_vmem)
-    copy = pltpu.make_async_copy(runs_vmem, runs, arrived.at[0])
-    copy.start()
+    runs = runs_vmem[...]
+    first = [[runs[s, 2 * c] for s in range(slabs)] for c in range(parts)]
+    last = [[runs[s, 2 * c + 1] for s in range(slabs)] for c in range(parts)]
+    longest = runs[0, 2 * parts]
     one = jnp.ones((), F8)
     zero = jnp.zeros((), F8)
     y_id = iota((width_y, lanes), 0).astype(F32).astype(BF16)
     totals[...] = jnp.zeros(totals.shape, F32)
-    copy.wait()
-    longest = runs[0, 2 * parts]
 
     def add_rows(turn, carry):
         for c in range(parts):
             row_id = (iota((part_rows, lanes), 0) + (c * part_rows + 1)).astype(F32).astype(BF16)
             for s in range(slabs):
-                spot = runs[s, 2 * c] + turn
-                last = runs[s, 2 * c + 1]
-                pieces = split_small(run_row(got, 0, s, spot, last))
-                code = run_row(got, 1, s, spot, last)
+                spot = first[c][s] + turn
+                pieces = split_small(run_row(got, 0, s, spot, last[c][s]))
+                code = run_row(got, 1, s, spot, last[c][s])
                 codes[turn * parts + c, pl.ds(s, 1), :] = code
                 row, y_cell = decode(code, width_y)
                 here = pl.ds(s * lanes, lanes)
@@ -296,8 +295,6 @@
         return carry
 
     lax.fori_loop(0, longest, add_rows, 0)
-    for i in range((levels - 1) * parts):
-        codes[longest * parts + i] = jnp.zeros((slabs, lanes), F32)
 
 
 def solve_kernel(dims, totals, temp, below, x_low, x_high, summary, factors):
@@ -412,14 +409,14 @@
     one = jnp.ones((), F8)
     zero = jnp.zeros((), F8)
     y_id = iota((width_y, lanes), 0).astype(F32).astype(BF16)
-    last_lane = iota((1, lanes), 1) == 2 * parts
-    turns = jnp.max(jnp.where(last_lane, runs[0:1, :].astype(F32), 0.0)).astype(jnp.int32)
+    order = levels - 1 - phase
+    turns = runs[0:1, :][0, 2 * parts]
 
     def find_rows(step, carry):
         wanted = []
         for c in range(parts):
             block = step * parts + c
-            row, y_cell = decode(codes[(step * levels + phase) * parts + c], width_y)
+            row, y_cell = decode(codes[(step * levels + order) * parts + c], width_y)
             wanted.append(row)
             hot = y_cell.astype(BF16)
             for s in range(slabs):
@@ -451,7 +448,7 @@
                     found[t, block, pl.ds(s, 1), :] = chosen * (1.0 / SCALE)
         return carry
 
-    lax.fori_loop(0, quotient_up(turns, levels), find_rows, 0)
+    lax.fori_loop(0, quotient_up(turns - order, levels), find_rows, 0)
 
 
 def quotient_up(value, size):
@@ -466,13 +463,14 @@
     found = refs[levels + 1 : 2 * levels + 1]
     keys = refs[2 * levels + 1 : 3 * levels + 1]
     lane_of = refs[3 * levels + 1 : 4 * levels + 1]
-    edges, reply, temps, runs, arrived = refs[4 * levels + 1 :]
+    edges, reply, temps, spread = refs[4 * levels + 1 :]
     slabs, rows, lanes = reply.shape
     part_x = width_x // parts
     halves = width_y // lanes
-    copy = pltpu.make_async_copy(runs_vmem, runs, arrived.at[0])
-    copy.start()
-    reply[...] = jnp.zeros(reply.shape, F32)
+    runs = runs_vmem[...]
+    first = [[runs[s, 2 * c] for s in range(slabs)] for c in range(parts)]
+    longest = runs[0, 2 * parts]
+    spread[:, :, pl.ds(0, rows), :] = jnp.zeros((parts, slabs, rows, lanes), F32)
     index = lax.axis_index("gz")
     zeros = jnp.zeros_like(own[0])
     top = (index & (1 << (levels - 1))) != 0
@@ -489,14 +487,14 @@
     value = (through[1] + after[1]) / (through[0] + after[0])
     edges[0] = (before[1] + own[2] + own[0] * value) / (before[0] + own[1] + own[0])
     edges[1] = value
-    copy.wait()
 
     def fill_rows(step, carry):
         for phase in range(levels):
+            done = step * levels + (levels - 1 - phase) < longest
             for c in range(parts):
                 block = step * parts + c
                 key = keys[phase][block]
-                lane = lane_of[phase][block]
+                lane = lane_of[phase][block] & (lanes - 1)
                 ends = [jnp.zeros((slabs, lanes), F32), jnp.zeros((slabs, lanes), F32)]
                 for x in range(part_x):
                     for h in range(halves):
@@ -507,20 +505,25 @@
                             ends[e] = jnp.where(
                                 hit, jnp.take_along_axis(line, lane, axis=1), ends[e]
                             )
-                temps[phase * parts + c] = (
+                temps[phase * parts + c] = jnp.where(
+                    done,
                     found[phase][0, block]
                     + found[phase][1, block] * ends[0]
-                    + found[phase][2, block] * ends[1]
+                    + found[phase][2, block] * ends[1],
+                    0.0,
                 )
         for phase in range(levels):
             for c in range(parts):
                 for s in range(slabs):
-                    spot = runs[s, 2 * c] + (step * levels + phase)
-                    here = pl.ds(jnp.minimum(spot, rows - 1), 1)
-                    reply[s, here, :] += temps[phase * parts + c, pl.ds(s, 1), :]
+                    spot = first[c][s] + step * levels + (levels - 1 - phase)
+                    spread[c, s, pl.ds(spot, 1), :] = temps[phase * parts + c, pl.ds(s, 1), :]
         return carry
 
-    lax.fori_loop(0, quotient_up(runs[0, 2 * parts], levels), fill_rows, 0)
+    lax.fori_loop(0, quotient_up(longest, levels), fill_rows, 0)
+    total = spread[0, :, pl.ds(0, rows), :]
+    for c in range(1, parts):
+        total = total + spread[c, :, pl.ds(0, rows), :]
+    reply[...] = total
 
 
 def fill_kernel(factors, edges, new_temp):
@@ -619,9 +622,6 @@
     rows = 2 * bricks // slabs
     parts = PARTS
     assert width_x % parts == 0 and parts <= 4 and lanes <= 128
-    run_shape = (slabs, lanes)
-    run_scratch = (pltpu.SMEM(run_shape, jnp.int32), pltpu.SemaphoreType.DMA((1,)))
-
     send, meta, starts = route_call(
         dims, slabs, rows, parts, atom_velocity.shape, atom_plane.shape
     )(
@@ -639,17 +639,16 @@
         electron_temp[:, :1], "gx", [((i + 1) % groups, i) for i in range(groups)]
     )
     totals, codes, runs = call(
-        functools.partial(bin_kernel, dims, parts, levels),
+        functools.partial(bin_kernel, dims, parts),
         (
             struct(PIECES + 1, width_y // lanes, cells, lanes),
-            struct(parts * (rows + levels - 1), slabs, lanes),
-            struct(*run_shape, dtype=jnp.int32),
+            struct(parts * (rows + 1), slabs, lanes),
+            struct(slabs, lanes, dtype=jnp.int32),
         ),
         (
             pltpu.VMEM((parts, (PIECES + 1) * cells // parts, slabs * lanes), F8),
             pltpu.VMEM((parts, width_y, slabs * lanes), F8),
-        )
-        + run_scratch,
+        ),
     )(got)
     total, factors = call(
         functools.partial(solve_kernel, dims),
@@ -686,7 +685,10 @@
     edges, reply = call(
         functools.partial(join_kernel, dims, parts, levels),
         (struct(2, width_x, width_y), struct(slabs, rows, lanes)),
-        (pltpu.VMEM((levels * parts, slabs, lanes), F32),) + run_scratch,
+        (
+            pltpu.VMEM((levels * parts, slabs, lanes), F32),
+            pltpu.VMEM((parts, slabs, 2 * rows + 8 * levels, lanes), F32),
+        ),
     )(runs, *pieces, *(phase[i] for i in range(3) for phase in found))
     new_temp = call(fill_kernel, struct(*dims))(factors, edges)
     returned = lax.all_to_all(reply, "gz", split_axis=0, concat_axis=0, tiled=True)

time: 53.6 us -> 52.6 us (0.981)
  waiting for transfers between devices: 13.4 us -> 17.1 us
  Pallas kernels: 18.8 us -> 15.2 us
  starting transfers between devices: 20.3 us -> 19.1 us
    ppermute x3, waiting for transfers between devices: 2.39 us -> 6.18 us  [body(): lax.ppermute(total, 'gz', [(i, i ^ 1 << level) for i in range(slabs)])]
    pallas_call x3, Pallas kernels: 7.59 us -> 5.24 us  [body(): call(functools.partial(look_kernel, dims, parts, levels, level), found_sh...]
    all_to_all x1, starting transfers between devices: 4.52 us -> 3.57 us  [body(): lax.all_to_all(reply, 'gz', split_axis=0, concat_axis=0, tiled=True)]
    pallas_call x1, Pallas kernels: 2.39 us -> 1.52 us  [body(): call(functools.partial(join_kernel, dims, parts, levels), (struct(2, widt...]
  transfers between devices with their start and end apart: 8 -> 8, of which waited for: 5 -> 5; matrix products, arithmetic and copies ran while one was open for 0% -> 0% of each run, Pallas kernels for 21% -> 16%
where the time goes in v4:
time: 52.6 us; the launch traced here: 52.3 us
  starting transfers between devices  19.1 us (36%)
  waiting for transfers between devices  17.1 us (33%)
  Pallas kernels  15.2 us (29%)
  between operations  0.77 us (1%)
    all_to_all x1, starting transfers between devices, body(): got = lax.all_to_all(send, 'gz', split_axis=0, concat_axis=0, tiled=True)  7.4 us
    all_to_all x1, waiting for transfers between devices, body(): lax.all_to_all(reply, 'gz', split_axis=0, concat_axis=0, tiled=True)  6.59 us
    ppermute x3, waiting for transfers between devices, body(): lax.ppermute(total, 'gz', [(i, i ^ 1 << level) for i in range(slabs)])  6.18 us
    pallas_call x3, Pallas kernels, body(): call(functools.partial(look_kernel, dims, parts, levels, level), found_sh...  5.24 us
    all_to_all x1, waiting for transfers between devices, body(): got = lax.all_to_all(send, 'gz', split_axis=0, concat_axis=0, tiled=True)  4.38 us
    ppermute x1, starting transfers between devices, body(): lax.ppermute(electron_temp[-1:], 'gz', [(i, i + 1) for i in range(slabs -...  3.92 us
    ppermute x3, starting transfers between devices, body(): lax.ppermute(total, 'gz', [(i, i ^ 1 << level) for i in range(slabs)])  3.66 us
    all_to_all x1, starting transfers between devices, body(): lax.all_to_all(reply, 'gz', split_axis=0, concat_axis=0, tiled=True)  3.57 us
  transfers between devices with their start and end apart: 8, of which 5 were waited for; matrix products, arithmetic and copies ran while one was open for 0% of the time, Pallas kernels for 16%

profile of v4, /device:TPU:0, one launch (start us, length us, event | category | flops | bytes accessed | tf_op | source)
XLA Modules:
  0.0 52.3 jit_solution(1047250053730921653)
XLA Ops:
  0.6 3.4 %shard_map.77 = (f32[8,2,32,128]{3,2,1,0:T(8,128)}, s32[128,128]{1,0:T(8,128)S(1)}, s32[128,128]{1,0:T(8,128)S(1)}) custom-call(s32[1,128]{1,0:T(1,128)} %bitcast.3, f32[3,128,128]{2,1,0:T(8,128)} %velocity.1, s32[128,128]{1,0:T(8,128)} %plane_hbm.1, s32[128,128]{1,0:T(8,128)} %column_hbm.1), custom_call_target="tpu_custom_call" | custom-call | tf_op jit(solution)/shard_map/pallas_call | solution.py:625
  4.1 0.0 copy-start.1
  4.1 7.4 %all-to-all-start = ((f32[8,2,32,128]{3,2,1,0:T(8,128)}), f32[8,2,32,128]{3,2,1,0:T(8,128)S(1)}, u32[]{:S(2)}, u32[]{:S(2)}) async-start(f32[8,2,32,128]{3,2,1,0:T(8,128)} %get-tuple-element.22), calls=%async_computation | async-start | bytes 524288 | tf_op jit(solution)/shard_map/all_to_all | solution.py:633
  11.5 3.9 %collective-permute-start = (f32[1,16,256]{2,1,0:T(8,128)S(1)}, f32[1,16,256]{2,1,0:T(8,128)S(1)}, u32[]{:S(2)}, u32[]{:S(2)}) collective-permute-start(f32[1,16,256]{2,1,0:T(8,128)S(1)} %slice.9), channel_id=1, source_target_pairs={{0,4},{4,8},{8,12},{12,16},{16,20},{20,24},{24,28},{1,5},{5,9},{9,... | collective-permute-start | bytes 49160 | tf_op jit(solution)/shard_map/ppermute | solution.py:634
  15.5 0.2 collective-permute-start.2
  15.6 0.4 collective-permute-start.1
  16.0 4.4 %all-to-all-done.got = f32[8,2,32,128]{3,2,1,0:T(8,128)S(1)} async-done(((f32[8,2,32,128]{3,2,1,0:T(8,128)}), f32[8,2,32,128]{3,2,1,0:T(8,128)S(1)}, u32[]{:S(2)}, u32[]{:S(2)}) %all-to-all-start) | async-done | bytes 262176 | tf_op jit(solution)/shard_map/all_to_all | solution.py:633
  20.4 2.3 %shard_map.78 = (f32[4,2,256,128]{3,2,1,0:T(8,128)S(1)}, f32[132,8,128]{2,1,0:T(8,128)S(1)}, s32[8,128]{1,0:T(8,128)S(1)}) custom-call(f32[8,2,32,128]{3,2,1,0:T(8,128)S(1)} %all-to-all-done.got), custom_call_target="tpu_custom_call" | custom-call | tf_op jit(solution)/shard_map/pallas_call | solution.py:641
  22.8 0.7 %shard_map.79 = (f32[5,16,256]{2,1,0:T(8,128)S(1)}, f32[15,3,16,256]{3,2,1,0:T(8,128)S(1)}) custom-call(f32[4,2,256,128]{3,2,1,0:T(8,128)S(1)} %get-tuple-element.23.totals, f32[16,16,256]{2,1,0:T(8,128)S(1)} %copy-done.1, f32[1,16,256]{2,1,0:T(8,128)S(1)} %collective-permute-done.below, f32[16,1,256]{2,1,0:T(1,128)S(1)} %collective-permute-done.1.x_low, ...), custom_call_target="tpu_custom_call" | custom-call | tf_op jit(solution)/shard_map/pallas_call | solution.py:653
  23.4 2.9 %collective-permute-start.3 = (f32[5,16,256]{2,1,0:T(8,128)S(1)}, f32[5,16,256]{2,1,0:T(8,128)S(1)}, u32[]{:S(2)}, u32[]{:S(2)}) collective-permute-start(f32[5,16,256]{2,1,0:T(8,128)S(1)} %get-tuple-element.26.mine.refs_0_), channel_id=1, source_target_pairs={{0,4},{4,0},{8,12},{12,8},{16,20},{20,16},{24,28},{28,24},{1,5},{5... | collective-permute-start | bytes 245768 | tf_op jit(solution)/shard_map/ppermute | solution.py:667
  26.3 1.7 %shard_map.80 = (f32[3,44,8,128]{3,2,1,0:T(8,128)S(1)}, f32[44,8,128]{2,1,0:T(8,128)S(1)}, s32[44,8,128]{2,1,0:T(8,128)S(1)}, f8e4m3fn[4,576,256]{2,1,0:T(32,128)(4,1)S(1)}) custom-call(f32[132,8,128]{2,1,0:T(8,128)S(1)} %get-tuple-element.27.codes, s32[8,128]{1,0:T(8,128)S(1)} %get-tuple-element.25.runs.runs_vmem, ...), custom_call_target="tpu_custom_call" | custom-call | flops 2000000000 | bytes 10000000 | tf_op jit(solution)/shard_map/pallas_call | solution.py:668
  28.0 0.7 %collective-permute-done.3.other.refs_1_ = f32[5,16,256]{2,1,0:T(8,128)S(1)} collective-permute-done((f32[5,16,256]{2,1,0:T(8,128)S(1)}, f32[5,16,256]{2,1,0:T(8,128)S(1)}, u32[]{:S(2)}, u32[]{:S(2)}) %collective-permute-start.3) | collective-permute-done | bytes 81952 | tf_op jit(solution)/shard_map/ppermute | solution.py:667
  28.7 0.3 collective-permute-start.4
  29.1 1.2 %shard_map.82 = (f32[3,44,8,128]{3,2,1,0:T(8,128)S(1)}, f32[44,8,128]{2,1,0:T(8,128)S(1)}, s32[44,8,128]{2,1,0:T(8,128)S(1)}) custom-call(f32[132,8,128]{2,1,0:T(8,128)S(1)} %get-tuple-element.27.codes, s32[8,128]{1,0:T(8,128)S(1)} %get-tuple-element.25.runs.runs_vmem, f8e4m3fn[4,576,256]{2,1,0:T(32,128)(4,1)S(1)} %get-tuple-element.29.refs_0_, ...), custom_call_target="tpu_custom_call" | custom-call | flops 2000000000 | bytes 10000000 | tf_op jit(solution)/shard_map/pallas_call | solution.py:668
  30.3 3.3 %collective-permute-done.4.other.refs_2_ = f32[5,16,256]{2,1,0:T(8,128)S(1)} collective-permute-done((f32[5,16,256]{2,1,0:T(8,128)S(1)}, f32[5,16,256]{2,1,0:T(8,128)S(1)}, u32[]{:S(2)}, u32[]{:S(2)}) %collective-permute-start.4) | collective-permute-done | bytes 81952 | tf_op jit(solution)/shard_map/ppermute | solution.py:667
  33.6 0.4 collective-permute-start.5
  34.1 2.3 %shard_map.84 = (f32[3,44,8,128]{3,2,1,0:T(8,128)S(1)}, f32[44,8,128]{2,1,0:T(8,128)S(1)}, s32[44,8,128]{2,1,0:T(8,128)S(1)}) custom-call(f32[132,8,128]{2,1,0:T(8,128)S(1)} %get-tuple-element.27.codes, s32[8,128]{1,0:T(8,128)S(1)} %get-tuple-element.25.runs.runs_vmem, f8e4m3fn[4,576,256]{2,1,0:T(32,128)(4,1)S(1)} %get-tuple-element.29.refs_0_, ...), custom_call_target="tpu_custom_call" | custom-call | flops 2000000000 | bytes 10000000 | tf_op jit(solution)/shard_map/pallas_call | solution.py:668
  36.4 2.2 %collective-permute-done.5.refs_3_ = f32[2,16,256]{2,1,0:T(8,128)S(1)} collective-permute-done((f32[2,16,256]{2,1,0:T(8,128)S(1)}, f32[2,16,256]{2,1,0:T(8,128)S(1)}, u32[]{:S(2)}, u32[]{:S(2)}) %collective-permute-start.5) | collective-permute-done | bytes 32800 | tf_op jit(solution)/shard_map/ppermute | solution.py:667
  38.6 1.5 %shard_map.85 = (f32[2,16,256]{2,1,0:T(8,128)S(1)}, f32[8,32,128]{2,1,0:T(8,128)}) custom-call(s32[8,128]{1,0:T(8,128)S(1)} %get-tuple-element.25.runs.runs_vmem, f32[5,16,256]{2,1,0:T(8,128)S(1)} %get-tuple-element.26.mine.refs_0_, f32[5,16,256]{2,1,0:T(8,128)S(1)} %collective-permute-done.3.other.refs_1_, ...), custom_call_target="tpu_custom_call" | custom-call | tf_op jit(solution)/shard_map/pallas_call | solution.py:685
  40.1 3.6 %all-to-all-start.1 = ((f32[8,32,128]{2,1,0:T(8,128)}), f32[8,32,128]{2,1,0:T(8,128)S(1)}, u32[]{:S(2)}, u32[]{:S(2)}) async-start(f32[8,32,128]{2,1,0:T(8,128)} %get-tuple-element.39), calls=%async_computation.1 | async-start | bytes 262144 | tf_op jit(solution)/shard_map/all_to_all | solution.py:694
  43.7 0.0 copy-start.2
  43.7 0.7 %shard_map.86 = f32[16,16,256]{2,1,0:T(8,128)} custom-call(f32[15,3,16,256]{3,2,1,0:T(8,128)S(1)} %get-tuple-element.24.refs_0_.factors, f32[2,16,256]{2,1,0:T(8,128)S(1)} %get-tuple-element.38.edges), custom_call_target="tpu_custom_call" | custom-call | tf_op jit(solution)/shard_map/pallas_call | solution.py:693
  44.4 6.6 %all-to-all-done.1 = f32[8,32,128]{2,1,0:T(8,128)S(1)} async-done(((f32[8,32,128]{2,1,0:T(8,128)}), f32[8,32,128]{2,1,0:T(8,128)S(1)}, u32[]{:S(2)}, u32[]{:S(2)}) %all-to-all-start.1) | async-done | bytes 131104 | tf_op jit(solution)/shard_map/all_to_all | solution.py:694
  51.0 1.2 %shard_map.87 = f32[3,128,128]{2,1,0:T(8,128)} custom-call(f32[256,128]{1,0:T(8,128)S(1)} %bitcast.2, s32[128,128]{1,0:T(8,128)S(1)} %get-tuple-element.40.meta, s32[128,128]{1,0:T(8,128)S(1)} %get-tuple-element.41.starts, f32[3,128,128]{2,1,0:T(8,128)S(1)} %copy-done, f32[3,128,128]{2,1,0:T(8,128)S(1)} %copy-done.2), custom_call_target="tpu_custom_call" | custom-call | tf_op jit(solution)/shard_map/pallas_call | solution.py:695
  (11 shorter events, 0.1 us)
Async XLA Ops:
  4.1 7.4 %copy-start.1 = (f32[16,16,256]{2,1,0:T(8,128)S(1)}, f32[16,16,256]{2,1,0:T(8,128)}, u32[]{:S(2)}) copy-start(f32[16,16,256]{2,1,0:T(8,128)} %temp.1) | copy-start | bytes 786436
  4.1 16.3 %all-to-all-start = ((f32[8,2,32,128]{3,2,1,0:T(8,128)}), f32[8,2,32,128]{3,2,1,0:T(8,128)S(1)}, u32[]{:S(2)}, u32[]{:S(2)}) async-start(f32[8,2,32,128]{3,2,1,0:T(8,128)} %get-tuple-element.22), calls=%async_computation | async-start | bytes 524288 | tf_op jit(solution)/shard_map/all_to_all | solution.py:633
  11.5 11.2 %collective-permute-start = (f32[1,16,256]{2,1,0:T(8,128)S(1)}, f32[1,16,256]{2,1,0:T(8,128)S(1)}, u32[]{:S(2)}, u32[]{:S(2)}) collective-permute-start(f32[1,16,256]{2,1,0:T(8,128)S(1)} %slice.9), channel_id=1, source_target_pairs={{0,4},{4,8},{8,12},{12,16},{16,20},{20,24},{24,28},{1,5},{5,9},{9,... | collective-permute-start | bytes 49160 | tf_op jit(solution)/shard_map/ppermute | solution.py:634
  15.5 7.3 %collective-permute-start.2 = (f32[16,1,256]{2,1,0:T(1,128)S(1)}, f32[16,1,256]{2,1,0:T(1,128)S(1)}, u32[]{:S(2)}, u32[]{:S(2)}) collective-permute-start(f32[16,1,256]{2,1,0:T(1,128)S(1)} %get-tuple-element.42), channel_id=1, source_target_pairs={{1,0},{2,1},{3,2},{0,3},{5,4},{6,5},{7,6},{4,7},{9,8},{10,9},{11,1... | collective-permute-start | bytes 49160 | tf_op jit(solution)/shard_map/ppermute | solution.py:638
  15.6 7.1 %collective-permute-start.1 = (f32[16,1,256]{2,1,0:T(1,128)S(1)}, f32[16,1,256]{2,1,0:T(1,128)S(1)}, u32[]{:S(2)}, u32[]{:S(2)}) collective-permute-start(f32[16,1,256]{2,1,0:T(1,128)S(1)} %get-tuple-element.43), channel_id=1, source_target_pairs={{0,1},{1,2},{2,3},{3,0},{4,5},{5,6},{6,7},{7,4},{8,9},{9,10},{10,1... | collective-permute-start | bytes 49160 | tf_op jit(solution)/shard_map/ppermute | solution.py:635
  23.4 5.3 %collective-permute-start.3 = (f32[5,16,256]{2,1,0:T(8,128)S(1)}, f32[5,16,256]{2,1,0:T(8,128)S(1)}, u32[]{:S(2)}, u32[]{:S(2)}) collective-permute-start(f32[5,16,256]{2,1,0:T(8,128)S(1)} %get-tuple-element.26.mine.refs_0_), channel_id=1, source_target_pairs={{0,4},{4,0},{8,12},{12,8},{16,20},{20,16},{24,28},{28,24},{1,5},{5... | collective-permute-start | bytes 245768 | tf_op jit(solution)/shard_map/ppermute | solution.py:667
  28.7 4.9 %collective-permute-start.4 = (f32[5,16,256]{2,1,0:T(8,128)S(1)}, f32[5,16,256]{2,1,0:T(8,128)S(1)}, u32[]{:S(2)}, u32[]{:S(2)}) collective-permute-start(f32[5,16,256]{2,1,0:T(8,128)S(1)} %shard_map.81.refs_1_.mine), channel_id=1, source_target_pairs={{0,8},{4,12},{8,0},{12,4},{16,24},{20,28},{24,16},{28,20},{1,9},{5... | collective-permute-start | bytes 245768 | tf_op jit(solution)/shard_map/ppermute | solution.py:667
  33.6 4.9 %collective-permute-start.5 = (f32[2,16,256]{2,1,0:T(8,128)S(1)}, f32[2,16,256]{2,1,0:T(8,128)S(1)}, u32[]{:S(2)}, u32[]{:S(2)}) collective-permute-start(f32[2,16,256]{2,1,0:T(8,128)S(1)} %shard_map.83.refs_1_), channel_id=1, source_target_pairs={{0,16},{4,20},{8,24},{12,28},{16,0},{20,4},{24,8},{28,12},{1,17},{... | collective-permute-start | bytes 98312 | tf_op jit(solution)/shard_map/ppermute | solution.py:667
  40.1 10.9 %all-to-all-start.1 = ((f32[8,32,128]{2,1,0:T(8,128)}), f32[8,32,128]{2,1,0:T(8,128)S(1)}, u32[]{:S(2)}, u32[]{:S(2)}) async-start(f32[8,32,128]{2,1,0:T(8,128)} %get-tuple-element.39), calls=%async_computation.1 | async-start | bytes 262144 | tf_op jit(solution)/shard_map/all_to_all | solution.py:694
  43.7 7.3 %copy-start = (f32[3,128,128]{2,1,0:T(8,128)S(1)}, f32[3,128,128]{2,1,0:T(8,128)}, u32[]{:S(2)}) copy-start(f32[3,128,128]{2,1,0:T(8,128)} %velocity.1) | copy-start | bytes 589828
  43.7 7.3 %copy-start.2 = (f32[3,128,128]{2,1,0:T(8,128)S(1)}, f32[3,128,128]{2,1,0:T(8,128)}, u32[]{:S(2)}) copy-start(f32[3,128,128]{2,1,0:T(8,128)} %noise.1) | copy-start | bytes 589828

commit v5 on v4

--- a/solution.py
+++ b/solution.py
@@ -132,7 +132,7 @@
     owner_row = jnp.sum(jnp.where(eye, owner_f, 0.0), axis=0, keepdims=True)
     same = owner_f == owner_row
     ahead = same & (lane_b < sub_b)
-    peers = jnp.where(jnp.concatenate([same, ahead], axis=1), 1.0, 0.0).astype(BF16)
+    peers = jnp.where(jnp.concatenate([same, ahead], axis=0), 1.0, 0.0).astype(BF16)
     copies[2].wait()
     col = column[...]
     x_cell = quotient(col, width_y)
@@ -147,19 +147,27 @@
     earlier = [jnp.zeros_like(sizes[0])]
     for c in range(parts - 1):
         earlier.append(earlier[-1] + sizes[c])
-    offsets = jnp.dot(
-        peers,
-        jnp.concatenate(
-            [jnp.concatenate(earlier, axis=1), jnp.concatenate(sizes, axis=1)], axis=0
-        ).astype(BF16),
-        preferred_element_type=F32,
+    joint = jnp.dot(
+        peers, jnp.concatenate(sizes, axis=1).astype(BF16), preferred_element_type=F32
     )
     copies[3].wait()
     vx, vy, vz = velocity[0], velocity[1], velocity[2]
     kinetic = 0.5 * (vx * vx + vy * vy + vz * vz)
+    dense = jnp.zeros((bricks, lanes), F32)
+    whole = jnp.zeros((bricks, lanes), F32)
+    bases = []
+    for c in range(parts):
+        bases.append((dense, whole))
+        size = joint[:bricks, c * lanes : (c + 1) * lanes]
+        dense = dense + size
+        whole = whole + jnp.floor((size + (lanes - 1)) * (1.0 / lanes)) * lanes
     begins = [
-        offsets[:, c * lanes : (c + 1) * lanes].astype(jnp.int32) + owner * (rows * lanes)
-        for c in range(parts)
+        owner * (rows * lanes)
+        + (
+            jnp.where(whole <= rows * lanes, base[1], base[0])
+            + joint[bricks:, c * lanes : (c + 1) * lanes]
+        ).astype(jnp.int32)
+        for c, base in enumerate(bases)
     ]
     shifts = [begin & (lanes - 1) for begin in begins]
     packed = ranks[0].astype(jnp.int32)
@@ -232,19 +240,23 @@
     slabs, _, rows, lanes = got.shape
     part_rows = planes * width_x // parts
     codes = got[:, 1]
-    codes = jnp.where(codes > 0.0, codes, float((parts * part_rows + 1) * width_y + 1))
-    longest = jnp.zeros((slabs, lanes), F32)
-    first = jnp.zeros((slabs, lanes), F32)
+    beyond = float((parts * part_rows + 1) * width_y + 1)
+    lead = codes[:, :, 0:1]
+    used = lead > 0.0
+    lead = jnp.where(used, lead, beyond)
+    top = jnp.where(used, jnp.max(codes, axis=2, keepdims=True), beyond)
+    longest = jnp.zeros((slabs, 1), F32)
+    first = jnp.zeros((slabs, 1), F32)
     table = jnp.zeros((slabs, lanes), F32)
     lane = iota((slabs, lanes), 1)
     for c in range(parts):
         limit = float(((c + 1) * part_rows + 1) * width_y)
-        last = jnp.sum(jnp.where(codes < limit, 1.0, 0.0), axis=1)
+        last = jnp.sum(jnp.where(lead < limit, 1.0, 0.0), axis=1)
         longest = jnp.maximum(longest, last - first)
-        table = jnp.where(lane == 2 * c, pltpu.roll(first, 2 * c, 1) if c else first, table)
-        table = jnp.where(lane == 2 * c + 1, pltpu.roll(last, 2 * c + 1, 1), table)
-        first = pltpu.roll(last, 1, 1)
-    longest = jnp.max(jnp.where(lane == 0, longest, 0.0), keepdims=True)
+        table = jnp.where(lane == 2 * c, first, table)
+        table = jnp.where(lane == 2 * c + 1, last, table)
+        first = jnp.sum(jnp.where(top < limit, 1.0, 0.0), axis=1)
+    longest = jnp.max(longest, axis=0, keepdims=True)
     runs_vmem[...] = jnp.where(lane == 2 * parts, longest, table).astype(jnp.int32)
 
 
@@ -254,7 +266,7 @@
     return jnp.where(spot < last, loaded, 0.0)
 
 
-def bin_kernel(dims, parts, got, totals, codes, runs_vmem, lhs, rhs):
+def bin_kernel(dims, parts, got, _, totals, codes, runs_vmem, lhs, rhs):
     planes, width_x, width_y = dims
     slabs, _, rows, lanes = got.shape
     part_rows = planes * width_x // parts
@@ -526,7 +538,7 @@
     reply[...] = total
 
 
-def fill_kernel(factors, edges, new_temp):
+def fill_planes(factors, edges, new_temp):
     planes = new_temp.shape[0]
     edge = edges[0]
     value = edges[1]
@@ -536,46 +548,62 @@
         new_temp[z] = value
 
 
-def kick_kernel(parts, returned, meta, starts, velocity, noise, out):
+def spot_kernel(parts, slots, lanes, starts, meta, velocity, noise, spots, base, push):
+    in_use = meta[...] >= 0
+    for i in range(3):
+        base[i] = jnp.where(in_use, (1.0 - KICK_RATE) * velocity[i], 0.0)
+        push[i] = jnp.where(in_use, noise[i], 0.0)
+    bricks = starts.shape[0]
+    slot = iota((bricks, slots), 1).astype(F32).astype(BF16)
+    one = jnp.ones((), BF16)
+    zero = jnp.zeros((), BF16)
+    for c in range(parts):
+        begin = jnp.broadcast_to(starts[:, c : c + 1], (bricks, slots))
+        target = quotient(begin, lanes).astype(F32)
+        for i in range(2):
+            at = pl.ds((2 * c + i) * bricks, bricks)
+            spots[at, :] = jnp.where(slot == (target + float(i)).astype(BF16), one, zero)
+
+
+def kick_kernel(
+    parts, returned, spots, meta, starts, base, push, factors, edges,
+    out, new_temp, kicked, filled, left,
+):
+    fill_planes(factors, edges, filled)
+    copies = [pltpu.make_async_copy(filled, new_temp, left.at[3])]
+    copies[0].start()
     bricks, lanes = meta.shape
-    slots = returned.shape[0]
     packed = meta[...]
     lane = iota((bricks, lanes), 1)
     in_use = packed >= 0
     place = quotient(jnp.maximum(packed, 0), parts)
     part = jnp.maximum(packed, 0) - place * parts
-    slot = iota((bricks, slots), 1)
-    spots = []
-    shifts = []
-    for c in range(parts):
-        begin = jnp.broadcast_to(starts[:, c : c + 1], (bricks, lanes))
-        target = quotient(begin[:, 0:1], lanes)
-        shifts.append(begin & (lanes - 1))
-        spots.append(slot == target)
-        spots.append(slot == target + 1)
     values = jnp.concatenate(split(returned[...], 2), axis=1)
-    moved = jnp.dot(
-        jnp.where(jnp.concatenate(spots, axis=0), 1.0, 0.0).astype(BF16),
-        values,
-        preferred_element_type=F32,
-    )
+    moved = jnp.dot(spots[...], values, preferred_element_type=F32)
     moved = moved[:, :lanes] + moved[:, lanes:]
     at = place & (lanes - 1)
     temp = jnp.zeros((bricks, lanes), F32)
     for c in range(parts):
+        shift = jnp.broadcast_to(starts[:, c : c + 1], (bricks, lanes)) & (lanes - 1)
         here = moved[2 * c * bricks : (2 * c + 1) * bricks]
         after = moved[(2 * c + 1) * bricks : (2 * c + 2) * bricks]
-        whole = jnp.where(lane >= shifts[c], here, after)
+        whole = jnp.where(lane >= shift, here, after)
         temp = jnp.where(part == c, jnp.take_along_axis(whole, at, axis=1), temp)
-    root = jnp.sqrt(2.0 * KICK_RATE * temp)
+    root = jnp.where(in_use, jnp.sqrt(2.0 * KICK_RATE * temp), 0.0)
     for i in range(3):
-        out[i] = jnp.where(in_use, (1.0 - KICK_RATE) * velocity[i] + root * noise[i], 0.0)
-
-
-def call(kernel, out_shape, scratch=(), spaces=None, limit=VMEM_LIMIT, cost=None):
+        kicked[i] = base[i] + root * push[i]
+        copies.append(pltpu.make_async_copy(kicked.at[i], out.at[i], left.at[i]))
+        copies[-1].start()
+    for copy in copies:
+        copy.wait()
+
+
+def call(kernel, out_shape, scratch=(), spaces=None, limit=VMEM_LIMIT, cost=None, outs=None):
     extra = {} if cost is None else {"cost_estimate": cost}
     if spaces is not None:
         extra["in_specs"] = [pl.BlockSpec(memory_space=m) for m in spaces]
+    if outs is not None:
+        extra["out_specs"] = tuple(pl.BlockSpec(memory_space=m) for m in outs)
     return pl.pallas_call(
         kernel,
         out_shape=out_shape,
@@ -630,6 +658,14 @@
             for x in (brick_count.reshape(1, bricks), atom_velocity, atom_plane, atom_column)
         )
     )
+    spots, base, push = call(
+        functools.partial(spot_kernel, parts, slabs * rows, lanes),
+        (
+            struct(2 * parts * bricks, slabs * rows, dtype=BF16),
+            struct(*atom_velocity.shape),
+            struct(*atom_noise.shape),
+        ),
+    )(starts, meta, atom_velocity, atom_noise)
     got = lax.all_to_all(send, "gz", split_axis=0, concat_axis=0, tiled=True)
     below = lax.ppermute(electron_temp[-1:], "gz", [(i, i + 1) for i in range(slabs - 1)])
     x_low = lax.ppermute(
@@ -649,7 +685,7 @@
             pltpu.VMEM((parts, (PIECES + 1) * cells // parts, slabs * lanes), F8),
             pltpu.VMEM((parts, width_y, slabs * lanes), F8),
         ),
-    )(got)
+    )(got, spots)
     total, factors = call(
         functools.partial(solve_kernel, dims),
         (struct(5, width_x, width_y), struct(planes - 1, 3, width_x, width_y)),
@@ -690,10 +726,19 @@
             pltpu.VMEM((parts, slabs, 2 * rows + 8 * levels, lanes), F32),
         ),
     )(runs, *pieces, *(phase[i] for i in range(3) for phase in found))
-    new_temp = call(fill_kernel, struct(*dims))(factors, edges)
     returned = lax.all_to_all(reply, "gz", split_axis=0, concat_axis=0, tiled=True)
-    new_velocity = call(functools.partial(kick_kernel, parts), struct(*atom_velocity.shape))(
-        returned.reshape(slabs * rows, lanes), meta, starts, atom_velocity, atom_noise
+    new_velocity, new_temp = call(
+        functools.partial(kick_kernel, parts),
+        (struct(*atom_velocity.shape), struct(*dims)),
+        (
+            pltpu.VMEM(atom_velocity.shape, F32),
+            pltpu.VMEM(dims, F32),
+            pltpu.SemaphoreType.DMA((4,)),
+        ),
+        outs=(pltpu.HBM, pltpu.HBM),
+    )(
+        returned.reshape(slabs * rows, lanes), spots, meta, starts, base, push, factors,
+        edges,
     )
     return (new_temp, new_velocity)
 

time: 52.6 us -> 50.7 us (0.964)
  blocking collectives: 0 us -> 10.7 us
  waiting for transfers between devices: 17.1 us -> 11.5 us
  starting transfers between devices: 19.1 us -> 15.5 us
  Pallas kernels: 15.2 us -> 12.1 us
    all_to_all x0 -> x1, blocking collectives: none -> 10.7 us  [body(): lax.all_to_all(reply, 'gz', split_axis=0, concat_axis=0, tiled=True)]
    all_to_all x1 -> x0, waiting for transfers between devices: 6.59 us -> none  [body(): lax.all_to_all(reply, 'gz', split_axis=0, concat_axis=0, tiled=True)]
    all_to_all x1 -> x0, starting transfers between devices: 3.57 us -> none  [body(): lax.all_to_all(reply, 'gz', split_axis=0, concat_axis=0, tiled=True)]
    ppermute x3, waiting for transfers between devices: 6.18 us -> 7.27 us  [body(): lax.ppermute(total, 'gz', [(i, i ^ 1 << level) for i in range(slabs)])]
    pallas_call x3, Pallas kernels: 5.24 us -> 4.15 us  [body(): call(functools.partial(look_kernel, dims, parts, levels, level), found_sh...]
    pallas_call x1, Pallas kernels: 1.52 us -> 0.52 us  [body(): call(functools.partial(join_kernel, dims, parts, levels), (struct(2, widt...]
    pallas_call x2, Pallas kernels: 1.99 us -> 1.38 us  [the longest x1 1.19 us: body(): call(functools.partial(kick_kernel, parts), (struct(*atom_velocity.shape)...]
  transfers between devices with their start and end apart: 8 -> 7, of which waited for: 5 -> 4; matrix products, arithmetic and copies ran while one was open for 0% -> 0% of each run, Pallas kernels for 16% -> 12%
where the time goes in v5:
time: 50.7 us
  starting transfers between devices  15.5 us (31%)
  Pallas kernels  12.1 us (24%)
  waiting for transfers between devices  11.5 us (23%)
  blocking collectives  10.7 us (21%)
  between operations  0.78 us (2%)
    all_to_all x1, blocking collectives, body(): lax.all_to_all(reply, 'gz', split_axis=0, concat_axis=0, tiled=True)  10.7 us
    all_to_all x1, starting transfers between devices, body(): got = lax.all_to_all(send, 'gz', split_axis=0, concat_axis=0, tiled=True)  7.4 us
    ppermute x3, waiting for transfers between devices, body(): lax.ppermute(total, 'gz', [(i, i ^ 1 << level) for i in range(slabs)])  7.27 us
    all_to_all x1, waiting for transfers between devices, body(): got = lax.all_to_all(send, 'gz', split_axis=0, concat_axis=0, tiled=True)  4.18 us
    pallas_call x3, Pallas kernels, body(): call(functools.partial(look_kernel, dims, parts, levels, level), found_sh...  4.15 us
    ppermute x1, starting transfers between devices, body(): lax.ppermute(electron_temp[-1:], 'gz', [(i, i + 1) for i in range(slabs -...  3.92 us
    ppermute x3, starting transfers between devices, body(): lax.ppermute(total, 'gz', [(i, i ^ 1 << level) for i in range(slabs)])  3.65 us
    pallas_call x1, Pallas kernels, body(): route_call(dims, slabs, rows, parts, atom_velocity.shape, atom_plane.shape)  3.53 us
  transfers between devices with their start and end apart: 7, of which 4 were waited for; matrix products, arithmetic and copies ran while one was open for 0% of the time, Pallas kernels for 12%

profile of v5, /device:TPU:0, one launch (start us, length us, event | category | flops | bytes accessed | tf_op | source)
XLA Modules:
  0.0 50.7 jit_solution(2779402281655605810)
XLA Ops:
  0.6 3.5 %shard_map.77 = (f32[8,2,32,128]{3,2,1,0:T(8,128)}, s32[128,128]{1,0:T(8,128)S(1)}, s32[128,128]{1,0:T(8,128)S(1)}) custom-call(s32[1,128]{1,0:T(1,128)} %bitcast.3, f32[3,128,128]{2,1,0:T(8,128)} %velocity.1, s32[128,128]{1,0:T(8,128)} %plane_hbm.1, s32[128,128]{1,0:T(8,128)} %column_hbm.1), custom_call_target="tpu_custom_call" | custom-call | tf_op jit(solution)/shard_map/pallas_call | solution.py:653
  4.2 0.0 copy-start.1
  4.2 0.0 copy-start
  4.2 7.4 %all-to-all-start = ((f32[8,2,32,128]{3,2,1,0:T(8,128)}), f32[8,2,32,128]{3,2,1,0:T(8,128)S(1)}, u32[]{:S(2)}, u32[]{:S(2)}) async-start(f32[8,2,32,128]{3,2,1,0:T(8,128)} %get-tuple-element.27), calls=%async_computation | async-start | bytes 524288 | tf_op jit(solution)/shard_map/all_to_all | solution.py:669
  11.6 3.9 %collective-permute-start = (f32[1,16,256]{2,1,0:T(8,128)S(1)}, f32[1,16,256]{2,1,0:T(8,128)S(1)}, u32[]{:S(2)}, u32[]{:S(2)}) collective-permute-start(f32[1,16,256]{2,1,0:T(8,128)S(1)} %slice.9), channel_id=1, source_target_pairs={{0,4},{4,8},{8,12},{12,16},{16,20},{20,24},{24,28},{1,5},{5,9},{9,... | collective-permute-start | bytes 49160 | tf_op jit(solution)/shard_map/ppermute | solution.py:670
  15.6 0.2 collective-permute-start.2
  15.7 0.4 collective-permute-start.1
  16.1 0.2 shard_map.78
  16.3 4.2 %all-to-all-done.got = f32[8,2,32,128]{3,2,1,0:T(8,128)S(1)} async-done(((f32[8,2,32,128]{3,2,1,0:T(8,128)}), f32[8,2,32,128]{3,2,1,0:T(8,128)S(1)}, u32[]{:S(2)}, u32[]{:S(2)}) %all-to-all-start) | async-done | bytes 262176 | tf_op jit(solution)/shard_map/all_to_all | solution.py:669
  20.5 1.8 %shard_map.79 = (f32[4,2,256,128]{3,2,1,0:T(8,128)S(1)}, f32[132,8,128]{2,1,0:T(8,128)S(1)}, s32[8,128]{1,0:T(8,128)S(1)}) custom-call(f32[8,2,32,128]{3,2,1,0:T(8,128)S(1)} %all-to-all-done.got, bf16[1024,256]{1,0:T(8,128)(2,1)S(1)} %get-tuple-element.30._.spots), custom_call_target="tpu_custom_call" | custom-call | tf_op jit(solution)/shard_map/pallas_call | solution.py:677
  22.4 0.0 collective-permute-done.1.x_low
  22.4 0.7 %shard_map.80 = (f32[5,16,256]{2,1,0:T(8,128)S(1)}, f32[15,3,16,256]{3,2,1,0:T(8,128)S(1)}) custom-call(f32[4,2,256,128]{3,2,1,0:T(8,128)S(1)} %get-tuple-element.32.totals, f32[16,16,256]{2,1,0:T(8,128)S(1)} %copy-done.1, f32[1,16,256]{2,1,0:T(8,128)S(1)} %collective-permute-done.below, f32[16,1,256]{2,1,0:T(1,128)S(1)} %collective-permute-done.1.x_low, ...), custom_call_target="tpu_custom_call" | custom-call | tf_op jit(solution)/shard_map/pallas_call | solution.py:689
  23.1 2.9 %collective-permute-start.3 = (f32[5,16,256]{2,1,0:T(8,128)S(1)}, f32[5,16,256]{2,1,0:T(8,128)S(1)}, u32[]{:S(2)}, u32[]{:S(2)}) collective-permute-start(f32[5,16,256]{2,1,0:T(8,128)S(1)} %get-tuple-element.33.mine.refs_0_), channel_id=1, source_target_pairs={{0,4},{4,0},{8,12},{12,8},{16,20},{20,16},{24,28},{28,24},{1,5},{5... | collective-permute-start | bytes 245768 | tf_op jit(solution)/shard_map/ppermute | solution.py:703
  25.9 1.7 %shard_map.81 = (f32[3,44,8,128]{3,2,1,0:T(8,128)S(1)}, f32[44,8,128]{2,1,0:T(8,128)S(1)}, s32[44,8,128]{2,1,0:T(8,128)S(1)}, f8e4m3fn[4,576,256]{2,1,0:T(32,128)(4,1)S(1)}) custom-call(f32[132,8,128]{2,1,0:T(8,128)S(1)} %get-tuple-element.34.codes, s32[8,128]{1,0:T(8,128)S(1)} %get-tuple-element.31.runs.runs_vmem, ...), custom_call_target="tpu_custom_call" | custom-call | flops 2000000000 | bytes 10000000 | tf_op jit(solution)/shard_map/pallas_call | solution.py:704
  27.7 0.7 %collective-permute-done.3.other.refs_1_ = f32[5,16,256]{2,1,0:T(8,128)S(1)} collective-permute-done((f32[5,16,256]{2,1,0:T(8,128)S(1)}, f32[5,16,256]{2,1,0:T(8,128)S(1)}, u32[]{:S(2)}, u32[]{:S(2)}) %collective-permute-start.3) | collective-permute-done | bytes 81952 | tf_op jit(solution)/shard_map/ppermute | solution.py:703
  28.4 0.3 collective-permute-start.4
  28.7 1.2 %shard_map.83 = (f32[3,44,8,128]{3,2,1,0:T(8,128)S(1)}, f32[44,8,128]{2,1,0:T(8,128)S(1)}, s32[44,8,128]{2,1,0:T(8,128)S(1)}) custom-call(f32[132,8,128]{2,1,0:T(8,128)S(1)} %get-tuple-element.34.codes, s32[8,128]{1,0:T(8,128)S(1)} %get-tuple-element.31.runs.runs_vmem, f8e4m3fn[4,576,256]{2,1,0:T(32,128)(4,1)S(1)} %get-tuple-element.37.refs_0_, ...), custom_call_target="tpu_custom_call" | custom-call | flops 2000000000 | bytes 10000000 | tf_op jit(solution)/shard_map/pallas_call | solution.py:704
  29.9 3.3 %collective-permute-done.4.other.refs_2_ = f32[5,16,256]{2,1,0:T(8,128)S(1)} collective-permute-done((f32[5,16,256]{2,1,0:T(8,128)S(1)}, f32[5,16,256]{2,1,0:T(8,128)S(1)}, u32[]{:S(2)}, u32[]{:S(2)}) %collective-permute-start.4) | collective-permute-done | bytes 81952 | tf_op jit(solution)/shard_map/ppermute | solution.py:703
  33.3 0.4 collective-permute-start.5
  33.7 1.2 %shard_map.85 = (f32[3,44,8,128]{3,2,1,0:T(8,128)S(1)}, f32[44,8,128]{2,1,0:T(8,128)S(1)}, s32[44,8,128]{2,1,0:T(8,128)S(1)}) custom-call(f32[132,8,128]{2,1,0:T(8,128)S(1)} %get-tuple-element.34.codes, s32[8,128]{1,0:T(8,128)S(1)} %get-tuple-element.31.runs.runs_vmem, f8e4m3fn[4,576,256]{2,1,0:T(32,128)(4,1)S(1)} %get-tuple-element.37.refs_0_, ...), custom_call_target="tpu_custom_call" | custom-call | flops 2000000000 | bytes 10000000 | tf_op jit(solution)/shard_map/pallas_call | solution.py:704
  34.9 3.3 %collective-permute-done.5.refs_3_ = f32[2,16,256]{2,1,0:T(8,128)S(1)} collective-permute-done((f32[2,16,256]{2,1,0:T(8,128)S(1)}, f32[2,16,256]{2,1,0:T(8,128)S(1)}, u32[]{:S(2)}, u32[]{:S(2)}) %collective-permute-start.5) | collective-permute-done | bytes 32800 | tf_op jit(solution)/shard_map/ppermute | solution.py:703
  38.2 0.5 %shard_map.86 = (f32[2,16,256]{2,1,0:T(8,128)S(1)}, f32[8,32,128]{2,1,0:T(8,128)S(1)}) custom-call(s32[8,128]{1,0:T(8,128)S(1)} %get-tuple-element.31.runs.runs_vmem, f32[5,16,256]{2,1,0:T(8,128)S(1)} %get-tuple-element.33.mine.refs_0_, f32[5,16,256]{2,1,0:T(8,128)S(1)} %collective-permute-done.3.other.refs_1_, ...), custom_call_target="tpu_custom_call" | custom-call | tf_op jit(solution)/shard_map/pallas_call | solution.py:721
  38.7 10.7 %all_to_all.10 = f32[8,32,128]{2,1,0:T(8,128)S(1)} all-to-all(f32[8,32,128]{2,1,0:T(8,128)S(1)} %get-tuple-element.46), channel_id=1, replica_groups=mesh['gz'=8,'gx'=4] {'gz'}, dimensions={0} | all-to-all | bytes 262144 | tf_op jit(solution)/shard_map/all_to_all | solution.py:729
  49.5 1.2 %shard_map.87 = (f32[3,128,128]{2,1,0:T(8,128)}, f32[16,16,256]{2,1,0:T(8,128)}) custom-call(f32[256,128]{1,0:T(8,128)S(1)} %bitcast.2, bf16[1024,256]{1,0:T(8,128)(2,1)S(1)} %get-tuple-element.30._.spots, s32[128,128]{1,0:T(8,128)S(1)} %get-tuple-element.29.meta, s32[128,128]{1,0:T(8,128)S(1)} %get-tuple-element.28.starts, ...), custom_call_target="tpu_custom_call" | custom-call | tf_op jit(solution)/shard_map/pallas_call | solution.py:730
  (10 shorter events, 0.1 us)
Async XLA Ops:
  0.6 15.5 %copy-start.2 = (f32[3,128,128]{2,1,0:T(8,128)S(1)}, f32[3,128,128]{2,1,0:T(8,128)}, u32[]{:S(2)}) copy-start(f32[3,128,128]{2,1,0:T(8,128)} %noise.1) | copy-start | bytes 589828
  4.2 7.4 %copy-start.1 = (f32[16,16,256]{2,1,0:T(8,128)S(1)}, f32[16,16,256]{2,1,0:T(8,128)}, u32[]{:S(2)}) copy-start(f32[16,16,256]{2,1,0:T(8,128)} %temp.1) | copy-start | bytes 786436
  4.2 12.0 %copy-start = (f32[3,128,128]{2,1,0:T(8,128)S(1)}, f32[3,128,128]{2,1,0:T(8,128)}, u32[]{:S(2)}) copy-start(f32[3,128,128]{2,1,0:T(8,128)} %velocity.1) | copy-start | bytes 589828
  4.2 16.3 %all-to-all-start = ((f32[8,2,32,128]{3,2,1,0:T(8,128)}), f32[8,2,32,128]{3,2,1,0:T(8,128)S(1)}, u32[]{:S(2)}, u32[]{:S(2)}) async-start(f32[8,2,32,128]{3,2,1,0:T(8,128)} %get-tuple-element.27), calls=%async_computation | async-start | bytes 524288 | tf_op jit(solution)/shard_map/all_to_all | solution.py:669
  11.6 10.8 %collective-permute-start = (f32[1,16,256]{2,1,0:T(8,128)S(1)}, f32[1,16,256]{2,1,0:T(8,128)S(1)}, u32[]{:S(2)}, u32[]{:S(2)}) collective-permute-start(f32[1,16,256]{2,1,0:T(8,128)S(1)} %slice.9), channel_id=1, source_target_pairs={{0,4},{4,8},{8,12},{12,16},{16,20},{20,24},{24,28},{1,5},{5,9},{9,... | collective-permute-start | bytes 49160 | tf_op jit(solution)/shard_map/ppermute | solution.py:670
  15.6 6.8 %collective-permute-start.2 = (f32[16,1,256]{2,1,0:T(1,128)S(1)}, f32[16,1,256]{2,1,0:T(1,128)S(1)}, u32[]{:S(2)}, u32[]{:S(2)}) collective-permute-start(f32[16,1,256]{2,1,0:T(1,128)S(1)} %get-tuple-element.52), channel_id=1, source_target_pairs={{1,0},{2,1},{3,2},{0,3},{5,4},{6,5},{7,6},{4,7},{9,8},{10,9},{11,1... | collective-permute-start | bytes 49160 | tf_op jit(solution)/shard_map/ppermute | solution.py:674
  15.7 6.6 %collective-permute-start.1 = (f32[16,1,256]{2,1,0:T(1,128)S(1)}, f32[16,1,256]{2,1,0:T(1,128)S(1)}, u32[]{:S(2)}, u32[]{:S(2)}) collective-permute-start(f32[16,1,256]{2,1,0:T(1,128)S(1)} %get-tuple-element.53), channel_id=1, source_target_pairs={{0,1},{1,2},{2,3},{3,0},{4,5},{5,6},{6,7},{7,4},{8,9},{9,10},{10,1... | collective-permute-start | bytes 49160 | tf_op jit(solution)/shard_map/ppermute | solution.py:671
  23.1 5.3 %collective-permute-start.3 = (f32[5,16,256]{2,1,0:T(8,128)S(1)}, f32[5,16,256]{2,1,0:T(8,128)S(1)}, u32[]{:S(2)}, u32[]{:S(2)}) collective-permute-start(f32[5,16,256]{2,1,0:T(8,128)S(1)} %get-tuple-element.33.mine.refs_0_), channel_id=1, source_target_pairs={{0,4},{4,0},{8,12},{12,8},{16,20},{20,16},{24,28},{28,24},{1,5},{5... | collective-permute-start | bytes 245768 | tf_op jit(solution)/shard_map/ppermute | solution.py:703
  28.4 4.9 %collective-permute-start.4 = (f32[5,16,256]{2,1,0:T(8,128)S(1)}, f32[5,16,256]{2,1,0:T(8,128)S(1)}, u32[]{:S(2)}, u32[]{:S(2)}) collective-permute-start(f32[5,16,256]{2,1,0:T(8,128)S(1)} %shard_map.82.refs_1_.mine), channel_id=1, source_target_pairs={{0,8},{4,12},{8,0},{12,4},{16,24},{20,28},{24,16},{28,20},{1,9},{5... | collective-permute-start | bytes 245768 | tf_op jit(solution)/shard_map/ppermute | solution.py:703
  33.3 4.9 %collective-permute-start.5 = (f32[2,16,256]{2,1,0:T(8,128)S(1)}, f32[2,16,256]{2,1,0:T(8,128)S(1)}, u32[]{:S(2)}, u32[]{:S(2)}) collective-permute-start(f32[2,16,256]{2,1,0:T(8,128)S(1)} %shard_map.84.refs_1_), channel_id=1, source_target_pairs={{0,16},{4,20},{8,24},{12,28},{16,0},{20,4},{24,8},{28,12},{1,17},{... | collective-permute-start | bytes 98312 | tf_op jit(solution)/shard_map/ppermute | solution.py:703

commit v6 on v5

--- a/solution.py
+++ b/solution.py
@@ -180,12 +180,16 @@
         base = jnp.where(lane_f >= earlier[c], earlier[c], base)
     wanted = lane - base.astype(jnp.int32)
     found = jnp.zeros((bricks, lanes), jnp.int32)
-    step = lanes // 2
-    while step:
-        at = jnp.take_along_axis(packed, found + (step - 1), axis=1)
-        at = lax.shift_right_logical(at, run) & 255
-        found = jnp.where(at <= wanted, found + step, found)
-        step //= 2
+    step = lanes
+    while step > 1:
+        ways = 4 if step >= 4 else 2
+        step //= ways
+        gain = jnp.zeros((bricks, lanes), jnp.int32)
+        for way in range(1, ways):
+            at = jnp.take_along_axis(packed, found + (way * step - 1), axis=1)
+            at = lax.shift_right_logical(at, run) & 255
+            gain = jnp.where(at <= wanted, way * step, gain)
+        found = found + gain
     kinetic = jnp.take_along_axis(kinetic, found, axis=1)
     code = jnp.take_along_axis(code, found, axis=1)
     zero = jnp.zeros((bricks, lanes), BF16)
@@ -299,10 +303,11 @@
             added = lax.dot_general(
                 lhs[c], rhs[c], (((1,), (1,)), ((), ())), preferred_element_type=F32
             )
-            for i in range(PIECES + 1):
+            pieces = [added[i * part_rows : (i + 1) * part_rows] for i in range(PIECES + 1)]
+            for i, value in enumerate((join_small(pieces[:PIECES]), pieces[PIECES])):
                 for h in range(width_y // lanes):
-                    totals[i, h, pl.ds(c * part_rows, part_rows), :] += added[
-                        i * part_rows : (i + 1) * part_rows, h * lanes : (h + 1) * lanes
+                    totals[i, h, pl.ds(c * part_rows, part_rows), :] += value[
+                        :, h * lanes : (h + 1) * lanes
                     ]
         return carry
 
@@ -327,10 +332,9 @@
         at = pl.ds(z, width_x, stride=planes)
         sums = [
             jnp.concatenate([totals[i, h, at, :] for h in range(width_y // lanes)], axis=1)
-            for i in range(PIECES + 1)
+            for i in range(2)
         ]
-        energy = join_small(sums[:PIECES])
-        count = sums[PIECES]
+        energy, count = sums
         return here + COUPLE * count, here * here + lateral + COUPLE * TWO_THIRDS * energy
 
     start = temp[0]
@@ -677,7 +681,7 @@
     totals, codes, runs = call(
         functools.partial(bin_kernel, dims, parts),
         (
-            struct(PIECES + 1, width_y // lanes, cells, lanes),
+            struct(2, width_y // lanes, cells, lanes),
             struct(parts * (rows + 1), slabs, lanes),
             struct(slabs, lanes, dtype=jnp.int32),
         ),

time: 50.7 us -> 51 us (level)
  waiting for transfers between devices: 11.5 us -> 8.31 us
  starting transfers between devices: 15.5 us -> 17.7 us
  blocking collectives: 10.7 us -> 12 us
    ppermute x3, waiting for transfers between devices: 7.27 us -> 4.14 us  [body(): lax.ppermute(total, 'gz', [(i, i ^ 1 << level) for i in range(slabs)])]
    ppermute x3, starting transfers between devices: 3.65 us -> 5.79 us  [body(): lax.ppermute(total, 'gz', [(i, i ^ 1 << level) for i in range(slabs)])]
    all_to_all x1, blocking collectives: 10.7 us -> 12 us  [body(): lax.all_to_all(reply, 'gz', split_axis=0, concat_axis=0, tiled=True)]
where the time goes in v6:
time: 51 us; the launch traced here: 50.8 us
  starting transfers between devices  17.7 us (35%)
  Pallas kernels  12 us (24%)
  blocking collectives  12 us (24%)
  waiting for transfers between devices  8.31 us (16%)
  between operations  0.78 us (2%)
    all_to_all x1, blocking collectives, body(): lax.all_to_all(reply, 'gz', split_axis=0, concat_axis=0, tiled=True)  12 us
    all_to_all x1, starting transfers between devices, body(): got = lax.all_to_all(send, 'gz', split_axis=0, concat_axis=0, tiled=True)  7.4 us
    ppermute x3, starting transfers between devices, body(): lax.ppermute(total, 'gz', [(i, i ^ 1 << level) for i in range(slabs)])  5.79 us
    all_to_all x1, waiting for transfers between devices, body(): got = lax.all_to_all(send, 'gz', split_axis=0, concat_axis=0, tiled=True)  4.16 us
    pallas_call x3, Pallas kernels, body(): call(functools.partial(look_kernel, dims, parts, levels, level), found_sh...  4.15 us
    ppermute x3, waiting for transfers between devices, body(): lax.ppermute(total, 'gz', [(i, i ^ 1 << level) for i in range(slabs)])  4.14 us
    ppermute x1, starting transfers between devices, body(): lax.ppermute(electron_temp[-1:], 'gz', [(i, i + 1) for i in range(slabs -...  3.92 us
    pallas_call x1, Pallas kernels, body(): route_call(dims, slabs, rows, parts, atom_velocity.shape, atom_plane.shape)  3.54 us
  transfers between devices with their start and end apart: 7, of which 4 were waited for; matrix products, arithmetic and copies ran while one was open for 0% of the time, Pallas kernels for 12%

profile of v6, /device:TPU:0, one launch (start us, length us, event | category | flops | bytes accessed | tf_op | source)
XLA Modules:
  0.0 50.8 jit_solution(14349127170220602865)
XLA Ops:
  0.6 3.5 %shard_map.77 = (f32[8,2,32,128]{3,2,1,0:T(8,128)}, s32[128,128]{1,0:T(8,128)S(1)}, s32[128,128]{1,0:T(8,128)S(1)}) custom-call(s32[1,128]{1,0:T(1,128)} %bitcast.3, f32[3,128,128]{2,1,0:T(8,128)} %velocity.1, s32[128,128]{1,0:T(8,128)} %plane_hbm.1, s32[128,128]{1,0:T(8,128)} %column_hbm.1), custom_call_target="tpu_custom_call" | custom-call | tf_op jit(solution)/shard_map/pallas_call | solution.py:657
  4.2 0.0 copy-start.1
  4.2 0.0 copy-start
  4.2 7.4 %all-to-all-start = ((f32[8,2,32,128]{3,2,1,0:T(8,128)}), f32[8,2,32,128]{3,2,1,0:T(8,128)S(1)}, u32[]{:S(2)}, u32[]{:S(2)}) async-start(f32[8,2,32,128]{3,2,1,0:T(8,128)} %get-tuple-element.27), calls=%async_computation | async-start | bytes 524288 | tf_op jit(solution)/shard_map/all_to_all | solution.py:673
  11.6 3.9 %collective-permute-start = (f32[1,16,256]{2,1,0:T(8,128)S(1)}, f32[1,16,256]{2,1,0:T(8,128)S(1)}, u32[]{:S(2)}, u32[]{:S(2)}) collective-permute-start(f32[1,16,256]{2,1,0:T(8,128)S(1)} %slice.9), channel_id=1, source_target_pairs={{0,4},{4,8},{8,12},{12,16},{16,20},{20,24},{24,28},{1,5},{5,9},{9,... | collective-permute-start | bytes 49160 | tf_op jit(solution)/shard_map/ppermute | solution.py:674
  15.6 0.2 collective-permute-start.2
  15.8 0.4 collective-permute-start.1
  16.2 0.2 shard_map.78
  16.4 4.2 %all-to-all-done.got = f32[8,2,32,128]{3,2,1,0:T(8,128)S(1)} async-done(((f32[8,2,32,128]{3,2,1,0:T(8,128)}), f32[8,2,32,128]{3,2,1,0:T(8,128)S(1)}, u32[]{:S(2)}, u32[]{:S(2)}) %all-to-all-start) | async-done | bytes 262176 | tf_op jit(solution)/shard_map/all_to_all | solution.py:673
  20.5 1.9 %shard_map.79 = (f32[2,2,256,128]{3,2,1,0:T(8,128)S(1)}, f32[132,8,128]{2,1,0:T(8,128)S(1)}, s32[8,128]{1,0:T(8,128)S(1)}) custom-call(f32[8,2,32,128]{3,2,1,0:T(8,128)S(1)} %all-to-all-done.got, bf16[1024,256]{1,0:T(8,128)(2,1)S(1)} %get-tuple-element.30._.spots), custom_call_target="tpu_custom_call" | custom-call | tf_op jit(solution)/shard_map/pallas_call | solution.py:681
  22.4 0.0 collective-permute-done.2.x_high
  22.5 0.4 shard_map.80
  22.9 1.5 %collective-permute-start.3 = (f32[5,16,256]{2,1,0:T(8,128)S(1)}, f32[5,16,256]{2,1,0:T(8,128)S(1)}, u32[]{:S(2)}, u32[]{:S(2)}) collective-permute-start(f32[5,16,256]{2,1,0:T(8,128)S(1)} %get-tuple-element.33.mine.refs_0_), channel_id=1, source_target_pairs={{0,4},{4,0},{8,12},{12,8},{16,20},{20,16},{24,28},{28,24},{1,5},{5... | collective-permute-start | bytes 245768 | tf_op jit(solution)/shard_map/ppermute | solution.py:707
  24.3 1.7 %shard_map.81 = (f32[3,44,8,128]{3,2,1,0:T(8,128)S(1)}, f32[44,8,128]{2,1,0:T(8,128)S(1)}, s32[44,8,128]{2,1,0:T(8,128)S(1)}, f8e4m3fn[4,576,256]{2,1,0:T(32,128)(4,1)S(1)}) custom-call(f32[132,8,128]{2,1,0:T(8,128)S(1)} %get-tuple-element.34.codes, s32[8,128]{1,0:T(8,128)S(1)} %get-tuple-element.31.runs.runs_vmem, ...), custom_call_target="tpu_custom_call" | custom-call | flops 2000000000 | bytes 10000000 | tf_op jit(solution)/shard_map/pallas_call | solution.py:708
  26.1 1.3 %collective-permute-done.3.other.refs_1_ = f32[5,16,256]{2,1,0:T(8,128)S(1)} collective-permute-done((f32[5,16,256]{2,1,0:T(8,128)S(1)}, f32[5,16,256]{2,1,0:T(8,128)S(1)}, u32[]{:S(2)}, u32[]{:S(2)}) %collective-permute-start.3) | collective-permute-done | bytes 81952 | tf_op jit(solution)/shard_map/ppermute | solution.py:707
  27.4 1.1 %collective-permute-start.4 = (f32[5,16,256]{2,1,0:T(8,128)S(1)}, f32[5,16,256]{2,1,0:T(8,128)S(1)}, u32[]{:S(2)}, u32[]{:S(2)}) collective-permute-start(f32[5,16,256]{2,1,0:T(8,128)S(1)} %shard_map.82.refs_1_.mine), channel_id=1, source_target_pairs={{0,8},{4,12},{8,0},{12,4},{16,24},{20,28},{24,16},{28,20},{1,9},{5... | collective-permute-start | bytes 245768 | tf_op jit(solution)/shard_map/ppermute | solution.py:707
  28.5 1.2 %shard_map.83 = (f32[3,44,8,128]{3,2,1,0:T(8,128)S(1)}, f32[44,8,128]{2,1,0:T(8,128)S(1)}, s32[44,8,128]{2,1,0:T(8,128)S(1)}) custom-call(f32[132,8,128]{2,1,0:T(8,128)S(1)} %get-tuple-element.34.codes, s32[8,128]{1,0:T(8,128)S(1)} %get-tuple-element.31.runs.runs_vmem, f8e4m3fn[4,576,256]{2,1,0:T(32,128)(4,1)S(1)} %get-tuple-element.37.refs_0_, ...), custom_call_target="tpu_custom_call" | custom-call | flops 2000000000 | bytes 10000000 | tf_op jit(solution)/shard_map/pallas_call | solution.py:708
  29.7 2.2 %collective-permute-done.4.other.refs_2_ = f32[5,16,256]{2,1,0:T(8,128)S(1)} collective-permute-done((f32[5,16,256]{2,1,0:T(8,128)S(1)}, f32[5,16,256]{2,1,0:T(8,128)S(1)}, u32[]{:S(2)}, u32[]{:S(2)}) %collective-permute-start.4) | collective-permute-done | bytes 81952 | tf_op jit(solution)/shard_map/ppermute | solution.py:707
  32.0 3.2 %collective-permute-start.5 = (f32[2,16,256]{2,1,0:T(8,128)S(1)}, f32[2,16,256]{2,1,0:T(8,128)S(1)}, u32[]{:S(2)}, u32[]{:S(2)}) collective-permute-start(f32[2,16,256]{2,1,0:T(8,128)S(1)} %shard_map.84.refs_1_), channel_id=1, source_target_pairs={{0,16},{4,20},{8,24},{12,28},{16,0},{20,4},{24,8},{28,12},{1,17},{... | collective-permute-start | bytes 98312 | tf_op jit(solution)/shard_map/ppermute | solution.py:707
  35.1 1.2 %shard_map.85 = (f32[3,44,8,128]{3,2,1,0:T(8,128)S(1)}, f32[44,8,128]{2,1,0:T(8,128)S(1)}, s32[44,8,128]{2,1,0:T(8,128)S(1)}) custom-call(f32[132,8,128]{2,1,0:T(8,128)S(1)} %get-tuple-element.34.codes, s32[8,128]{1,0:T(8,128)S(1)} %get-tuple-element.31.runs.runs_vmem, f8e4m3fn[4,576,256]{2,1,0:T(32,128)(4,1)S(1)} %get-tuple-element.37.refs_0_, ...), custom_call_target="tpu_custom_call" | custom-call | flops 2000000000 | bytes 10000000 | tf_op jit(solution)/shard_map/pallas_call | solution.py:708
  36.3 0.7 %collective-permute-done.5.refs_3_ = f32[2,16,256]{2,1,0:T(8,128)S(1)} collective-permute-done((f32[2,16,256]{2,1,0:T(8,128)S(1)}, f32[2,16,256]{2,1,0:T(8,128)S(1)}, u32[]{:S(2)}, u32[]{:S(2)}) %collective-permute-start.5) | collective-permute-done | bytes 32800 | tf_op jit(solution)/shard_map/ppermute | solution.py:707
  37.0 0.5 %shard_map.86 = (f32[2,16,256]{2,1,0:T(8,128)S(1)}, f32[8,32,128]{2,1,0:T(8,128)S(1)}) custom-call(s32[8,128]{1,0:T(8,128)S(1)} %get-tuple-element.31.runs.runs_vmem, f32[5,16,256]{2,1,0:T(8,128)S(1)} %get-tuple-element.33.mine.refs_0_, f32[5,16,256]{2,1,0:T(8,128)S(1)} %collective-permute-done.3.other.refs_1_, ...), custom_call_target="tpu_custom_call" | custom-call | tf_op jit(solution)/shard_map/pallas_call | solution.py:725
  37.6 12.0 %all_to_all.10 = f32[8,32,128]{2,1,0:T(8,128)S(1)} all-to-all(f32[8,32,128]{2,1,0:T(8,128)S(1)} %get-tuple-element.46), channel_id=1, replica_groups=mesh['gz'=8,'gx'=4] {'gz'}, dimensions={0} | all-to-all | bytes 262144 | tf_op jit(solution)/shard_map/all_to_all | solution.py:733
  49.6 1.2 %shard_map.87 = (f32[3,128,128]{2,1,0:T(8,128)}, f32[16,16,256]{2,1,0:T(8,128)}) custom-call(f32[256,128]{1,0:T(8,128)S(1)} %bitcast.2, bf16[1024,256]{1,0:T(8,128)(2,1)S(1)} %get-tuple-element.30._.spots, s32[128,128]{1,0:T(8,128)S(1)} %get-tuple-element.29.meta, s32[128,128]{1,0:T(8,128)S(1)} %get-tuple-element.28.starts, ...), custom_call_target="tpu_custom_call" | custom-call | tf_op jit(solution)/shard_map/pallas_call | solution.py:734
  (10 shorter events, 0.1 us)
Async XLA Ops:
  0.6 15.5 %copy-start.2 = (f32[3,128,128]{2,1,0:T(8,128)S(1)}, f32[3,128,128]{2,1,0:T(8,128)}, u32[]{:S(2)}) copy-start(f32[3,128,128]{2,1,0:T(8,128)} %noise.1) | copy-start | bytes 589828
  4.2 7.4 %copy-start.1 = (f32[16,16,256]{2,1,0:T(8,128)S(1)}, f32[16,16,256]{2,1,0:T(8,128)}, u32[]{:S(2)}) copy-start(f32[16,16,256]{2,1,0:T(8,128)} %temp.1) | copy-start | bytes 786436
  4.2 12.0 %copy-start = (f32[3,128,128]{2,1,0:T(8,128)S(1)}, f32[3,128,128]{2,1,0:T(8,128)}, u32[]{:S(2)}) copy-start(f32[3,128,128]{2,1,0:T(8,128)} %velocity.1) | copy-start | bytes 589828
  4.2 16.3 %all-to-all-start = ((f32[8,2,32,128]{3,2,1,0:T(8,128)}), f32[8,2,32,128]{3,2,1,0:T(8,128)S(1)}, u32[]{:S(2)}, u32[]{:S(2)}) async-start(f32[8,2,32,128]{3,2,1,0:T(8,128)} %get-tuple-element.27), calls=%async_computation | async-start | bytes 524288 | tf_op jit(solution)/shard_map/all_to_all | solution.py:673
  11.6 10.8 %collective-permute-start = (f32[1,16,256]{2,1,0:T(8,128)S(1)}, f32[1,16,256]{2,1,0:T(8,128)S(1)}, u32[]{:S(2)}, u32[]{:S(2)}) collective-permute-start(f32[1,16,256]{2,1,0:T(8,128)S(1)} %slice.9), channel_id=1, source_target_pairs={{0,4},{4,8},{8,12},{12,16},{16,20},{20,24},{24,28},{1,5},{5,9},{9,... | collective-permute-start | bytes 49160 | tf_op jit(solution)/shard_map/ppermute | solution.py:674
  15.6 6.9 %collective-permute-start.2 = (f32[16,1,256]{2,1,0:T(1,128)S(1)}, f32[16,1,256]{2,1,0:T(1,128)S(1)}, u32[]{:S(2)}, u32[]{:S(2)}) collective-permute-start(f32[16,1,256]{2,1,0:T(1,128)S(1)} %get-tuple-element.52), channel_id=1, source_target_pairs={{1,0},{2,1},{3,2},{0,3},{5,4},{6,5},{7,6},{4,7},{9,8},{10,9},{11,1... | collective-permute-start | bytes 49160 | tf_op jit(solution)/shard_map/ppermute | solution.py:678
  15.8 6.7 %collective-permute-start.1 = (f32[16,1,256]{2,1,0:T(1,128)S(1)}, f32[16,1,256]{2,1,0:T(1,128)S(1)}, u32[]{:S(2)}, u32[]{:S(2)}) collective-permute-start(f32[16,1,256]{2,1,0:T(1,128)S(1)} %get-tuple-element.53), channel_id=1, source_target_pairs={{0,1},{1,2},{2,3},{3,0},{4,5},{5,6},{6,7},{7,4},{8,9},{9,10},{10,1... | collective-permute-start | bytes 49160 | tf_op jit(solution)/shard_map/ppermute | solution.py:675
  22.9 4.5 %collective-permute-start.3 = (f32[5,16,256]{2,1,0:T(8,128)S(1)}, f32[5,16,256]{2,1,0:T(8,128)S(1)}, u32[]{:S(2)}, u32[]{:S(2)}) collective-permute-start(f32[5,16,256]{2,1,0:T(8,128)S(1)} %get-tuple-element.33.mine.refs_0_), channel_id=1, source_target_pairs={{0,4},{4,0},{8,12},{12,8},{16,20},{20,16},{24,28},{28,24},{1,5},{5... | collective-permute-start | bytes 245768 | tf_op jit(solution)/shard_map/ppermute | solution.py:707
  27.4 4.5 %collective-permute-start.4 = (f32[5,16,256]{2,1,0:T(8,128)S(1)}, f32[5,16,256]{2,1,0:T(8,128)S(1)}, u32[]{:S(2)}, u32[]{:S(2)}) collective-permute-start(f32[5,16,256]{2,1,0:T(8,128)S(1)} %shard_map.82.refs_1_.mine), channel_id=1, source_target_pairs={{0,8},{4,12},{8,0},{12,4},{16,24},{20,28},{24,16},{28,20},{1,9},{5... | collective-permute-start | bytes 245768 | tf_op jit(solution)/shard_map/ppermute | solution.py:707
  32.0 5.1 %collective-permute-start.5 = (f32[2,16,256]{2,1,0:T(8,128)S(1)}, f32[2,16,256]{2,1,0:T(8,128)S(1)}, u32[]{:S(2)}, u32[]{:S(2)}) collective-permute-start(f32[2,16,256]{2,1,0:T(8,128)S(1)} %shard_map.84.refs_1_), channel_id=1, source_target_pairs={{0,16},{4,20},{8,24},{12,28},{16,0},{20,4},{24,8},{28,12},{1,17},{... | collective-permute-start | bytes 98312 | tf_op jit(solution)/shard_map/ppermute | solution.py:707

commit v7 on v6

--- a/solution.py
+++ b/solution.py
@@ -19,6 +19,7 @@
 STEP = 16.0
 PIECES = 3
 PARTS = 4
+AT_ONCE = 3
 ROUTE_LIMIT = 32 * 1024 * 1024
 VMEM_LIMIT = 32 * 1024 * 1024
 LOOK_COST = pl.CostEstimate(flops=2 * 10**9, bytes_accessed=10**7, transcendentals=0)
@@ -284,24 +285,30 @@
     y_id = iota((width_y, lanes), 0).astype(F32).astype(BF16)
     totals[...] = jnp.zeros(totals.shape, F32)
 
-    def add_rows(turn, carry):
+    def add_rows(begin, at_once):
         for c in range(parts):
             row_id = (iota((part_rows, lanes), 0) + (c * part_rows + 1)).astype(F32).astype(BF16)
-            for s in range(slabs):
+            for i in range(at_once * slabs):
+                s = i % slabs
+                turn = begin + i // slabs
                 spot = first[c][s] + turn
                 pieces = split_small(run_row(got, 0, s, spot, last[c][s]))
                 code = run_row(got, 1, s, spot, last[c][s])
                 codes[turn * parts + c, pl.ds(s, 1), :] = code
                 row, y_cell = decode(code, width_y)
-                here = pl.ds(s * lanes, lanes)
+                here = pl.ds(i * lanes, lanes)
                 hit = row_id == row.astype(BF16)
-                for i, piece in enumerate(pieces):
-                    lhs[c, pl.ds(i * part_rows, part_rows), here] = jnp.where(hit, piece, zero)
+                for j, piece in enumerate(pieces):
+                    lhs[c, pl.ds(j * part_rows, part_rows), here] = jnp.where(hit, piece, zero)
                 lhs[c, pl.ds(PIECES * part_rows, part_rows), here] = jnp.where(hit, one, zero)
                 rhs[c, :, here] = jnp.where(y_id == y_cell.astype(BF16), one, zero)
         for c in range(parts):
+            width = pl.ds(0, at_once * slabs * lanes)
             added = lax.dot_general(
-                lhs[c], rhs[c], (((1,), (1,)), ((), ())), preferred_element_type=F32
+                lhs[c, :, width],
+                rhs[c, :, width],
+                (((1,), (1,)), ((), ())),
+                preferred_element_type=F32,
             )
             pieces = [added[i * part_rows : (i + 1) * part_rows] for i in range(PIECES + 1)]
             for i, value in enumerate((join_small(pieces[:PIECES]), pieces[PIECES])):
@@ -309,9 +316,18 @@
                     totals[i, h, pl.ds(c * part_rows, part_rows), :] += value[
                         :, h * lanes : (h + 1) * lanes
                     ]
+
+    def many_turns(step, carry):
+        add_rows(step * AT_ONCE, AT_ONCE)
         return carry
 
-    lax.fori_loop(0, longest, add_rows, 0)
+    def one_turn(turn, carry):
+        add_rows(turn, 1)
+        return carry
+
+    steps = longest // AT_ONCE
+    lax.fori_loop(0, steps, many_turns, 0)
+    lax.fori_loop(steps * AT_ONCE, longest, one_turn, 0)
 
 
 def solve_kernel(dims, totals, temp, below, x_low, x_high, summary, factors):
@@ -686,8 +702,8 @@
             struct(slabs, lanes, dtype=jnp.int32),
         ),
         (
-            pltpu.VMEM((parts, (PIECES + 1) * cells // parts, slabs * lanes), F8),
-            pltpu.VMEM((parts, width_y, slabs * lanes), F8),
+            pltpu.VMEM((parts, (PIECES + 1) * cells // parts, AT_ONCE * slabs * lanes), F8),
+            pltpu.VMEM((parts, width_y, AT_ONCE * slabs * lanes), F8),
         ),
     )(got, spots)
     total, factors = call(

time: 51 us -> 49.9 us (0.978)
  waiting for transfers between devices: 8.31 us -> 11.2 us
  starting transfers between devices: 17.7 us -> 15.7 us
  blocking collectives: 12 us -> 10.5 us
    ppermute x3, waiting for transfers between devices: 4.14 us -> 7.07 us  [body(): lax.ppermute(total, 'gz', [(i, i ^ 1 << level) for i in range(slabs)])]
    ppermute x3, starting transfers between devices: 5.79 us -> 3.85 us  [body(): lax.ppermute(total, 'gz', [(i, i ^ 1 << level) for i in range(slabs)])]
    all_to_all x1, blocking collectives: 12 us -> 10.5 us  [body(): lax.all_to_all(reply, 'gz', split_axis=0, concat_axis=0, tiled=True)]
where the time goes in v7:
time: 49.9 us
  starting transfers between devices  15.7 us (31%)
  Pallas kernels  11.7 us (23%)
  waiting for transfers between devices  11.2 us (22%)
  blocking collectives  10.5 us (21%)
  between operations  0.78 us (2%)
    all_to_all x1, blocking collectives, body(): lax.all_to_all(reply, 'gz', split_axis=0, concat_axis=0, tiled=True)  10.5 us
    all_to_all x1, starting transfers between devices, body(): got = lax.all_to_all(send, 'gz', split_axis=0, concat_axis=0, tiled=True)  7.4 us
    ppermute x3, waiting for transfers between devices, body(): lax.ppermute(total, 'gz', [(i, i ^ 1 << level) for i in range(slabs)])  7.07 us
    all_to_all x1, waiting for transfers between devices, body(): got = lax.all_to_all(send, 'gz', split_axis=0, concat_axis=0, tiled=True)  4.16 us
    pallas_call x3, Pallas kernels, body(): call(functools.partial(look_kernel, dims, parts, levels, level), found_sh...  4.15 us
    ppermute x1, starting transfers between devices, body(): lax.ppermute(electron_temp[-1:], 'gz', [(i, i + 1) for i in range(slabs -...  3.92 us
    ppermute x3, starting transfers between devices, body(): lax.ppermute(total, 'gz', [(i, i ^ 1 << level) for i in range(slabs)])  3.85 us
    pallas_call x1, Pallas kernels, body(): route_call(dims, slabs, rows, parts, atom_velocity.shape, atom_plane.shape)  3.54 us
  transfers between devices with their start and end apart: 7, of which 4 were waited for; matrix products, arithmetic and copies ran while one was open for 0% of the time, Pallas kernels for 12%

profile of v7, /device:TPU:0, one launch (start us, length us, event | category | flops | bytes accessed | tf_op | source)
XLA Modules:
  0.0 49.9 jit_solution(4725734970446580999)
XLA Ops:
  0.6 3.5 %shard_map.77 = (f32[8,2,32,128]{3,2,1,0:T(8,128)}, s32[128,128]{1,0:T(8,128)S(1)}, s32[128,128]{1,0:T(8,128)S(1)}) custom-call(s32[1,128]{1,0:T(1,128)} %bitcast.3, f32[3,128,128]{2,1,0:T(8,128)} %velocity.1, s32[128,128]{1,0:T(8,128)} %plane_hbm.1, s32[128,128]{1,0:T(8,128)} %column_hbm.1), custom_call_target="tpu_custom_call" | custom-call | tf_op jit(solution)/shard_map/pallas_call | solution.py:673
  4.2 0.0 copy-start.1
  4.2 0.0 copy-start
  4.2 7.4 %all-to-all-start = ((f32[8,2,32,128]{3,2,1,0:T(8,128)}), f32[8,2,32,128]{3,2,1,0:T(8,128)S(1)}, u32[]{:S(2)}, u32[]{:S(2)}) async-start(f32[8,2,32,128]{3,2,1,0:T(8,128)} %get-tuple-element.27), calls=%async_computation | async-start | bytes 524288 | tf_op jit(solution)/shard_map/all_to_all | solution.py:689
  11.6 3.9 %collective-permute-start = (f32[1,16,256]{2,1,0:T(8,128)S(1)}, f32[1,16,256]{2,1,0:T(8,128)S(1)}, u32[]{:S(2)}, u32[]{:S(2)}) collective-permute-start(f32[1,16,256]{2,1,0:T(8,128)S(1)} %slice.9), channel_id=1, source_target_pairs={{0,4},{4,8},{8,12},{12,16},{16,20},{20,24},{24,28},{1,5},{5,9},{9,... | collective-permute-start | bytes 49160 | tf_op jit(solution)/shard_map/ppermute | solution.py:690
  15.6 0.2 collective-permute-start.2
  15.8 0.4 collective-permute-start.1
  16.2 0.2 shard_map.78
  16.4 4.2 %all-to-all-done.got = f32[8,2,32,128]{3,2,1,0:T(8,128)S(1)} async-done(((f32[8,2,32,128]{3,2,1,0:T(8,128)}), f32[8,2,32,128]{3,2,1,0:T(8,128)S(1)}, u32[]{:S(2)}, u32[]{:S(2)}) %all-to-all-start) | async-done | bytes 262176 | tf_op jit(solution)/shard_map/all_to_all | solution.py:689
  20.5 1.6 %shard_map.79 = (f32[2,2,256,128]{3,2,1,0:T(8,128)S(1)}, f32[132,8,128]{2,1,0:T(8,128)S(1)}, s32[8,128]{1,0:T(8,128)S(1)}) custom-call(f32[8,2,32,128]{3,2,1,0:T(8,128)S(1)} %all-to-all-done.got, bf16[1024,256]{1,0:T(8,128)(2,1)S(1)} %get-tuple-element.30._.spots), custom_call_target="tpu_custom_call" | custom-call | tf_op jit(solution)/shard_map/pallas_call | solution.py:697
  22.1 0.0 collective-permute-done.below
  22.2 0.4 shard_map.80
  22.6 2.6 %collective-permute-start.3 = (f32[5,16,256]{2,1,0:T(8,128)S(1)}, f32[5,16,256]{2,1,0:T(8,128)S(1)}, u32[]{:S(2)}, u32[]{:S(2)}) collective-permute-start(f32[5,16,256]{2,1,0:T(8,128)S(1)} %get-tuple-element.33.mine.refs_0_), channel_id=1, source_target_pairs={{0,4},{4,0},{8,12},{12,8},{16,20},{20,16},{24,28},{28,24},{1,5},{5... | collective-permute-start | bytes 245768 | tf_op jit(solution)/shard_map/ppermute | solution.py:723
  25.2 1.7 %shard_map.81 = (f32[3,44,8,128]{3,2,1,0:T(8,128)S(1)}, f32[44,8,128]{2,1,0:T(8,128)S(1)}, s32[44,8,128]{2,1,0:T(8,128)S(1)}, f8e4m3fn[4,576,256]{2,1,0:T(32,128)(4,1)S(1)}) custom-call(f32[132,8,128]{2,1,0:T(8,128)S(1)} %get-tuple-element.34.codes, s32[8,128]{1,0:T(8,128)S(1)} %get-tuple-element.31.runs.runs_vmem, ...), custom_call_target="tpu_custom_call" | custom-call | flops 2000000000 | bytes 10000000 | tf_op jit(solution)/shard_map/pallas_call | solution.py:724
  26.9 0.7 %collective-permute-done.3.other.refs_1_ = f32[5,16,256]{2,1,0:T(8,128)S(1)} collective-permute-done((f32[5,16,256]{2,1,0:T(8,128)S(1)}, f32[5,16,256]{2,1,0:T(8,128)S(1)}, u32[]{:S(2)}, u32[]{:S(2)}) %collective-permute-start.3) | collective-permute-done | bytes 81952 | tf_op jit(solution)/shard_map/ppermute | solution.py:723
  27.6 0.6 %collective-permute-start.4 = (f32[5,16,256]{2,1,0:T(8,128)S(1)}, f32[5,16,256]{2,1,0:T(8,128)S(1)}, u32[]{:S(2)}, u32[]{:S(2)}) collective-permute-start(f32[5,16,256]{2,1,0:T(8,128)S(1)} %shard_map.82.refs_1_.mine), channel_id=1, source_target_pairs={{0,8},{4,12},{8,0},{12,4},{16,24},{20,28},{24,16},{28,20},{1,9},{5... | collective-permute-start | bytes 245768 | tf_op jit(solution)/shard_map/ppermute | solution.py:723
  28.2 1.2 %shard_map.83 = (f32[3,44,8,128]{3,2,1,0:T(8,128)S(1)}, f32[44,8,128]{2,1,0:T(8,128)S(1)}, s32[44,8,128]{2,1,0:T(8,128)S(1)}) custom-call(f32[132,8,128]{2,1,0:T(8,128)S(1)} %get-tuple-element.34.codes, s32[8,128]{1,0:T(8,128)S(1)} %get-tuple-element.31.runs.runs_vmem, f8e4m3fn[4,576,256]{2,1,0:T(32,128)(4,1)S(1)} %get-tuple-element.37.refs_0_, ...), custom_call_target="tpu_custom_call" | custom-call | flops 2000000000 | bytes 10000000 | tf_op jit(solution)/shard_map/pallas_call | solution.py:724
  29.4 3.1 %collective-permute-done.4.other.refs_2_ = f32[5,16,256]{2,1,0:T(8,128)S(1)} collective-permute-done((f32[5,16,256]{2,1,0:T(8,128)S(1)}, f32[5,16,256]{2,1,0:T(8,128)S(1)}, u32[]{:S(2)}, u32[]{:S(2)}) %collective-permute-start.4) | collective-permute-done | bytes 81952 | tf_op jit(solution)/shard_map/ppermute | solution.py:723
  32.5 0.6 %collective-permute-start.5 = (f32[2,16,256]{2,1,0:T(8,128)S(1)}, f32[2,16,256]{2,1,0:T(8,128)S(1)}, u32[]{:S(2)}, u32[]{:S(2)}) collective-permute-start(f32[2,16,256]{2,1,0:T(8,128)S(1)} %shard_map.84.refs_1_), channel_id=1, source_target_pairs={{0,16},{4,20},{8,24},{12,28},{16,0},{20,4},{24,8},{28,12},{1,17},{... | collective-permute-start | bytes 98312 | tf_op jit(solution)/shard_map/ppermute | solution.py:723
  33.2 1.2 %shard_map.85 = (f32[3,44,8,128]{3,2,1,0:T(8,128)S(1)}, f32[44,8,128]{2,1,0:T(8,128)S(1)}, s32[44,8,128]{2,1,0:T(8,128)S(1)}) custom-call(f32[132,8,128]{2,1,0:T(8,128)S(1)} %get-tuple-element.34.codes, s32[8,128]{1,0:T(8,128)S(1)} %get-tuple-element.31.runs.runs_vmem, f8e4m3fn[4,576,256]{2,1,0:T(32,128)(4,1)S(1)} %get-tuple-element.37.refs_0_, ...), custom_call_target="tpu_custom_call" | custom-call | flops 2000000000 | bytes 10000000 | tf_op jit(solution)/shard_map/pallas_call | solution.py:724
  34.4 3.3 %collective-permute-done.5.refs_3_ = f32[2,16,256]{2,1,0:T(8,128)S(1)} collective-permute-done((f32[2,16,256]{2,1,0:T(8,128)S(1)}, f32[2,16,256]{2,1,0:T(8,128)S(1)}, u32[]{:S(2)}, u32[]{:S(2)}) %collective-permute-start.5) | collective-permute-done | bytes 32800 | tf_op jit(solution)/shard_map/ppermute | solution.py:723
  37.7 0.5 %shard_map.86 = (f32[2,16,256]{2,1,0:T(8,128)S(1)}, f32[8,32,128]{2,1,0:T(8,128)S(1)}) custom-call(s32[8,128]{1,0:T(8,128)S(1)} %get-tuple-element.31.runs.runs_vmem, f32[5,16,256]{2,1,0:T(8,128)S(1)} %get-tuple-element.33.mine.refs_0_, f32[5,16,256]{2,1,0:T(8,128)S(1)} %collective-permute-done.3.other.refs_1_, ...), custom_call_target="tpu_custom_call" | custom-call | tf_op jit(solution)/shard_map/pallas_call | solution.py:741
  38.3 10.5 %all_to_all.10 = f32[8,32,128]{2,1,0:T(8,128)S(1)} all-to-all(f32[8,32,128]{2,1,0:T(8,128)S(1)} %get-tuple-element.46), channel_id=1, replica_groups=mesh['gz'=8,'gx'=4] {'gz'}, dimensions={0} | all-to-all | bytes 262144 | tf_op jit(solution)/shard_map/all_to_all | solution.py:749
  48.7 1.2 %shard_map.87 = (f32[3,128,128]{2,1,0:T(8,128)}, f32[16,16,256]{2,1,0:T(8,128)}) custom-call(f32[256,128]{1,0:T(8,128)S(1)} %bitcast.2, bf16[1024,256]{1,0:T(8,128)(2,1)S(1)} %get-tuple-element.30._.spots, s32[128,128]{1,0:T(8,128)S(1)} %get-tuple-element.29.meta, s32[128,128]{1,0:T(8,128)S(1)} %get-tuple-element.28.starts, ...), custom_call_target="tpu_custom_call" | custom-call | tf_op jit(solution)/shard_map/pallas_call | solution.py:750
  (10 shorter events, 0.1 us)
Async XLA Ops:
  0.6 15.5 %copy-start.2 = (f32[3,128,128]{2,1,0:T(8,128)S(1)}, f32[3,128,128]{2,1,0:T(8,128)}, u32[]{:S(2)}) copy-start(f32[3,128,128]{2,1,0:T(8,128)} %noise.1) | copy-start | bytes 589828
  4.2 7.4 %copy-start.1 = (f32[16,16,256]{2,1,0:T(8,128)S(1)}, f32[16,16,256]{2,1,0:T(8,128)}, u32[]{:S(2)}) copy-start(f32[16,16,256]{2,1,0:T(8,128)} %temp.1) | copy-start | bytes 786436
  4.2 12.0 %copy-start = (f32[3,128,128]{2,1,0:T(8,128)S(1)}, f32[3,128,128]{2,1,0:T(8,128)}, u32[]{:S(2)}) copy-start(f32[3,128,128]{2,1,0:T(8,128)} %velocity.1) | copy-start | bytes 589828
  4.2 16.3 %all-to-all-start = ((f32[8,2,32,128]{3,2,1,0:T(8,128)}), f32[8,2,32,128]{3,2,1,0:T(8,128)S(1)}, u32[]{:S(2)}, u32[]{:S(2)}) async-start(f32[8,2,32,128]{3,2,1,0:T(8,128)} %get-tuple-element.27), calls=%async_computation | async-start | bytes 524288 | tf_op jit(solution)/shard_map/all_to_all | solution.py:689
  11.6 10.5 %collective-permute-start = (f32[1,16,256]{2,1,0:T(8,128)S(1)}, f32[1,16,256]{2,1,0:T(8,128)S(1)}, u32[]{:S(2)}, u32[]{:S(2)}) collective-permute-start(f32[1,16,256]{2,1,0:T(8,128)S(1)} %slice.9), channel_id=1, source_target_pairs={{0,4},{4,8},{8,12},{12,16},{16,20},{20,24},{24,28},{1,5},{5,9},{9,... | collective-permute-start | bytes 49160 | tf_op jit(solution)/shard_map/ppermute | solution.py:690
  15.6 6.6 %collective-permute-start.2 = (f32[16,1,256]{2,1,0:T(1,128)S(1)}, f32[16,1,256]{2,1,0:T(1,128)S(1)}, u32[]{:S(2)}, u32[]{:S(2)}) collective-permute-start(f32[16,1,256]{2,1,0:T(1,128)S(1)} %get-tuple-element.52), channel_id=1, source_target_pairs={{1,0},{2,1},{3,2},{0,3},{5,4},{6,5},{7,6},{4,7},{9,8},{10,9},{11,1... | collective-permute-start | bytes 49160 | tf_op jit(solution)/shard_map/ppermute | solution.py:694
  15.8 6.4 %collective-permute-start.1 = (f32[16,1,256]{2,1,0:T(1,128)S(1)}, f32[16,1,256]{2,1,0:T(1,128)S(1)}, u32[]{:S(2)}, u32[]{:S(2)}) collective-permute-start(f32[16,1,256]{2,1,0:T(1,128)S(1)} %get-tuple-element.53), channel_id=1, source_target_pairs={{0,1},{1,2},{2,3},{3,0},{4,5},{5,6},{6,7},{7,4},{8,9},{9,10},{10,1... | collective-permute-start | bytes 49160 | tf_op jit(solution)/shard_map/ppermute | solution.py:691
  22.6 5.0 %collective-permute-start.3 = (f32[5,16,256]{2,1,0:T(8,128)S(1)}, f32[5,16,256]{2,1,0:T(8,128)S(1)}, u32[]{:S(2)}, u32[]{:S(2)}) collective-permute-start(f32[5,16,256]{2,1,0:T(8,128)S(1)} %get-tuple-element.33.mine.refs_0_), channel_id=1, source_target_pairs={{0,4},{4,0},{8,12},{12,8},{16,20},{20,16},{24,28},{28,24},{1,5},{5... | collective-permute-start | bytes 245768 | tf_op jit(solution)/shard_map/ppermute | solution.py:723
  27.6 4.9 %collective-permute-start.4 = (f32[5,16,256]{2,1,0:T(8,128)S(1)}, f32[5,16,256]{2,1,0:T(8,128)S(1)}, u32[]{:S(2)}, u32[]{:S(2)}) collective-permute-start(f32[5,16,256]{2,1,0:T(8,128)S(1)} %shard_map.82.refs_1_.mine), channel_id=1, source_target_pairs={{0,8},{4,12},{8,0},{12,4},{16,24},{20,28},{24,16},{28,20},{1,9},{5... | collective-permute-start | bytes 245768 | tf_op jit(solution)/shard_map/ppermute | solution.py:723
  32.5 5.2 %collective-permute-start.5 = (f32[2,16,256]{2,1,0:T(8,128)S(1)}, f32[2,16,256]{2,1,0:T(8,128)S(1)}, u32[]{:S(2)}, u32[]{:S(2)}) collective-permute-start(f32[2,16,256]{2,1,0:T(8,128)S(1)} %shard_map.84.refs_1_), channel_id=1, source_target_pairs={{0,16},{4,20},{8,24},{12,28},{16,0},{20,4},{24,8},{28,12},{1,17},{... | collective-permute-start | bytes 98312 | tf_op jit(solution)/shard_map/ppermute | solution.py:723

commit v8 on v7

--- a/solution.py
+++ b/solution.py
@@ -19,7 +19,7 @@
 STEP = 16.0
 PIECES = 3
 PARTS = 4
-AT_ONCE = 3
+AT_ONCE = 6
 ROUTE_LIMIT = 32 * 1024 * 1024
 VMEM_LIMIT = 32 * 1024 * 1024
 LOOK_COST = pl.CostEstimate(flops=2 * 10**9, bytes_accessed=10**7, transcendentals=0)

time: 49.9 us -> 50 us (level)
  Pallas kernels: 11.7 us -> 16.2 us
  waiting for transfers between devices: 11.2 us -> 9.08 us
  starting transfers between devices: 15.7 us -> 14.1 us
  blocking collectives: 10.5 us -> 9.74 us
    pallas_call x3, Pallas kernels: 4.15 us -> 7.42 us  [body(): call(functools.partial(look_kernel, dims, parts, levels, level), found_sh...]
    ppermute x3, waiting for transfers between devices: 7.07 us -> 4.91 us  [body(): lax.ppermute(total, 'gz', [(i, i ^ 1 << level) for i in range(slabs)])]
    ppermute x3, starting transfers between devices: 3.85 us -> 2.22 us  [body(): lax.ppermute(total, 'gz', [(i, i ^ 1 << level) for i in range(slabs)])]
    pallas_call x1, Pallas kernels: 1.61 us -> 2.53 us  [body(): call(functools.partial(bin_kernel, dims, parts), (struct(2, width_y // la...]
    all_to_all x1, blocking collectives: 10.5 us -> 9.74 us  [body(): lax.all_to_all(reply, 'gz', split_axis=0, concat_axis=0, tiled=True)]
  transfers between devices with their start and end apart: 7 -> 7, of which waited for: 4 -> 4; matrix products, arithmetic and copies ran while one was open for 0% -> 0% of each run, Pallas kernels for 12% -> 20%
where the time goes in v8:
time: 50 us; the launch traced here: 49.9 us
  Pallas kernels  16.2 us (32%)
  starting transfers between devices  14.1 us (28%)
  blocking collectives  9.74 us (19%)
  waiting for transfers between devices  9.08 us (18%)
  between operations  0.78 us (2%)
    all_to_all x1, blocking collectives, body(): lax.all_to_all(reply, 'gz', split_axis=0, concat_axis=0, tiled=True)  9.74 us
    pallas_call x3, Pallas kernels, body(): call(functools.partial(look_kernel, dims, parts, levels, level), found_sh...  7.42 us
    all_to_all x1, starting transfers between devices, body(): got = lax.all_to_all(send, 'gz', split_axis=0, concat_axis=0, tiled=True)  7.4 us
    ppermute x3, waiting for transfers between devices, body(): lax.ppermute(total, 'gz', [(i, i ^ 1 << level) for i in range(slabs)])  4.91 us
    all_to_all x1, waiting for transfers between devices, body(): got = lax.all_to_all(send, 'gz', split_axis=0, concat_axis=0, tiled=True)  4.16 us
    ppermute x1, starting transfers between devices, body(): lax.ppermute(electron_temp[-1:], 'gz', [(i, i + 1) for i in range(slabs -...  3.92 us
    pallas_call x1, Pallas kernels, body(): route_call(dims, slabs, rows, parts, atom_velocity.shape, atom_plane.shape)  3.54 us
    pallas_call x1, Pallas kernels, body(): call(functools.partial(bin_kernel, dims, parts), (struct(2, width_y // la...  2.53 us
  transfers between devices with their start and end apart: 7, of which 4 were waited for; matrix products, arithmetic and copies ran while one was open for 0% of the time, Pallas kernels for 20%

profile of v8, /device:TPU:0, one launch (start us, length us, event | category | flops | bytes accessed | tf_op | source)
XLA Modules:
  0.0 49.9 jit_solution(1445600069413905701)
XLA Ops:
  0.6 3.5 %shard_map.77 = (f32[8,2,32,128]{3,2,1,0:T(8,128)}, s32[128,128]{1,0:T(8,128)S(1)}, s32[128,128]{1,0:T(8,128)S(1)}) custom-call(s32[1,128]{1,0:T(1,128)} %bitcast.3, f32[3,128,128]{2,1,0:T(8,128)} %velocity.1, s32[128,128]{1,0:T(8,128)} %plane_hbm.1, s32[128,128]{1,0:T(8,128)} %column_hbm.1), custom_call_target="tpu_custom_call" | custom-call | tf_op jit(solution)/shard_map/pallas_call | solution.py:673
  4.2 0.0 copy-start.1
  4.2 0.0 copy-start
  4.2 7.4 %all-to-all-start = ((f32[8,2,32,128]{3,2,1,0:T(8,128)}), f32[8,2,32,128]{3,2,1,0:T(8,128)S(1)}, u32[]{:S(2)}, u32[]{:S(2)}) async-start(f32[8,2,32,128]{3,2,1,0:T(8,128)} %get-tuple-element.27), calls=%async_computation | async-start | bytes 524288 | tf_op jit(solution)/shard_map/all_to_all | solution.py:689
  11.6 3.9 %collective-permute-start = (f32[1,16,256]{2,1,0:T(8,128)S(1)}, f32[1,16,256]{2,1,0:T(8,128)S(1)}, u32[]{:S(2)}, u32[]{:S(2)}) collective-permute-start(f32[1,16,256]{2,1,0:T(8,128)S(1)} %slice.9), channel_id=1, source_target_pairs={{0,4},{4,8},{8,12},{12,16},{16,20},{20,24},{24,28},{1,5},{5,9},{9,... | collective-permute-start | bytes 49160 | tf_op jit(solution)/shard_map/ppermute | solution.py:690
  15.6 0.2 collective-permute-start.2
  15.8 0.4 collective-permute-start.1
  16.2 0.2 shard_map.78
  16.4 4.2 %all-to-all-done.got = f32[8,2,32,128]{3,2,1,0:T(8,128)S(1)} async-done(((f32[8,2,32,128]{3,2,1,0:T(8,128)}), f32[8,2,32,128]{3,2,1,0:T(8,128)S(1)}, u32[]{:S(2)}, u32[]{:S(2)}) %all-to-all-start) | async-done | bytes 262176 | tf_op jit(solution)/shard_map/all_to_all | solution.py:689
  20.5 2.5 %shard_map.79 = (f32[2,2,256,128]{3,2,1,0:T(8,128)S(1)}, f32[132,8,128]{2,1,0:T(8,128)S(1)}, s32[8,128]{1,0:T(8,128)S(1)}) custom-call(f32[8,2,32,128]{3,2,1,0:T(8,128)S(1)} %all-to-all-done.got, bf16[1024,256]{1,0:T(8,128)(2,1)S(1)} %get-tuple-element.30._.spots), custom_call_target="tpu_custom_call" | custom-call | tf_op jit(solution)/shard_map/pallas_call | solution.py:697
  23.1 0.0 collective-permute-done.2.x_high
  23.1 0.4 shard_map.80
  23.5 1.0 %collective-permute-start.3 = (f32[5,16,256]{2,1,0:T(8,128)S(1)}, f32[5,16,256]{2,1,0:T(8,128)S(1)}, u32[]{:S(2)}, u32[]{:S(2)}) collective-permute-start(f32[5,16,256]{2,1,0:T(8,128)S(1)} %get-tuple-element.33.mine.refs_0_), channel_id=1, source_target_pairs={{0,4},{4,0},{8,12},{12,8},{16,20},{20,16},{24,28},{28,24},{1,5},{5... | collective-permute-start | bytes 245768 | tf_op jit(solution)/shard_map/ppermute | solution.py:723
  24.4 2.8 %shard_map.81 = (f32[3,44,8,128]{3,2,1,0:T(8,128)S(1)}, f32[44,8,128]{2,1,0:T(8,128)S(1)}, s32[44,8,128]{2,1,0:T(8,128)S(1)}, f8e4m3fn[4,576,256]{2,1,0:T(32,128)(4,1)S(1)}) custom-call(f32[132,8,128]{2,1,0:T(8,128)S(1)} %get-tuple-element.34.codes, s32[8,128]{1,0:T(8,128)S(1)} %get-tuple-element.31.runs.runs_vmem, ...), custom_call_target="tpu_custom_call" | custom-call | flops 2000000000 | bytes 10000000 | tf_op jit(solution)/shard_map/pallas_call | solution.py:724
  27.3 0.7 %collective-permute-done.3.other.refs_1_ = f32[5,16,256]{2,1,0:T(8,128)S(1)} collective-permute-done((f32[5,16,256]{2,1,0:T(8,128)S(1)}, f32[5,16,256]{2,1,0:T(8,128)S(1)}, u32[]{:S(2)}, u32[]{:S(2)}) %collective-permute-start.3) | collective-permute-done | bytes 81952 | tf_op jit(solution)/shard_map/ppermute | solution.py:723
  28.0 0.6 %collective-permute-start.4 = (f32[5,16,256]{2,1,0:T(8,128)S(1)}, f32[5,16,256]{2,1,0:T(8,128)S(1)}, u32[]{:S(2)}, u32[]{:S(2)}) collective-permute-start(f32[5,16,256]{2,1,0:T(8,128)S(1)} %shard_map.82.refs_1_.mine), channel_id=1, source_target_pairs={{0,8},{4,12},{8,0},{12,4},{16,24},{20,28},{24,16},{28,20},{1,9},{5... | collective-permute-start | bytes 245768 | tf_op jit(solution)/shard_map/ppermute | solution.py:723
  28.6 2.3 %shard_map.83 = (f32[3,44,8,128]{3,2,1,0:T(8,128)S(1)}, f32[44,8,128]{2,1,0:T(8,128)S(1)}, s32[44,8,128]{2,1,0:T(8,128)S(1)}) custom-call(f32[132,8,128]{2,1,0:T(8,128)S(1)} %get-tuple-element.34.codes, s32[8,128]{1,0:T(8,128)S(1)} %get-tuple-element.31.runs.runs_vmem, f8e4m3fn[4,576,256]{2,1,0:T(32,128)(4,1)S(1)} %get-tuple-element.37.refs_0_, ...), custom_call_target="tpu_custom_call" | custom-call | flops 2000000000 | bytes 10000000 | tf_op jit(solution)/shard_map/pallas_call | solution.py:724
  30.9 2.0 %collective-permute-done.4.other.refs_2_ = f32[5,16,256]{2,1,0:T(8,128)S(1)} collective-permute-done((f32[5,16,256]{2,1,0:T(8,128)S(1)}, f32[5,16,256]{2,1,0:T(8,128)S(1)}, u32[]{:S(2)}, u32[]{:S(2)}) %collective-permute-start.4) | collective-permute-done | bytes 81952 | tf_op jit(solution)/shard_map/ppermute | solution.py:723
  32.9 0.7 %collective-permute-start.5 = (f32[2,16,256]{2,1,0:T(8,128)S(1)}, f32[2,16,256]{2,1,0:T(8,128)S(1)}, u32[]{:S(2)}, u32[]{:S(2)}) collective-permute-start(f32[2,16,256]{2,1,0:T(8,128)S(1)} %shard_map.84.refs_1_), channel_id=1, source_target_pairs={{0,16},{4,20},{8,24},{12,28},{16,0},{20,4},{24,8},{28,12},{1,17},{... | collective-permute-start | bytes 98312 | tf_op jit(solution)/shard_map/ppermute | solution.py:723
  33.6 2.3 %shard_map.85 = (f32[3,44,8,128]{3,2,1,0:T(8,128)S(1)}, f32[44,8,128]{2,1,0:T(8,128)S(1)}, s32[44,8,128]{2,1,0:T(8,128)S(1)}) custom-call(f32[132,8,128]{2,1,0:T(8,128)S(1)} %get-tuple-element.34.codes, s32[8,128]{1,0:T(8,128)S(1)} %get-tuple-element.31.runs.runs_vmem, f8e4m3fn[4,576,256]{2,1,0:T(32,128)(4,1)S(1)} %get-tuple-element.37.refs_0_, ...), custom_call_target="tpu_custom_call" | custom-call | flops 2000000000 | bytes 10000000 | tf_op jit(solution)/shard_map/pallas_call | solution.py:724
  35.9 2.3 %collective-permute-done.5.refs_3_ = f32[2,16,256]{2,1,0:T(8,128)S(1)} collective-permute-done((f32[2,16,256]{2,1,0:T(8,128)S(1)}, f32[2,16,256]{2,1,0:T(8,128)S(1)}, u32[]{:S(2)}, u32[]{:S(2)}) %collective-permute-start.5) | collective-permute-done | bytes 32800 | tf_op jit(solution)/shard_map/ppermute | solution.py:723
  38.1 0.9 %shard_map.86 = (f32[2,16,256]{2,1,0:T(8,128)S(1)}, f32[8,32,128]{2,1,0:T(8,128)S(1)}) custom-call(s32[8,128]{1,0:T(8,128)S(1)} %get-tuple-element.31.runs.runs_vmem, f32[5,16,256]{2,1,0:T(8,128)S(1)} %get-tuple-element.33.mine.refs_0_, f32[5,16,256]{2,1,0:T(8,128)S(1)} %collective-permute-done.3.other.refs_1_, ...), custom_call_target="tpu_custom_call" | custom-call | tf_op jit(solution)/shard_map/pallas_call | solution.py:741
  39.0 9.7 %all_to_all.10 = f32[8,32,128]{2,1,0:T(8,128)S(1)} all-to-all(f32[8,32,128]{2,1,0:T(8,128)S(1)} %get-tuple-element.46), channel_id=1, replica_groups=mesh['gz'=8,'gx'=4] {'gz'}, dimensions={0} | all-to-all | bytes 262144 | tf_op jit(solution)/shard_map/all_to_all | solution.py:749
  48.7 1.2 %shard_map.87 = (f32[3,128,128]{2,1,0:T(8,128)}, f32[16,16,256]{2,1,0:T(8,128)}) custom-call(f32[256,128]{1,0:T(8,128)S(1)} %bitcast.2, bf16[1024,256]{1,0:T(8,128)(2,1)S(1)} %get-tuple-element.30._.spots, s32[128,128]{1,0:T(8,128)S(1)} %get-tuple-element.29.meta, s32[128,128]{1,0:T(8,128)S(1)} %get-tuple-element.28.starts, ...), custom_call_target="tpu_custom_call" | custom-call | tf_op jit(solution)/shard_map/pallas_call | solution.py:750
  (10 shorter events, 0.1 us)
Async XLA Ops:
  0.6 15.5 %copy-start.2 = (f32[3,128,128]{2,1,0:T(8,128)S(1)}, f32[3,128,128]{2,1,0:T(8,128)}, u32[]{:S(2)}) copy-start(f32[3,128,128]{2,1,0:T(8,128)} %noise.1) | copy-start | bytes 589828
  4.2 7.4 %copy-start.1 = (f32[16,16,256]{2,1,0:T(8,128)S(1)}, f32[16,16,256]{2,1,0:T(8,128)}, u32[]{:S(2)}) copy-start(f32[16,16,256]{2,1,0:T(8,128)} %temp.1) | copy-start | bytes 786436
  4.2 12.0 %copy-start = (f32[3,128,128]{2,1,0:T(8,128)S(1)}, f32[3,128,128]{2,1,0:T(8,128)}, u32[]{:S(2)}) copy-start(f32[3,128,128]{2,1,0:T(8,128)} %velocity.1) | copy-start | bytes 589828
  4.2 16.3 %all-to-all-start = ((f32[8,2,32,128]{3,2,1,0:T(8,128)}), f32[8,2,32,128]{3,2,1,0:T(8,128)S(1)}, u32[]{:S(2)}, u32[]{:S(2)}) async-start(f32[8,2,32,128]{3,2,1,0:T(8,128)} %get-tuple-element.27), calls=%async_computation | async-start | bytes 524288 | tf_op jit(solution)/shard_map/all_to_all | solution.py:689
  11.6 11.4 %collective-permute-start = (f32[1,16,256]{2,1,0:T(8,128)S(1)}, f32[1,16,256]{2,1,0:T(8,128)S(1)}, u32[]{:S(2)}, u32[]{:S(2)}) collective-permute-start(f32[1,16,256]{2,1,0:T(8,128)S(1)} %slice.9), channel_id=1, source_target_pairs={{0,4},{4,8},{8,12},{12,16},{16,20},{20,24},{24,28},{1,5},{5,9},{9,... | collective-permute-start | bytes 49160 | tf_op jit(solution)/shard_map/ppermute | solution.py:690
  15.6 7.5 %collective-permute-start.2 = (f32[16,1,256]{2,1,0:T(1,128)S(1)}, f32[16,1,256]{2,1,0:T(1,128)S(1)}, u32[]{:S(2)}, u32[]{:S(2)}) collective-permute-start(f32[16,1,256]{2,1,0:T(1,128)S(1)} %get-tuple-element.52), channel_id=1, source_target_pairs={{1,0},{2,1},{3,2},{0,3},{5,4},{6,5},{7,6},{4,7},{9,8},{10,9},{11,1... | collective-permute-start | bytes 49160 | tf_op jit(solution)/shard_map/ppermute | solution.py:694
  15.8 7.3 %collective-permute-start.1 = (f32[16,1,256]{2,1,0:T(1,128)S(1)}, f32[16,1,256]{2,1,0:T(1,128)S(1)}, u32[]{:S(2)}, u32[]{:S(2)}) collective-permute-start(f32[16,1,256]{2,1,0:T(1,128)S(1)} %get-tuple-element.53), channel_id=1, source_target_pairs={{0,1},{1,2},{2,3},{3,0},{4,5},{5,6},{6,7},{7,4},{8,9},{9,10},{10,1... | collective-permute-start | bytes 49160 | tf_op jit(solution)/shard_map/ppermute | solution.py:691
  23.5 4.5 %collective-permute-start.3 = (f32[5,16,256]{2,1,0:T(8,128)S(1)}, f32[5,16,256]{2,1,0:T(8,128)S(1)}, u32[]{:S(2)}, u32[]{:S(2)}) collective-permute-start(f32[5,16,256]{2,1,0:T(8,128)S(1)} %get-tuple-element.33.mine.refs_0_), channel_id=1, source_target_pairs={{0,4},{4,0},{8,12},{12,8},{16,20},{20,16},{24,28},{28,24},{1,5},{5... | collective-permute-start | bytes 245768 | tf_op jit(solution)/shard_map/ppermute | solution.py:723
  28.0 4.9 %collective-permute-start.4 = (f32[5,16,256]{2,1,0:T(8,128)S(1)}, f32[5,16,256]{2,1,0:T(8,128)S(1)}, u32[]{:S(2)}, u32[]{:S(2)}) collective-permute-start(f32[5,16,256]{2,1,0:T(8,128)S(1)} %shard_map.82.refs_1_.mine), channel_id=1, source_target_pairs={{0,8},{4,12},{8,0},{12,4},{16,24},{20,28},{24,16},{28,20},{1,9},{5... | collective-permute-start | bytes 245768 | tf_op jit(solution)/shard_map/ppermute | solution.py:723
  32.9 5.2 %collective-permute-start.5 = (f32[2,16,256]{2,1,0:T(8,128)S(1)}, f32[2,16,256]{2,1,0:T(8,128)S(1)}, u32[]{:S(2)}, u32[]{:S(2)}) collective-permute-start(f32[2,16,256]{2,1,0:T(8,128)S(1)} %shard_map.84.refs_1_), channel_id=1, source_target_pairs={{0,16},{4,20},{8,24},{12,28},{16,0},{20,4},{24,8},{28,12},{1,17},{... | collective-permute-start | bytes 98312 | tf_op jit(solution)/shard_map/ppermute | solution.py:723

commit v9 on v6

--- a/solution.py
+++ b/solution.py
@@ -19,6 +19,7 @@
 STEP = 16.0
 PIECES = 3
 PARTS = 4
+AT_ONCE = 3
 ROUTE_LIMIT = 32 * 1024 * 1024
 VMEM_LIMIT = 32 * 1024 * 1024
 LOOK_COST = pl.CostEstimate(flops=2 * 10**9, bytes_accessed=10**7, transcendentals=0)
@@ -284,19 +285,21 @@
     y_id = iota((width_y, lanes), 0).astype(F32).astype(BF16)
     totals[...] = jnp.zeros(totals.shape, F32)
 
-    def add_rows(turn, carry):
+    def add_rows(step, carry):
         for c in range(parts):
             row_id = (iota((part_rows, lanes), 0) + (c * part_rows + 1)).astype(F32).astype(BF16)
-            for s in range(slabs):
+            for i in range(AT_ONCE * slabs):
+                s = i % slabs
+                turn = step * AT_ONCE + i // slabs
                 spot = first[c][s] + turn
                 pieces = split_small(run_row(got, 0, s, spot, last[c][s]))
                 code = run_row(got, 1, s, spot, last[c][s])
                 codes[turn * parts + c, pl.ds(s, 1), :] = code
                 row, y_cell = decode(code, width_y)
-                here = pl.ds(s * lanes, lanes)
+                here = pl.ds(i * lanes, lanes)
                 hit = row_id == row.astype(BF16)
-                for i, piece in enumerate(pieces):
-                    lhs[c, pl.ds(i * part_rows, part_rows), here] = jnp.where(hit, piece, zero)
+                for j, piece in enumerate(pieces):
+                    lhs[c, pl.ds(j * part_rows, part_rows), here] = jnp.where(hit, piece, zero)
                 lhs[c, pl.ds(PIECES * part_rows, part_rows), here] = jnp.where(hit, one, zero)
                 rhs[c, :, here] = jnp.where(y_id == y_cell.astype(BF16), one, zero)
         for c in range(parts):
@@ -311,7 +314,7 @@
                     ]
         return carry
 
-    lax.fori_loop(0, longest, add_rows, 0)
+    lax.fori_loop(0, quotient_up(longest, AT_ONCE), add_rows, 0)
 
 
 def solve_kernel(dims, totals, temp, below, x_low, x_high, summary, factors):
@@ -682,12 +685,12 @@
         functools.partial(bin_kernel, dims, parts),
         (
             struct(2, width_y // lanes, cells, lanes),
-            struct(parts * (rows + 1), slabs, lanes),
+            struct(parts * (rows + AT_ONCE), slabs, lanes),
             struct(slabs, lanes, dtype=jnp.int32),
         ),
         (
-            pltpu.VMEM((parts, (PIECES + 1) * cells // parts, slabs * lanes), F8),
-            pltpu.VMEM((parts, width_y, slabs * lanes), F8),
+            pltpu.VMEM((parts, (PIECES + 1) * cells // parts, AT_ONCE * slabs * lanes), F8),
+            pltpu.VMEM((parts, width_y, AT_ONCE * slabs * lanes), F8),
         ),
     )(got, spots)
     total, factors = call(

time: 51 us -> 49.4 us (0.969)
  waiting for transfers between devices: 8.31 us -> 10.5 us
  starting transfers between devices: 17.7 us -> 15.7 us
  blocking collectives: 12 us -> 10.6 us
    ppermute x3, waiting for transfers between devices: 4.14 us -> 6.29 us  [body(): lax.ppermute(total, 'gz', [(i, i ^ 1 << level) for i in range(slabs)])]
    ppermute x3, starting transfers between devices: 5.79 us -> 3.78 us  [body(): lax.ppermute(total, 'gz', [(i, i ^ 1 << level) for i in range(slabs)])]
    all_to_all x1, blocking collectives: 12 us -> 10.6 us  [body(): lax.all_to_all(reply, 'gz', split_axis=0, concat_axis=0, tiled=True)]
where the time goes in v9:
time: 49.4 us; the launch traced here: 49.1 us
  starting transfers between devices  15.7 us (32%)
  Pallas kernels  11.6 us (23%)
  blocking collectives  10.6 us (21%)
  waiting for transfers between devices  10.5 us (21%)
  between operations  0.78 us (2%)
    all_to_all x1, blocking collectives, body(): lax.all_to_all(reply, 'gz', split_axis=0, concat_axis=0, tiled=True)  10.6 us
    all_to_all x1, starting transfers between devices, body(): got = lax.all_to_all(send, 'gz', split_axis=0, concat_axis=0, tiled=True)  7.4 us
    ppermute x3, waiting for transfers between devices, body(): lax.ppermute(total, 'gz', [(i, i ^ 1 << level) for i in range(slabs)])  6.29 us
    all_to_all x1, waiting for transfers between devices, body(): got = lax.all_to_all(send, 'gz', split_axis=0, concat_axis=0, tiled=True)  4.16 us
    pallas_call x3, Pallas kernels, body(): call(functools.partial(look_kernel, dims, parts, levels, level), found_sh...  4.15 us
    ppermute x1, starting transfers between devices, body(): lax.ppermute(electron_temp[-1:], 'gz', [(i, i + 1) for i in range(slabs -...  3.92 us
    ppermute x3, starting transfers between devices, body(): lax.ppermute(total, 'gz', [(i, i ^ 1 << level) for i in range(slabs)])  3.78 us
    pallas_call x1, Pallas kernels, body(): route_call(dims, slabs, rows, parts, atom_velocity.shape, atom_plane.shape)  3.54 us
  transfers between devices with their start and end apart: 7, of which 4 were waited for; matrix products, arithmetic and copies ran while one was open for 0% of the time, Pallas kernels for 12%

profile of v9, /device:TPU:0, one launch (start us, length us, event | category | flops | bytes accessed | tf_op | source)
XLA Modules:
  0.0 49.1 jit_solution(5987187446993463913)
XLA Ops:
  0.6 3.5 %shard_map.77 = (f32[8,2,32,128]{3,2,1,0:T(8,128)}, s32[128,128]{1,0:T(8,128)S(1)}, s32[128,128]{1,0:T(8,128)S(1)}) custom-call(s32[1,128]{1,0:T(1,128)} %bitcast.3, f32[3,128,128]{2,1,0:T(8,128)} %velocity.1, s32[128,128]{1,0:T(8,128)} %plane_hbm.1, s32[128,128]{1,0:T(8,128)} %column_hbm.1), custom_call_target="tpu_custom_call" | custom-call | tf_op jit(solution)/shard_map/pallas_call | solution.py:660
  4.2 0.0 copy-start.1
  4.2 0.0 copy-start
  4.2 7.4 %all-to-all-start = ((f32[8,2,32,128]{3,2,1,0:T(8,128)}), f32[8,2,32,128]{3,2,1,0:T(8,128)S(1)}, u32[]{:S(2)}, u32[]{:S(2)}) async-start(f32[8,2,32,128]{3,2,1,0:T(8,128)} %get-tuple-element.27), calls=%async_computation | async-start | bytes 524288 | tf_op jit(solution)/shard_map/all_to_all | solution.py:676
  11.6 3.9 %collective-permute-start = (f32[1,16,256]{2,1,0:T(8,128)S(1)}, f32[1,16,256]{2,1,0:T(8,128)S(1)}, u32[]{:S(2)}, u32[]{:S(2)}) collective-permute-start(f32[1,16,256]{2,1,0:T(8,128)S(1)} %slice.9), channel_id=1, source_target_pairs={{0,4},{4,8},{8,12},{12,16},{16,20},{20,24},{24,28},{1,5},{5,9},{9,... | collective-permute-start | bytes 49160 | tf_op jit(solution)/shard_map/ppermute | solution.py:677
  15.6 0.2 collective-permute-start.2
  15.8 0.4 collective-permute-start.1
  16.2 0.2 shard_map.78
  16.4 4.2 %all-to-all-done.got = f32[8,2,32,128]{3,2,1,0:T(8,128)S(1)} async-done(((f32[8,2,32,128]{3,2,1,0:T(8,128)}), f32[8,2,32,128]{3,2,1,0:T(8,128)S(1)}, u32[]{:S(2)}, u32[]{:S(2)}) %all-to-all-start) | async-done | bytes 262176 | tf_op jit(solution)/shard_map/all_to_all | solution.py:676
  20.5 1.6 %shard_map.79 = (f32[2,2,256,128]{3,2,1,0:T(8,128)S(1)}, f32[140,8,128]{2,1,0:T(8,128)S(1)}, s32[8,128]{1,0:T(8,128)S(1)}) custom-call(f32[8,2,32,128]{3,2,1,0:T(8,128)S(1)} %all-to-all-done.got, bf16[1024,256]{1,0:T(8,128)(2,1)S(1)} %get-tuple-element.30._.spots), custom_call_target="tpu_custom_call" | custom-call | tf_op jit(solution)/shard_map/pallas_call | solution.py:684
  22.1 0.0 collective-permute-done.below
  22.1 0.4 shard_map.80
  22.5 1.5 %collective-permute-start.3 = (f32[5,16,256]{2,1,0:T(8,128)S(1)}, f32[5,16,256]{2,1,0:T(8,128)S(1)}, u32[]{:S(2)}, u32[]{:S(2)}) collective-permute-start(f32[5,16,256]{2,1,0:T(8,128)S(1)} %get-tuple-element.33.mine.refs_0_), channel_id=1, source_target_pairs={{0,4},{4,0},{8,12},{12,8},{16,20},{20,16},{24,28},{28,24},{1,5},{5... | collective-permute-start | bytes 245768 | tf_op jit(solution)/shard_map/ppermute | solution.py:710
  24.0 1.7 %shard_map.81 = (f32[3,44,8,128]{3,2,1,0:T(8,128)S(1)}, f32[44,8,128]{2,1,0:T(8,128)S(1)}, s32[44,8,128]{2,1,0:T(8,128)S(1)}, f8e4m3fn[4,576,256]{2,1,0:T(32,128)(4,1)S(1)}) custom-call(f32[140,8,128]{2,1,0:T(8,128)S(1)} %get-tuple-element.34.codes, s32[8,128]{1,0:T(8,128)S(1)} %get-tuple-element.31.runs.runs_vmem, ...), custom_call_target="tpu_custom_call" | custom-call | flops 2000000000 | bytes 10000000 | tf_op jit(solution)/shard_map/pallas_call | solution.py:711
  25.7 1.3 %collective-permute-done.3.other.refs_1_ = f32[5,16,256]{2,1,0:T(8,128)S(1)} collective-permute-done((f32[5,16,256]{2,1,0:T(8,128)S(1)}, f32[5,16,256]{2,1,0:T(8,128)S(1)}, u32[]{:S(2)}, u32[]{:S(2)}) %collective-permute-start.3) | collective-permute-done | bytes 81952 | tf_op jit(solution)/shard_map/ppermute | solution.py:710
  27.1 1.1 %collective-permute-start.4 = (f32[5,16,256]{2,1,0:T(8,128)S(1)}, f32[5,16,256]{2,1,0:T(8,128)S(1)}, u32[]{:S(2)}, u32[]{:S(2)}) collective-permute-start(f32[5,16,256]{2,1,0:T(8,128)S(1)} %shard_map.82.refs_1_.mine), channel_id=1, source_target_pairs={{0,8},{4,12},{8,0},{12,4},{16,24},{20,28},{24,16},{28,20},{1,9},{5... | collective-permute-start | bytes 245768 | tf_op jit(solution)/shard_map/ppermute | solution.py:710
  28.2 1.2 %shard_map.83 = (f32[3,44,8,128]{3,2,1,0:T(8,128)S(1)}, f32[44,8,128]{2,1,0:T(8,128)S(1)}, s32[44,8,128]{2,1,0:T(8,128)S(1)}) custom-call(f32[140,8,128]{2,1,0:T(8,128)S(1)} %get-tuple-element.34.codes, s32[8,128]{1,0:T(8,128)S(1)} %get-tuple-element.31.runs.runs_vmem, f8e4m3fn[4,576,256]{2,1,0:T(32,128)(4,1)S(1)} %get-tuple-element.37.refs_0_, ...), custom_call_target="tpu_custom_call" | custom-call | flops 2000000000 | bytes 10000000 | tf_op jit(solution)/shard_map/pallas_call | solution.py:711
  29.4 2.5 %collective-permute-done.4.other.refs_2_ = f32[5,16,256]{2,1,0:T(8,128)S(1)} collective-permute-done((f32[5,16,256]{2,1,0:T(8,128)S(1)}, f32[5,16,256]{2,1,0:T(8,128)S(1)}, u32[]{:S(2)}, u32[]{:S(2)}) %collective-permute-start.4) | collective-permute-done | bytes 81952 | tf_op jit(solution)/shard_map/ppermute | solution.py:710
  31.9 1.2 %collective-permute-start.5 = (f32[2,16,256]{2,1,0:T(8,128)S(1)}, f32[2,16,256]{2,1,0:T(8,128)S(1)}, u32[]{:S(2)}, u32[]{:S(2)}) collective-permute-start(f32[2,16,256]{2,1,0:T(8,128)S(1)} %shard_map.84.refs_1_), channel_id=1, source_target_pairs={{0,16},{4,20},{8,24},{12,28},{16,0},{20,4},{24,8},{28,12},{1,17},{... | collective-permute-start | bytes 98312 | tf_op jit(solution)/shard_map/ppermute | solution.py:710
  33.1 1.2 %shard_map.85 = (f32[3,44,8,128]{3,2,1,0:T(8,128)S(1)}, f32[44,8,128]{2,1,0:T(8,128)S(1)}, s32[44,8,128]{2,1,0:T(8,128)S(1)}) custom-call(f32[140,8,128]{2,1,0:T(8,128)S(1)} %get-tuple-element.34.codes, s32[8,128]{1,0:T(8,128)S(1)} %get-tuple-element.31.runs.runs_vmem, f8e4m3fn[4,576,256]{2,1,0:T(32,128)(4,1)S(1)} %get-tuple-element.37.refs_0_, ...), custom_call_target="tpu_custom_call" | custom-call | flops 2000000000 | bytes 10000000 | tf_op jit(solution)/shard_map/pallas_call | solution.py:711
  34.3 2.5 %collective-permute-done.5.refs_3_ = f32[2,16,256]{2,1,0:T(8,128)S(1)} collective-permute-done((f32[2,16,256]{2,1,0:T(8,128)S(1)}, f32[2,16,256]{2,1,0:T(8,128)S(1)}, u32[]{:S(2)}, u32[]{:S(2)}) %collective-permute-start.5) | collective-permute-done | bytes 32800 | tf_op jit(solution)/shard_map/ppermute | solution.py:710
  36.8 0.5 %shard_map.86 = (f32[2,16,256]{2,1,0:T(8,128)S(1)}, f32[8,32,128]{2,1,0:T(8,128)S(1)}) custom-call(s32[8,128]{1,0:T(8,128)S(1)} %get-tuple-element.31.runs.runs_vmem, f32[5,16,256]{2,1,0:T(8,128)S(1)} %get-tuple-element.33.mine.refs_0_, f32[5,16,256]{2,1,0:T(8,128)S(1)} %collective-permute-done.3.other.refs_1_, ...), custom_call_target="tpu_custom_call" | custom-call | tf_op jit(solution)/shard_map/pallas_call | solution.py:728
  37.4 10.6 %all_to_all.10 = f32[8,32,128]{2,1,0:T(8,128)S(1)} all-to-all(f32[8,32,128]{2,1,0:T(8,128)S(1)} %get-tuple-element.46), channel_id=1, replica_groups=mesh['gz'=8,'gx'=4] {'gz'}, dimensions={0} | all-to-all | bytes 262144 | tf_op jit(solution)/shard_map/all_to_all | solution.py:736
  47.9 1.2 %shard_map.87 = (f32[3,128,128]{2,1,0:T(8,128)}, f32[16,16,256]{2,1,0:T(8,128)}) custom-call(f32[256,128]{1,0:T(8,128)S(1)} %bitcast.2, bf16[1024,256]{1,0:T(8,128)(2,1)S(1)} %get-tuple-element.30._.spots, s32[128,128]{1,0:T(8,128)S(1)} %get-tuple-element.29.meta, s32[128,128]{1,0:T(8,128)S(1)} %get-tuple-element.28.starts, ...), custom_call_target="tpu_custom_call" | custom-call | tf_op jit(solution)/shard_map/pallas_call | solution.py:737
  (10 shorter events, 0.1 us)
Async XLA Ops:
  0.6 15.5 %copy-start.2 = (f32[3,128,128]{2,1,0:T(8,128)S(1)}, f32[3,128,128]{2,1,0:T(8,128)}, u32[]{:S(2)}) copy-start(f32[3,128,128]{2,1,0:T(8,128)} %noise.1) | copy-start | bytes 589828
  4.2 7.4 %copy-start.1 = (f32[16,16,256]{2,1,0:T(8,128)S(1)}, f32[16,16,256]{2,1,0:T(8,128)}, u32[]{:S(2)}) copy-start(f32[16,16,256]{2,1,0:T(8,128)} %temp.1) | copy-start | bytes 786436
  4.2 12.0 %copy-start = (f32[3,128,128]{2,1,0:T(8,128)S(1)}, f32[3,128,128]{2,1,0:T(8,128)}, u32[]{:S(2)}) copy-start(f32[3,128,128]{2,1,0:T(8,128)} %velocity.1) | copy-start | bytes 589828
  4.2 16.3 %all-to-all-start = ((f32[8,2,32,128]{3,2,1,0:T(8,128)}), f32[8,2,32,128]{3,2,1,0:T(8,128)S(1)}, u32[]{:S(2)}, u32[]{:S(2)}) async-start(f32[8,2,32,128]{3,2,1,0:T(8,128)} %get-tuple-element.27), calls=%async_computation | async-start | bytes 524288 | tf_op jit(solution)/shard_map/all_to_all | solution.py:676
  11.6 10.5 %collective-permute-start = (f32[1,16,256]{2,1,0:T(8,128)S(1)}, f32[1,16,256]{2,1,0:T(8,128)S(1)}, u32[]{:S(2)}, u32[]{:S(2)}) collective-permute-start(f32[1,16,256]{2,1,0:T(8,128)S(1)} %slice.9), channel_id=1, source_target_pairs={{0,4},{4,8},{8,12},{12,16},{16,20},{20,24},{24,28},{1,5},{5,9},{9,... | collective-permute-start | bytes 49160 | tf_op jit(solution)/shard_map/ppermute | solution.py:677
  15.6 6.5 %collective-permute-start.2 = (f32[16,1,256]{2,1,0:T(1,128)S(1)}, f32[16,1,256]{2,1,0:T(1,128)S(1)}, u32[]{:S(2)}, u32[]{:S(2)}) collective-permute-start(f32[16,1,256]{2,1,0:T(1,128)S(1)} %get-tuple-element.52), channel_id=1, source_target_pairs={{1,0},{2,1},{3,2},{0,3},{5,4},{6,5},{7,6},{4,7},{9,8},{10,9},{11,1... | collective-permute-start | bytes 49160 | tf_op jit(solution)/shard_map/ppermute | solution.py:681
  15.8 6.4 %collective-permute-start.1 = (f32[16,1,256]{2,1,0:T(1,128)S(1)}, f32[16,1,256]{2,1,0:T(1,128)S(1)}, u32[]{:S(2)}, u32[]{:S(2)}) collective-permute-start(f32[16,1,256]{2,1,0:T(1,128)S(1)} %get-tuple-element.53), channel_id=1, source_target_pairs={{0,1},{1,2},{2,3},{3,0},{4,5},{5,6},{6,7},{7,4},{8,9},{9,10},{10,1... | collective-permute-start | bytes 49160 | tf_op jit(solution)/shard_map/ppermute | solution.py:678
  22.5 4.5 %collective-permute-start.3 = (f32[5,16,256]{2,1,0:T(8,128)S(1)}, f32[5,16,256]{2,1,0:T(8,128)S(1)}, u32[]{:S(2)}, u32[]{:S(2)}) collective-permute-start(f32[5,16,256]{2,1,0:T(8,128)S(1)} %get-tuple-element.33.mine.refs_0_), channel_id=1, source_target_pairs={{0,4},{4,0},{8,12},{12,8},{16,20},{20,16},{24,28},{28,24},{1,5},{5... | collective-permute-start | bytes 245768 | tf_op jit(solution)/shard_map/ppermute | solution.py:710
  27.1 4.9 %collective-permute-start.4 = (f32[5,16,256]{2,1,0:T(8,128)S(1)}, f32[5,16,256]{2,1,0:T(8,128)S(1)}, u32[]{:S(2)}, u32[]{:S(2)}) collective-permute-start(f32[5,16,256]{2,1,0:T(8,128)S(1)} %shard_map.82.refs_1_.mine), channel_id=1, source_target_pairs={{0,8},{4,12},{8,0},{12,4},{16,24},{20,28},{24,16},{28,20},{1,9},{5... | collective-permute-start | bytes 245768 | tf_op jit(solution)/shard_map/ppermute | solution.py:710
  31.9 4.9 %collective-permute-start.5 = (f32[2,16,256]{2,1,0:T(8,128)S(1)}, f32[2,16,256]{2,1,0:T(8,128)S(1)}, u32[]{:S(2)}, u32[]{:S(2)}) collective-permute-start(f32[2,16,256]{2,1,0:T(8,128)S(1)} %shard_map.84.refs_1_), channel_id=1, source_target_pairs={{0,16},{4,20},{8,24},{12,28},{16,0},{20,4},{24,8},{28,12},{1,17},{... | collective-permute-start | bytes 98312 | tf_op jit(solution)/shard_map/ppermute | solution.py:710
